TPU v7x, 128 devices: a whole 4x4x4 slice. The times are simulated.
128 devices in a mesh: expert: 8 (over z, core), shard: 16 (over y, x).
Axes of the slice: x: 4, y: 4, z: 4, core: 2. Of those that a mesh axis runs over, the one named last changes fastest.
Arguments:
- tokens: bfloat16 [1024, 6144], P('expert'), may hold values from -6 to 6
- routes: int32 [1024, 2], P('expert'), may hold values from 0 to 7, all different within a row; in each aligned block of 128 rows (0 to 127, 128 to 255, ...) at most 64 rows name the same one
- route_weights: float32 [1024, 2], P('expert'), may hold values from 0.1 to 1
- out_grad: bfloat16 [1024, 6144], P('expert'), may hold values from -6 to 6
- w_gate: bfloat16 [8, 6144, 8192], P('expert', None, 'shard'), may hold values from -0.078125 to 0.078125
- w_up: bfloat16 [8, 6144, 8192], P('expert', None, 'shard'), may hold values from -0.078125 to 0.078125
- w_down: bfloat16 [8, 8192, 6144], P('expert', 'shard'), may hold values from -0.0625 to 0.0625
Outputs:
- moe_out: bfloat16 [1024, 6144], P('expert')
- input_grad: bfloat16 [1024, 6144], P('expert')
Inputs may be any that keep to these rules, and one draw needn't show every extreme that they name: `routes`: the two experts of a token differ. In each aligned block of 128 rows (the tokens of one expert group) no expert is named by more than 64 rows, and in every draw some expert is named by exactly 64 rows of some block.
All inputs are finite; a program needn't handle non-finite values.
Results may differ from a plain program's by a relative error of at most 0.02.
Values may be sent and summed in bfloat16 or wider, within the bound.
No kernel may reach another device: no remote copies, remote signals or barrier semaphores. Data moves between devices by JAX's collectives and lax.ppermute only.
A program may use at most 128 MiB of HBM per device.

v0:
```python
import functools

import jax
import jax.numpy as jnp
from jax import lax
from jax.experimental import pallas as pl
from jax.experimental.pallas import tpu as pltpu
from jax.sharding import Mesh
from jax.sharding import PartitionSpec as P

F32 = jnp.float32
BF16 = jnp.bfloat16
EXPERT = ("z", "core")
AXES = ("x", "y")
RING = 4
GROUPS = 8
ROWS = 256
MIB = 1 << 20


def shift(rows, axis, step):
    return lax.ppermute(rows, axis, [(i, (i + step) % RING) for i in range(RING)])


def dot(a, b):
    return jnp.dot(a, b, preferred_element_type=F32)


def dot_t(a, b):
    return lax.dot_general(a, b, (((1,), (1,)), ((), ())), preferred_element_type=F32)


def slots_of(routes, per_expert):
    flat = routes.reshape(-1)
    order = jnp.arange(flat.shape[0], dtype=jnp.int32)
    earlier = (flat[:, None] == flat[None, :]) & (order[:, None] > order[None, :])
    before = jnp.sum(earlier.astype(jnp.int32), axis=1)
    return (flat * per_expert + before).reshape(routes.shape)


def whole(shape):
    return pl.BlockSpec(shape, lambda *_: (0,) * len(shape))


def halves_kernel(*refs):
    for source, to in zip(refs[:4], refs[4:]):
        to[...] = source[...]


def gathered(owns):
    rows, chunk = owns[0].shape
    half = rows // 2
    befores = [shift(own, axis, 1) for own, axis in zip(owns, AXES)]
    afters = [shift(own, axis, -1) for own, axis in zip(owns, AXES)]
    top = pl.BlockSpec((half, chunk), lambda i: (0, 0))
    bottom = pl.BlockSpec((half, chunk), lambda i: (1, 0))
    send = pl.pallas_call(
        halves_kernel,
        out_shape=[jax.ShapeDtypeStruct((half, chunk), BF16)] * 4,
        grid=(1,),
        in_specs=[top, top, bottom, bottom],
        out_specs=[whole((half, chunk))] * 4,
        compiler_params=params(12),
        cost_estimate=cost(0, 16 * half * chunk),
        name="halves",
    )(*befores, *afters)
    near = [[owns[h], afters[h], befores[h]] for h in range(2)]
    far = [[shift(send[h], AXES[h], 1), shift(send[2 + h], AXES[h], -1)] for h in range(2)]
    return near, far


def forward_near_kernel(place, *refs):
    rows, (wg, wu), (gate, up) = refs[:6], refs[6:8], refs[8:]
    for h in range(2):
        for i in range(3):

            @pl.when((pl.program_id(0) == h) & (pl.program_id(1) == i))
            def _(h=h, i=i):
                block = rows[3 * h + i][...]
                for acc, w in ((gate, wg), (up, wu)):
                    value = dot(block, w[...])
                    acc[...] = value if i == 0 else acc[...] + value


def forward_far_kernel(place, *refs):
    rows, (wg, wu, gate, up), (hidden, to_gate, to_up) = refs[:4], refs[4:8], refs[8:]
    for h in range(2):

        @pl.when(pl.program_id(0) == h)
        def _(h=h):
            block = jnp.concatenate([rows[2 * h][...], rows[2 * h + 1][...]], axis=0)
            g = gate[...] + dot(block, wg[...])
            u = up[...] + dot(block, wu[...])
            s = 1.0 / (1.0 + jnp.exp(-g))
            hidden[...] = (g * s * u).astype(BF16)
            to_gate[...] = u * s * (1.0 + g * (1.0 - s))
            to_up[...] = g * s


STEPS = 8


def hidden_grad_kernel(rows, wd, to_gate, to_up, after, d_gate, d_up, acc):
    step = pl.program_id(0)
    for h in range(2):
        at = slice(h * ROWS, (h + 1) * ROWS)
        value = dot_t(rows[:, h].reshape(ROWS, rows.shape[-1]), wd[...])

        @pl.when(step == 0)
        def _(at=at, value=value):
            acc[at] = value

        @pl.when(step > 0)
        def _(at=at, value=value):
            acc[at] += value

    @pl.when(step == STEPS - 1)
    def _():
        d_gate[...] = (acc[...] * to_gate[...]).astype(BF16)
        d_up[...] = (acc[...] * to_up[...]).astype(BF16)


def params(mib):
    return pltpu.CompilerParams(vmem_limit_bytes=mib * MIB)


def cost(flops, moved):
    return pl.CostEstimate(flops=int(flops), bytes_accessed=int(moved), transcendentals=0)


def forward(place, near, far, w_gate, w_up):
    width, hid = w_gate.shape
    chunk = width // RING

    def weights(distance):
        return pl.BlockSpec((chunk, hid), lambda *at: ((at[-1][at[0]] + distance(at)) % RING, 0))

    def by_half(*_):
        return pl.BlockSpec((ROWS, hid), lambda *at: (at[0], 0))

    near_w = weights(lambda at: jnp.where(at[1] == 2, 3, at[1]))
    rows = near[0] + near[1]
    gate, up = pl.pallas_call(
        forward_near_kernel,
        out_shape=[jax.ShapeDtypeStruct((2 * ROWS, hid), F32)] * 2,
        grid_spec=pltpu.PrefetchScalarGridSpec(
            num_scalar_prefetch=1,
            grid=(2, 3),
            in_specs=[whole(r.shape) for r in rows] + [near_w, near_w],
            out_specs=[by_half()] * 2,
        ),
        compiler_params=params(32),
        cost_estimate=cost(6 * ROWS * width * hid, 3 * width * ROWS + 6 * width * hid),
        name="forward_near",
    )(place, *rows, w_gate, w_up)
    far_w = weights(lambda at: 2)
    rows = far[0] + far[1]
    return pl.pallas_call(
        forward_far_kernel,
        out_shape=[jax.ShapeDtypeStruct((2 * ROWS, hid), t) for t in (BF16, F32, F32)],
        grid_spec=pltpu.PrefetchScalarGridSpec(
            num_scalar_prefetch=1,
            grid=(2,),
            in_specs=[whole(r.shape) for r in rows] + [far_w, far_w, by_half(), by_half()],
            out_specs=[by_half()] * 3,
        ),
        compiler_params=params(32),
        cost_estimate=cost(2 * ROWS * width * hid, width * ROWS + 2 * width * hid + 20 * ROWS * hid),
        name="forward_far",
    )(place, *rows, w_gate, w_up, gate, up)


def hidden_grad(rows, w_down, to_gate, to_up, after):
    hid, width = w_down.shape
    count = 2 * ROWS
    block = width // STEPS
    rows = rows.reshape(GROUPS, 2, ROWS // GROUPS, width)
    return pl.pallas_call(
        hidden_grad_kernel,
        out_shape=[jax.ShapeDtypeStruct((count, hid), BF16)] * 2,
        grid=(STEPS,),
        in_specs=[
            pl.BlockSpec((*rows.shape[:3], block), lambda i: (0, 0, 0, i)),
            pl.BlockSpec((hid, block), lambda i: (0, i)),
            whole((count, hid)),
            whole((count, hid)),
            pl.BlockSpec(memory_space=pl.ANY),
        ],
        out_specs=[whole((count, hid))] * 2,
        scratch_shapes=[pltpu.VMEM((count, hid), F32)],
        compiler_params=params(32),
        cost_estimate=cost(2 * count * width * hid, 2 * width * count + 2 * width * hid),
        name="hidden_grad",
    )(rows, w_down, to_gate, to_up, after)


def order(i):
    return jnp.where(i == 0, 2, jnp.where(i == 1, 1, jnp.where(i == 2, 3, 0)))


def parts_kernel(terms, transposed, place, after, *refs):
    part = refs[-1].shape[-1]
    acts = refs[:terms]
    weights = refs[terms : 6 * terms]
    outs = refs[6 * terms :]
    mult = dot_t if transposed else dot

    def product(h, j):
        total = 0.0
        for t in range(terms):
            mine = weights[5 * t : 5 * t + 5]
            act = acts[t][h * ROWS : (h + 1) * ROWS, :]
            if h == 1:
                block = mine[1 + j][...]
            elif transposed:
                block = mine[0][j * part : (j + 1) * part, :]
            else:
                block = mine[0][:, j * part : (j + 1) * part]
            total += mult(act, block)
        return total.astype(BF16)

    top, bottom = slice(0, ROWS // 2), slice(ROWS // 2, ROWS)
    for step in range(4):

        @pl.when(pl.program_id(0) == step)
        def _(step=step):
            for h in range(2):
                plus, minus, plus_later, minus_later, own = outs[5 * h : 5 * h + 5]
                for j in range(RING):
                    value = product(h, j)
                    if step == 0:
                        plus[0, j] = value[top]
                        minus[0, j] = value[bottom]
                    elif step == 1:
                        plus_later[j] = value[top]
                        plus[0, j] = value[bottom]
                    elif step == 2:
                        minus[0, j] = value[top]
                        minus_later[j] = value[bottom]
                    else:
                        own[j] = value


def ring_parts(place, after, acts, weights, transposed):
    hid = acts[0].shape[1]
    width = weights[0].shape[0] if transposed else weights[0].shape[1]
    chunk, part = width // RING, width // RING // RING

    def block(size, index):
        if transposed:
            return pl.BlockSpec((size, hid), lambda i, place: (index(i, place), 0))
        return pl.BlockSpec((hid, size), lambda i, place: (0, index(i, place)))

    specs, args = [], []
    for w in weights:
        specs.append(block(chunk, lambda i, place: (place[0] + order(i)) % RING))
        args.append(w)
        for j in range(RING):
            specs.append(block(part, lambda i, place, j=j: j * RING + (place[1] + order(i)) % RING))
            args.append(w)
    half = (RING, ROWS // 2, part)
    shapes = [(2, *half), (2, *half), half, half, (RING, ROWS, part)]
    out_specs = [
        pl.BlockSpec((1, *half), lambda i, place: (jnp.minimum(i, 1), 0, 0, 0)),
        pl.BlockSpec((1, *half), lambda i, place: (jnp.where(i >= 2, 1, 0), 0, 0, 0)),
        whole(half),
        whole(half),
        whole((RING, ROWS, part)),
    ]
    outs = pl.pallas_call(
        functools.partial(parts_kernel, len(acts), transposed),
        out_shape=[jax.ShapeDtypeStruct(s, BF16) for s in shapes] * 2,
        grid_spec=pltpu.PrefetchScalarGridSpec(
            num_scalar_prefetch=1,
            grid=(4,),
            in_specs=[pl.BlockSpec(memory_space=pl.ANY)] + [whole(a.shape) for a in acts] + specs,
            out_specs=out_specs * 2,
        ),
        compiler_params=params(44),
        cost_estimate=cost(len(acts) * 4 * ROWS * width * hid, len(acts) * 4 * width * hid + 4 * ROWS * width),
        name="grad_parts" if transposed else "out_parts",
    )(place, after, *acts, *args)
    return outs[:5], outs[5:]


def later_kernel(*refs):
    for own, got, total in zip(refs[:4], refs[4:8], refs[8:]):
        total[...] = (own[...].astype(F32) + got[0].astype(F32)).astype(BF16)


def total_kernel(*refs):
    half = ROWS // 2
    for h in range(2):
        own, first_plus, first_minus, later_plus, later_minus = refs[5 * h : 5 * h + 5]
        total = refs[10 + h]
        top = own[:, :half].astype(F32) + later_plus[...].astype(F32) + first_minus[0].astype(F32)
        bottom = own[:, half:].astype(F32) + first_plus[0].astype(F32) + later_minus[...].astype(F32)
        total[:, :half] = top.astype(BF16)
        total[:, half:] = bottom.astype(BF16)


def ring_sums(parts):
    half = parts[0][2].shape
    full = parts[0][4].shape
    plus = [shift(p[0], axis, 1) for p, axis in zip(parts, AXES)]
    minus = [shift(p[1], axis, -1) for p, axis in zip(parts, AXES)]
    first = pl.BlockSpec((1, *half), lambda i: (0, 0, 0, 0))
    second = pl.BlockSpec((1, *half), lambda i: (1, 0, 0, 0))
    send = pl.pallas_call(
        later_kernel,
        out_shape=[jax.ShapeDtypeStruct(half, BF16)] * 4,
        grid=(1,),
        in_specs=[whole(half)] * 4 + [first] * 4,
        out_specs=[whole(half)] * 4,
        compiler_params=params(16),
        cost_estimate=cost(0, 24 * ROWS // 2 * full[0] * full[2]),
        name="ring_later",
    )(*[p[2] for p in parts], *[p[3] for p in parts], *plus, *minus)
    operands, specs = [], []
    for h in range(2):
        operands += [parts[h][4], plus[h], minus[h], shift(send[h], AXES[h], 1), shift(send[2 + h], AXES[h], -1)]
        specs += [whole(full), second, second, whole(half), whole(half)]
    totals = pl.pallas_call(
        total_kernel,
        out_shape=[jax.ShapeDtypeStruct(full, BF16)] * 2,
        grid=(1,),
        in_specs=specs,
        out_specs=[whole(full)] * 2,
        compiler_params=params(24),
        cost_estimate=cost(0, 16 * ROWS * full[0] * full[2]),
        name="ring_total",
    )(*operands)
    return totals, send


def per_device(tokens, routes, route_weights, out_grad, w_gate, w_up, w_down):
    count_rows, width = tokens.shape
    per_expert = 4 * count_rows // GROUPS
    half = per_expert // 2
    chunk = width // RING
    part = chunk // RING
    w_gate, w_up, w_down = w_gate[0], w_up[0], w_down[0]
    place = [lax.axis_index(axis) for axis in AXES]
    places = jnp.stack(place).astype(jnp.int32)
    target = slots_of(routes, per_expert)
    slots = jnp.arange(GROUPS * per_expert, dtype=jnp.int32).reshape(GROUPS, 2, half)

    def placed(rows, h):
        mine = slots if h is None else slots[:, h]
        mine = mine.reshape(-1, 1)
        dispatch = ((mine == target[None, :, 0]) | (mine == target[None, :, 1])).astype(BF16)
        return dot(dispatch, rows).astype(BF16)

    def to_experts(rows):
        return lax.all_to_all(rows, EXPERT, split_axis=0, concat_axis=0, tiled=True)

    def quarter(h):
        return lax.dynamic_slice_in_dim(tokens, place[h] * chunk, chunk, axis=1)

    def go_home(totals):
        homes = []
        for h in range(2):
            total = totals[h].reshape(RING * GROUPS, half, part)
            axes = (AXES[1 - h], *EXPERT)
            homes.append(lax.all_to_all(total, axes, split_axis=0, concat_axis=0, tiled=True))
        return homes

    def finish(home):
        total = 0.0
        chosen = 0.0
        for h in range(2):
            own = jnp.broadcast_to(slots[None, :, h], (RING, GROUPS, half)).reshape(1, -1)
            choose = jnp.concatenate([target[:, k : k + 1] == own for k in range(2)], axis=0).astype(BF16)
            chosen += dot(choose, home[h].reshape(-1, part))
        for k in range(2):
            total += route_weights[:, k : k + 1] * chosen[k * count_rows : (k + 1) * count_rows]
        return total.astype(BF16)

    def ordered(slices):
        return slices.transpose(1, 0, 2).reshape(count_rows, width)

    quarters = jnp.stack([placed(quarter(h), h).reshape(GROUPS, half, chunk) for h in range(2)], axis=1)
    got = to_experts(quarters)
    rows_g = to_experts(placed(out_grad, None))
    near, far = gathered([got[:, h].reshape(ROWS, chunk) for h in range(2)])
    hidden, to_gate, to_up = forward(places, near, far, w_gate, w_up)
    out_parts = ring_parts(places, places, [hidden], [w_down], False)
    out_totals, sent = ring_sums(out_parts)
    d_gate, d_up = hidden_grad(rows_g, w_down, to_gate, to_up, out_parts[1][4])
    grad_parts = ring_parts(places, sent[0], [d_gate, d_up], [w_gate, w_up], True)
    grad_totals, _ = ring_sums(grad_parts)
    moe_out = ordered(lax.all_gather(finish(go_home(out_totals)), AXES, axis=0))
    copies = jnp.broadcast_to(finish(go_home(grad_totals))[None], (RING * RING, count_rows, part))
    input_grad = ordered(lax.all_to_all(copies, AXES, split_axis=0, concat_axis=0, tiled=True))
    return moe_out, input_grad


def solution(mesh):
    fine = Mesh(mesh.devices.reshape(4, 2, 4, 4), ("z", "core", "y", "x"))
    row = P(EXPERT, None)
    wide = P(EXPERT, None, ("y", "x"))
    tall = P(EXPERT, ("y", "x"), None)
    return jax.shard_map(
        per_device,
        mesh=fine,
        in_specs=(row, row, row, row, wide, wide, tall),
        out_specs=(row, row),
        check_vma=False,
    )
```

profile of v0, /device:TPU:0, one launch (start us, length us, event | category | flops | bytes accessed | tf_op | source)
XLA Modules:
  0.0 321.9 jit_solution(15921482215573896211)
XLA Ops:
  13.6 5.4 %all-to-all-start = ((bf16[8,2,32,1536]{3,2,1,0:T(8,128)(2,1)}), bf16[8,2,32,1536]{3,2,1,0:T(8,128)(2,1)S(1)}, u32[]{:S(2)}, u32[]{:S(2)}) async-start(bf16[8,2,32,1536]{3,2,1,0:T(8,128)(2,1)} %pad_maximum_fusion), calls=%async_computation | async-start | bytes 3145728 | tf_op jit(solution)/shard_map/all_to_all | solution.py:355
  19.0 4.5 %convolution_convert_fusion = bf16[512,6144]{1,0:T(8,128)(2,1)} fusion(bf16[128,6144]{1,0:T(8,128)(2,1)S(1)} %copy-done, s32[128]{0:T(128)S(1)} %get-tuple-element.111, s32[128]{0:T(128)S(1)} %get-tuple-element.110), kind=kOutput, calls=%fused_computation | convolution fusion | flops 808648704 | bytes 7865344 | tf_op jit(solution)/shard_map/dot_general | solution.py:26
  23.5 17.1 %all-to-all-done = bf16[8,2,32,1536]{3,2,1,0:T(8,128)(2,1)S(1)} async-done(((bf16[8,2,32,1536]{3,2,1,0:T(8,128)(2,1)}), bf16[8,2,32,1536]{3,2,1,0:T(8,128)(2,1)S(1)}, u32[]{:S(2)}, u32[]{:S(2)}) %all-to-all-start) | async-done | bytes 1572896 | tf_op jit(solution)/shard_map/all_to_all | solution.py:355
  40.6 4.8 %all-to-all-start.3 = ((bf16[8,64,6144]{2,1,0:T(8,128)(2,1)}), bf16[8,64,6144]{2,1,0:T(8,128)(2,1)}, u32[]{:S(2)}, u32[]{:S(2)}) async-start(bf16[8,64,6144]{2,1,0:T(8,128)(2,1)} %bitcast.75), calls=%async_computation.3 | async-start | bytes 12582912 | tf_op jit(solution)/shard_map/all_to_all | solution.py:355
  52.2 14.5 %collective-permute-done.refs_0_.refs_2_ = bf16[256,1536]{1,0:T(8,128)(2,1)S(1)} collective-permute-done((bf16[256,1536]{1,0:T(8,128)(2,1)S(1)}, bf16[256,1536]{1,0:T(8,128)(2,1)S(1)}, u32[]{:S(2)}, u32[]{:S(2)}) %collective-permute-start) | collective-permute-done | bytes 786464 | tf_op jit(solution)/shard_map/ppermute | solution.py:22
  69.9 3.0 collective-permute-start.5
  76.2 2.8 copy-done.2
  81.8 6.7 %forward_near.1 = (f32[512,512]{1,0:T(8,128)S(1)}, f32[512,512]{1,0:T(8,128)S(1)}) custom-call(s32[2]{0:T(128)S(1)} %pad_add_fusion.6.place.after, bf16[256,1536]{1,0:T(8,128)(2,1)S(1)} %bitcast.74, bf16[256,1536]{1,0:T(8,128)(2,1)S(1)} %collective-permute-done.2.refs_2_.refs_1_, bf16[256,1536]{1,0:T(8,128)(2,1)S(1)} %collective-permute-done.refs_0_.refs_2_, ...), custom_call_target="tpu_custom_call" | custom-call | flops 4831838208 | bytes 23592960 | tf_op jit(solution)/shard_map/forward_near/pallas_call | solution.py:143
  91.3 2.8 copy-done.5
  96.8 8.3 %out_parts.1 = (bf16[2,4,128,384]{3,2,1,0:T(8,128)(2,1)S(1)}, bf16[2,4,128,384]{3,2,1,0:T(8,128)(2,1)S(1)}, bf16[4,128,384]{2,1,0:T(8,128)(2,1)S(1)}, bf16[4,128...) custom-call(s32[2]{0:T(128)S(1)} %pad_add_fusion.6.place.after, ...), custom_call_target="tpu_custom_call" | custom-call | flops 3221225472 | bytes 18874368 | tf_op jit(solution)/shard_map/out_parts/pallas_call | solution.py:270
  105.6 2.9 collective-permute-start.11
  108.5 3.2 %collective-permute-start.9 = (bf16[2,4,128,384]{3,2,1,0:T(8,128)(2,1)S(1)}, bf16[2,4,128,384]{3,2,1,0:T(8,128)(2,1)S(1)}, u32[]{:S(2)}, u32[]{:S(2)}) collective-permute-start(bf16[2,4,128,384]{3,2,1,0:T(8,128)(2,1)S(1)} %get-tuple-element.54), channel_id=1, source_target_pairs={{0,3},{1,0},{2,1},{3,2},{4,7},{5,4},{6,5},{7,6},{8,11},{9,8},{10,9... | collective-permute-start | bytes 2359304 | tf_op jit(solution)/shard_map/ppermute | solution.py:22
  111.7 11.8 %collective-permute-done.10.refs_5_.refs_6_ = bf16[2,4,128,384]{3,2,1,0:T(8,128)(2,1)S(1)} collective-permute-done((bf16[2,4,128,384]{3,2,1,0:T(8,128)(2,1)S(1)}, bf16[2,4,128,384]{3,2,1,0:T(8,128)(2,1)S(1)}, u32[]{:S(2)}, u32[]{:S(2)}) %collective-permute-start.10) | collective-permute-done | bytes 786464 | tf_op jit(solution)/shard_map/ppermute | solution.py:22
  127.6 3.2 %collective-permute-start.13 = (bf16[4,128,384]{2,1,0:T(8,128)(2,1)S(1)}, bf16[4,128,384]{2,1,0:T(8,128)(2,1)S(1)}, u32[]{:S(2)}, u32[]{:S(2)}) collective-permute-start(bf16[4,128,384]{2,1,0:T(8,128)(2,1)S(1)} %get-tuple-element.62), channel_id=1, source_target_pairs={{0,3},{1,0},{2,1},{3,2},{4,7},{5,4},{6,5},{7,6},{8,11},{9,8},{10,9... | collective-permute-start | bytes 1179656 | tf_op jit(solution)/shard_map/ppermute | solution.py:22
  130.8 3.2 %collective-permute-start.15 = (bf16[4,128,384]{2,1,0:T(8,128)(2,1)S(1)}, bf16[4,128,384]{2,1,0:T(8,128)(2,1)S(1)}, u32[]{:S(2)}, u32[]{:S(2)}) collective-permute-start(bf16[4,128,384]{2,1,0:T(8,128)(2,1)S(1)} %get-tuple-element.65), channel_id=1, source_target_pairs={{0,12},{4,0},{8,4},{12,8},{1,13},{5,1},{9,5},{13,9},{2,14},{6,2},{... | collective-permute-start | bytes 1179656 | tf_op jit(solution)/shard_map/ppermute | solution.py:22
  136.1 3.7 %collective-permute-done.14.refs_8_ = bf16[4,128,384]{2,1,0:T(8,128)(2,1)S(1)} collective-permute-done((bf16[4,128,384]{2,1,0:T(8,128)(2,1)S(1)}, bf16[4,128,384]{2,1,0:T(8,128)(2,1)S(1)}, u32[]{:S(2)}, u32[]{:S(2)}) %collective-permute-start.14) | collective-permute-done | bytes 393248 | tf_op jit(solution)/shard_map/ppermute | solution.py:22
  142.2 7.4 %all-to-all-start.1 = ((bf16[32,32,384]{2,1,0:T(8,128)(2,1)}), bf16[32,32,384]{2,1,0:T(8,128)(2,1)}, u32[]{:S(2)}, u32[]{:S(2)}) async-start(bf16[32,32,384]{2,1,0:T(8,128)(2,1)} %bitcast.67), calls=%async_computation.1 | async-start | bytes 1572864 | tf_op jit(solution)/shard_map/all_to_all | solution.py:365
  152.4 9.5 %hidden_grad.1 = (bf16[512,512]{1,0:T(8,128)(2,1)S(1)}, bf16[512,512]{1,0:T(8,128)(2,1)S(1)}) custom-call(bf16[8,2,32,6144]{3,2,1,0:T(8,128)(2,1)} %bitcast.24.rows, bf16[512,6144]{1,0:T(8,128)(2,1)S(1)} %bitcast.65, f32[512,512]{1,0:T(8,128)S(1)} %get-tuple-element.68.to_gate, f32[512,512]{1,0:T(8,128)S(1)} %get-tuple-element.69.to_up, ...), custom_call_target="tpu_custom_call" | custom-call | flops 3221225472 | bytes 12582912 | tf_op jit(solution)/shard_map/hidden_grad/pallas_call | solution.py:178
  161.9 15.0 %grad_parts.1 = (bf16[2,4,128,384]{3,2,1,0:T(8,128)(2,1)}, bf16[2,4,128,384]{3,2,1,0:T(8,128)(2,1)}, bf16[4,128,384]{2,1,0:T(8,128)(2,1)S(1)}, bf16[4,128,384]{2...) custom-call(s32[2]{0:T(128)S(1)} %pad_add_fusion.6.place.after, ...), custom_call_target="tpu_custom_call" | custom-call | flops 6442450944 | bytes 31457280 | tf_op jit(solution)/shard_map/grad_parts/pallas_call | solution.py:270
  181.1 3.2 %collective-permute-start.17 = (bf16[2,4,128,384]{3,2,1,0:T(8,128)(2,1)}, bf16[2,4,128,384]{3,2,1,0:T(8,128)(2,1)S(1)}, u32[]{:S(2)}, u32[]{:S(2)}) collective-permute-start(bf16[2,4,128,384]{3,2,1,0:T(8,128)(2,1)} %get-tuple-element.74), channel_id=1, source_target_pairs={{0,3},{1,0},{2,1},{3,2},{4,7},{5,4},{6,5},{7,6},{8,11},{9,8},{10,9... | collective-permute-start | bytes 2359304 | tf_op jit(solution)/shard_map/ppermute | solution.py:22
  184.4 3.0 collective-permute-start.18
  187.8 4.9 %all-to-all-start.2 = ((bf16[32,32,384]{2,1,0:T(8,128)(2,1)}), bf16[32,32,384]{2,1,0:T(8,128)(2,1)}, u32[]{:S(2)}, u32[]{:S(2)}) async-start(bf16[32,32,384]{2,1,0:T(8,128)(2,1)} %bitcast.66), calls=%async_computation.2 | async-start | bytes 1572864 | tf_op jit(solution)/shard_map/all_to_all | solution.py:365
  192.7 10.5 %collective-permute-done.16.refs_4_.refs_1_ = bf16[2,4,128,384]{3,2,1,0:T(8,128)(2,1)S(1)} collective-permute-done((bf16[2,4,128,384]{3,2,1,0:T(8,128)(2,1)}, bf16[2,4,128,384]{3,2,1,0:T(8,128)(2,1)S(1)}, u32[]{:S(2)}, u32[]{:S(2)}) %collective-permute-start.16) | collective-permute-done | bytes 786464 | tf_op jit(solution)/shard_map/ppermute | solution.py:22
  209.7 3.2 %collective-permute-start.21 = (bf16[4,128,384]{2,1,0:T(8,128)(2,1)S(1)}, bf16[4,128,384]{2,1,0:T(8,128)(2,1)S(1)}, u32[]{:S(2)}, u32[]{:S(2)}) collective-permute-start(bf16[4,128,384]{2,1,0:T(8,128)(2,1)S(1)} %get-tuple-element.82), channel_id=1, source_target_pairs={{0,3},{1,0},{2,1},{3,2},{4,7},{5,4},{6,5},{7,6},{8,11},{9,8},{10,9... | collective-permute-start | bytes 1179656 | tf_op jit(solution)/shard_map/ppermute | solution.py:22
  216.2 4.2 %collective-permute-done.20.refs_3_ = bf16[4,128,384]{2,1,0:T(8,128)(2,1)S(1)} collective-permute-done((bf16[4,128,384]{2,1,0:T(8,128)(2,1)S(1)}, bf16[4,128,384]{2,1,0:T(8,128)(2,1)S(1)}, u32[]{:S(2)}, u32[]{:S(2)}) %collective-permute-start.20) | collective-permute-done | bytes 393248 | tf_op jit(solution)/shard_map/ppermute | solution.py:22
  225.4 6.9 %all-to-all-start.4 = ((bf16[32,32,384]{2,1,0:T(8,128)(2,1)}), bf16[32,32,384]{2,1,0:T(8,128)(2,1)S(1)}, u32[]{:S(2)}, u32[]{:S(2)}) async-start(bf16[32,32,384]{2,1,0:T(8,128)(2,1)} %bitcast.68), calls=%async_computation.4 | async-start | bytes 1572864 | tf_op jit(solution)/shard_map/all_to_all | solution.py:365
  232.9 13.3 %all-to-all-done.4 = bf16[32,32,384]{2,1,0:T(8,128)(2,1)S(1)} async-done(((bf16[32,32,384]{2,1,0:T(8,128)(2,1)}), bf16[32,32,384]{2,1,0:T(8,128)(2,1)S(1)}, u32[]{:S(2)}, u32[]{:S(2)}) %all-to-all-start.4) | async-done | bytes 786464 | tf_op jit(solution)/shard_map/all_to_all | solution.py:365
  246.2 3.9 %all-to-all-start.5 = ((bf16[32,32,384]{2,1,0:T(8,128)(2,1)}), bf16[32,32,384]{2,1,0:T(8,128)(2,1)S(1)}, u32[]{:S(2)}, u32[]{:S(2)}) async-start(bf16[32,32,384]{2,1,0:T(8,128)(2,1)} %bitcast.27), calls=%async_computation.5 | async-start | bytes 1572864 | tf_op jit(solution)/shard_map/all_to_all | solution.py:365
  253.8 10.1 %all-to-all-done.5 = bf16[32,32,384]{2,1,0:T(8,128)(2,1)S(1)} async-done(((bf16[32,32,384]{2,1,0:T(8,128)(2,1)}), bf16[32,32,384]{2,1,0:T(8,128)(2,1)S(1)}, u32[]{:S(2)}, u32[]{:S(2)}) %all-to-all-start.5) | async-done | bytes 786464 | tf_op jit(solution)/shard_map/all_to_all | solution.py:365
  265.4 28.7 %all_to_all.39 = bf16[16,128,384]{2,1,0:T(8,128)(2,1)S(1)} all-to-all(bf16[16,128,384]{2,1,0:T(8,128)(2,1)S(1)} %broadcast_in_dim.40), channel_id=1, replica_groups=mesh['z'=4,'core'=2,'y'=4,'x'=4] {'x','y'}, dimensions={0} | all-to-all | bytes 3145728 | tf_op jit(solution)/shard_map/all_to_all | solution.py:394
  296.6 15.1 %all-gather.3.cloned.1.call-done = bf16[2048,384]{1,0:T(8,128)(2,1)} async-done(((bf16[128,384]{1,0:T(8,128)(2,1)}), bf16[2048,384]{1,0:T(8,128)(2,1)}) %all-gather.3.cloned.1.call-update) | async-done | bytes 1572880 | tf_op jit(solution)/shard_map/all_gather | solution.py:392
  311.7 2.9 copy.47
  (120 shorter events, 67.4 us)
Async XLA Ops:
  13.6 27.0 %all-to-all-start = ((bf16[8,2,32,1536]{3,2,1,0:T(8,128)(2,1)}), bf16[8,2,32,1536]{3,2,1,0:T(8,128)(2,1)S(1)}, u32[]{:S(2)}, u32[]{:S(2)}) async-start(bf16[8,2,32,1536]{3,2,1,0:T(8,128)(2,1)} %pad_maximum_fusion), calls=%async_computation | async-start | bytes 3145728 | tf_op jit(solution)/shard_map/all_to_all | solution.py:355
  40.6 101.6 %all-to-all-start.3 = ((bf16[8,64,6144]{2,1,0:T(8,128)(2,1)}), bf16[8,64,6144]{2,1,0:T(8,128)(2,1)}, u32[]{:S(2)}, u32[]{:S(2)}) async-start(bf16[8,64,6144]{2,1,0:T(8,128)(2,1)} %bitcast.75), calls=%async_computation.3 | async-start | bytes 12582912 | tf_op jit(solution)/shard_map/all_to_all | solution.py:355
  45.5 21.1 %collective-permute-start = (bf16[256,1536]{1,0:T(8,128)(2,1)S(1)}, bf16[256,1536]{1,0:T(8,128)(2,1)S(1)}, u32[]{:S(2)}, u32[]{:S(2)}) collective-permute-start(bf16[256,1536]{1,0:T(8,128)(2,1)S(1)} %bitcast.72), channel_id=1, source_target_pairs={{0,1},{1,2},{2,3},{3,0},{4,5},{5,6},{6,7},{7,4},{8,9},{9,10},{10,1... | collective-permute-start | bytes 2359304 | tf_op jit(solution)/shard_map/ppermute | solution.py:22
  47.1 20.8 %collective-permute-start.1 = (bf16[256,1536]{1,0:T(8,128)(2,1)S(1)}, bf16[256,1536]{1,0:T(8,128)(2,1)S(1)}, u32[]{:S(2)}, u32[]{:S(2)}) collective-permute-start(bf16[256,1536]{1,0:T(8,128)(2,1)S(1)} %bitcast.69), channel_id=1, source_target_pairs={{0,4},{4,8},{8,12},{12,0},{1,5},{5,9},{9,13},{13,1},{2,6},{6,10},{... | collective-permute-start | bytes 2359304 | tf_op jit(solution)/shard_map/ppermute | solution.py:22
  48.7 19.2 %collective-permute-start.2 = (bf16[256,1536]{1,0:T(8,128)(2,1)S(1)}, bf16[256,1536]{1,0:T(8,128)(2,1)S(1)}, u32[]{:S(2)}, u32[]{:S(2)}) collective-permute-start(bf16[256,1536]{1,0:T(8,128)(2,1)S(1)} %bitcast.73), channel_id=1, source_target_pairs={{0,3},{1,0},{2,1},{3,2},{4,7},{5,4},{6,5},{7,6},{8,11},{9,8},{10,9... | collective-permute-start | bytes 2359304 | tf_op jit(solution)/shard_map/ppermute | solution.py:22
  50.4 19.0 %collective-permute-start.3 = (bf16[256,1536]{1,0:T(8,128)(2,1)S(1)}, bf16[256,1536]{1,0:T(8,128)(2,1)S(1)}, u32[]{:S(2)}, u32[]{:S(2)}) collective-permute-start(bf16[256,1536]{1,0:T(8,128)(2,1)S(1)} %bitcast.70), channel_id=1, source_target_pairs={{0,12},{4,0},{8,4},{12,8},{1,13},{5,1},{9,5},{13,9},{2,14},{6,2},{... | collective-permute-start | bytes 2359304 | tf_op jit(solution)/shard_map/ppermute | solution.py:22
  69.5 19.0 %collective-permute-start.4 = (bf16[128,1536]{1,0:T(8,128)(2,1)S(1)}, bf16[128,1536]{1,0:T(8,128)(2,1)S(1)}, u32[]{:S(2)}, u32[]{:S(2)}) collective-permute-start(bf16[128,1536]{1,0:T(8,128)(2,1)S(1)} %get-tuple-element.45), channel_id=1, source_target_pairs={{0,1},{1,2},{2,3},{3,0},{4,5},{5,6},{6,7},{7,4},{8,9},{9,10},{10,1... | collective-permute-start | bytes 1179656 | tf_op jit(solution)/shard_map/ppermute | solution.py:22
  69.9 18.6 %collective-permute-start.5 = (bf16[128,1536]{1,0:T(8,128)(2,1)S(1)}, bf16[128,1536]{1,0:T(8,128)(2,1)S(1)}, u32[]{:S(2)}, u32[]{:S(2)}) collective-permute-start(bf16[128,1536]{1,0:T(8,128)(2,1)S(1)} %get-tuple-element.46), channel_id=1, source_target_pairs={{0,3},{1,0},{2,1},{3,2},{4,7},{5,4},{6,5},{7,6},{8,11},{9,8},{10,9... | collective-permute-start | bytes 1179656 | tf_op jit(solution)/shard_map/ppermute | solution.py:22
  72.8 15.7 %collective-permute-start.6 = (bf16[128,1536]{1,0:T(8,128)(2,1)S(1)}, bf16[128,1536]{1,0:T(8,128)(2,1)S(1)}, u32[]{:S(2)}, u32[]{:S(2)}) collective-permute-start(bf16[128,1536]{1,0:T(8,128)(2,1)S(1)} %get-tuple-element.47), channel_id=1, source_target_pairs={{0,4},{4,8},{8,12},{12,0},{1,5},{5,9},{9,13},{13,1},{2,6},{6,10},{... | collective-permute-start | bytes 1179656 | tf_op jit(solution)/shard_map/ppermute | solution.py:22
  74.4 14.1 %collective-permute-start.7 = (bf16[128,1536]{1,0:T(8,128)(2,1)S(1)}, bf16[128,1536]{1,0:T(8,128)(2,1)S(1)}, u32[]{:S(2)}, u32[]{:S(2)}) collective-permute-start(bf16[128,1536]{1,0:T(8,128)(2,1)S(1)} %get-tuple-element.48), channel_id=1, source_target_pairs={{0,12},{4,0},{8,4},{12,8},{1,13},{5,1},{9,5},{13,9},{2,14},{6,2},{... | collective-permute-start | bytes 1179656 | tf_op jit(solution)/shard_map/ppermute | solution.py:22
  105.2 18.3 %collective-permute-start.10 = (bf16[2,4,128,384]{3,2,1,0:T(8,128)(2,1)S(1)}, bf16[2,4,128,384]{3,2,1,0:T(8,128)(2,1)S(1)}, u32[]{:S(2)}, u32[]{:S(2)}) collective-permute-start(bf16[2,4,128,384]{3,2,1,0:T(8,128)(2,1)S(1)} %get-tuple-element.59), channel_id=1, source_target_pairs={{0,4},{4,8},{8,12},{12,0},{1,5},{5,9},{9,13},{13,1},{2,6},{6,10},{... | collective-permute-start | bytes 2359304 | tf_op jit(solution)/shard_map/ppermute | solution.py:22
  105.6 17.9 %collective-permute-start.11 = (bf16[2,4,128,384]{3,2,1,0:T(8,128)(2,1)S(1)}, bf16[2,4,128,384]{3,2,1,0:T(8,128)(2,1)S(1)}, u32[]{:S(2)}, u32[]{:S(2)}) collective-permute-start(bf16[2,4,128,384]{3,2,1,0:T(8,128)(2,1)S(1)} %get-tuple-element.60), channel_id=1, source_target_pairs={{0,12},{4,0},{8,4},{12,8},{1,13},{5,1},{9,5},{13,9},{2,14},{6,2},{... | collective-permute-start | bytes 2359304 | tf_op jit(solution)/shard_map/ppermute | solution.py:22
  108.5 17.7 %collective-permute-start.8 = (bf16[2,4,128,384]{3,2,1,0:T(8,128)(2,1)S(1)}, bf16[2,4,128,384]{3,2,1,0:T(8,128)(2,1)S(1)}, u32[]{:S(2)}, u32[]{:S(2)}) collective-permute-start(bf16[2,4,128,384]{3,2,1,0:T(8,128)(2,1)S(1)} %get-tuple-element.53), channel_id=1, source_target_pairs={{0,1},{1,2},{2,3},{3,0},{4,5},{5,6},{6,7},{7,4},{8,9},{9,10},{10,1... | collective-permute-start | bytes 2359304 | tf_op jit(solution)/shard_map/ppermute | solution.py:22
  108.5 17.7 %collective-permute-start.9 = (bf16[2,4,128,384]{3,2,1,0:T(8,128)(2,1)S(1)}, bf16[2,4,128,384]{3,2,1,0:T(8,128)(2,1)S(1)}, u32[]{:S(2)}, u32[]{:S(2)}) collective-permute-start(bf16[2,4,128,384]{3,2,1,0:T(8,128)(2,1)S(1)} %get-tuple-element.54), channel_id=1, source_target_pairs={{0,3},{1,0},{2,1},{3,2},{4,7},{5,4},{6,5},{7,6},{8,11},{9,8},{10,9... | collective-permute-start | bytes 2359304 | tf_op jit(solution)/shard_map/ppermute | solution.py:22
  126.6 9.3 %collective-permute-start.12 = (bf16[4,128,384]{2,1,0:T(8,128)(2,1)S(1)}, bf16[4,128,384]{2,1,0:T(8,128)(2,1)S(1)}, u32[]{:S(2)}, u32[]{:S(2)}) collective-permute-start(bf16[4,128,384]{2,1,0:T(8,128)(2,1)S(1)} %get-tuple-element.61.after), channel_id=1, source_target_pairs={{0,1},{1,2},{2,3},{3,0},{4,5},{5,6},{6,7},{7,4},{8,9},{9,10},{10,1... | collective-permute-start | bytes 1179656 | tf_op jit(solution)/shard_map/ppermute | solution.py:22
  127.6 8.5 %collective-permute-start.13 = (bf16[4,128,384]{2,1,0:T(8,128)(2,1)S(1)}, bf16[4,128,384]{2,1,0:T(8,128)(2,1)S(1)}, u32[]{:S(2)}, u32[]{:S(2)}) collective-permute-start(bf16[4,128,384]{2,1,0:T(8,128)(2,1)S(1)} %get-tuple-element.62), channel_id=1, source_target_pairs={{0,3},{1,0},{2,1},{3,2},{4,7},{5,4},{6,5},{7,6},{8,11},{9,8},{10,9... | collective-permute-start | bytes 1179656 | tf_op jit(solution)/shard_map/ppermute | solution.py:22
  130.8 9.0 %collective-permute-start.14 = (bf16[4,128,384]{2,1,0:T(8,128)(2,1)S(1)}, bf16[4,128,384]{2,1,0:T(8,128)(2,1)S(1)}, u32[]{:S(2)}, u32[]{:S(2)}) collective-permute-start(bf16[4,128,384]{2,1,0:T(8,128)(2,1)S(1)} %get-tuple-element.64), channel_id=1, source_target_pairs={{0,4},{4,8},{8,12},{12,0},{1,5},{5,9},{9,13},{13,1},{2,6},{6,10},{... | collective-permute-start | bytes 1179656 | tf_op jit(solution)/shard_map/ppermute | solution.py:22
  130.8 9.0 %collective-permute-start.15 = (bf16[4,128,384]{2,1,0:T(8,128)(2,1)S(1)}, bf16[4,128,384]{2,1,0:T(8,128)(2,1)S(1)}, u32[]{:S(2)}, u32[]{:S(2)}) collective-permute-start(bf16[4,128,384]{2,1,0:T(8,128)(2,1)S(1)} %get-tuple-element.65), channel_id=1, source_target_pairs={{0,12},{4,0},{8,4},{12,8},{1,13},{5,1},{9,5},{13,9},{2,14},{6,2},{... | collective-permute-start | bytes 1179656 | tf_op jit(solution)/shard_map/ppermute | solution.py:22
  142.2 45.6 %all-to-all-start.1 = ((bf16[32,32,384]{2,1,0:T(8,128)(2,1)}), bf16[32,32,384]{2,1,0:T(8,128)(2,1)}, u32[]{:S(2)}, u32[]{:S(2)}) async-start(bf16[32,32,384]{2,1,0:T(8,128)(2,1)} %bitcast.67), calls=%async_computation.1 | async-start | bytes 1572864 | tf_op jit(solution)/shard_map/all_to_all | solution.py:365
  181.1 22.1 %collective-permute-start.16 = (bf16[2,4,128,384]{3,2,1,0:T(8,128)(2,1)}, bf16[2,4,128,384]{3,2,1,0:T(8,128)(2,1)S(1)}, u32[]{:S(2)}, u32[]{:S(2)}) collective-permute-start(bf16[2,4,128,384]{3,2,1,0:T(8,128)(2,1)} %get-tuple-element.73), channel_id=1, source_target_pairs={{0,1},{1,2},{2,3},{3,0},{4,5},{5,6},{6,7},{7,4},{8,9},{9,10},{10,1... | collective-permute-start | bytes 2359304 | tf_op jit(solution)/shard_map/ppermute | solution.py:22
  181.1 23.2 %collective-permute-start.17 = (bf16[2,4,128,384]{3,2,1,0:T(8,128)(2,1)}, bf16[2,4,128,384]{3,2,1,0:T(8,128)(2,1)S(1)}, u32[]{:S(2)}, u32[]{:S(2)}) collective-permute-start(bf16[2,4,128,384]{3,2,1,0:T(8,128)(2,1)} %get-tuple-element.74), channel_id=1, source_target_pairs={{0,3},{1,0},{2,1},{3,2},{4,7},{5,4},{6,5},{7,6},{8,11},{9,8},{10,9... | collective-permute-start | bytes 2359304 | tf_op jit(solution)/shard_map/ppermute | solution.py:22
  184.4 20.9 %collective-permute-start.18 = (bf16[2,4,128,384]{3,2,1,0:T(8,128)(2,1)}, bf16[2,4,128,384]{3,2,1,0:T(8,128)(2,1)S(1)}, u32[]{:S(2)}, u32[]{:S(2)}) collective-permute-start(bf16[2,4,128,384]{3,2,1,0:T(8,128)(2,1)} %get-tuple-element.79), channel_id=1, source_target_pairs={{0,4},{4,8},{8,12},{12,0},{1,5},{5,9},{9,13},{13,1},{2,6},{6,10},{... | collective-permute-start | bytes 2359304 | tf_op jit(solution)/shard_map/ppermute | solution.py:22
  187.3 19.0 %collective-permute-start.19 = (bf16[2,4,128,384]{3,2,1,0:T(8,128)(2,1)}, bf16[2,4,128,384]{3,2,1,0:T(8,128)(2,1)S(1)}, u32[]{:S(2)}, u32[]{:S(2)}) collective-permute-start(bf16[2,4,128,384]{3,2,1,0:T(8,128)(2,1)} %get-tuple-element.80), channel_id=1, source_target_pairs={{0,12},{4,0},{8,4},{12,8},{1,13},{5,1},{9,5},{13,9},{2,14},{6,2},{... | collective-permute-start | bytes 2359304 | tf_op jit(solution)/shard_map/ppermute | solution.py:22
  187.8 37.7 %all-to-all-start.2 = ((bf16[32,32,384]{2,1,0:T(8,128)(2,1)}), bf16[32,32,384]{2,1,0:T(8,128)(2,1)}, u32[]{:S(2)}, u32[]{:S(2)}) async-start(bf16[32,32,384]{2,1,0:T(8,128)(2,1)} %bitcast.66), calls=%async_computation.2 | async-start | bytes 1572864 | tf_op jit(solution)/shard_map/all_to_all | solution.py:365
  209.3 14.1 %copy-start.10 = (bf16[4,256,384]{2,1,0:T(8,128)(2,1)S(1)}, bf16[4,256,384]{2,1,0:T(8,128)(2,1)}, u32[]{:S(2)}) copy-start(bf16[4,256,384]{2,1,0:T(8,128)(2,1)} %copy-done.9) | copy-start | bytes 2359300
  209.7 10.8 %collective-permute-start.20 = (bf16[4,128,384]{2,1,0:T(8,128)(2,1)S(1)}, bf16[4,128,384]{2,1,0:T(8,128)(2,1)S(1)}, u32[]{:S(2)}, u32[]{:S(2)}) collective-permute-start(bf16[4,128,384]{2,1,0:T(8,128)(2,1)S(1)} %get-tuple-element.81), channel_id=1, source_target_pairs={{0,1},{1,2},{2,3},{3,0},{4,5},{5,6},{6,7},{7,4},{8,9},{9,10},{10,1... | collective-permute-start | bytes 1179656 | tf_op jit(solution)/shard_map/ppermute | solution.py:22
  209.7 10.7 %collective-permute-start.21 = (bf16[4,128,384]{2,1,0:T(8,128)(2,1)S(1)}, bf16[4,128,384]{2,1,0:T(8,128)(2,1)S(1)}, u32[]{:S(2)}, u32[]{:S(2)}) collective-permute-start(bf16[4,128,384]{2,1,0:T(8,128)(2,1)S(1)} %get-tuple-element.82), channel_id=1, source_target_pairs={{0,3},{1,0},{2,1},{3,2},{4,7},{5,4},{6,5},{7,6},{8,11},{9,8},{10,9... | collective-permute-start | bytes 1179656 | tf_op jit(solution)/shard_map/ppermute | solution.py:22
  213.0 10.2 %collective-permute-start.22 = (bf16[4,128,384]{2,1,0:T(8,128)(2,1)S(1)}, bf16[4,128,384]{2,1,0:T(8,128)(2,1)S(1)}, u32[]{:S(2)}, u32[]{:S(2)}) collective-permute-start(bf16[4,128,384]{2,1,0:T(8,128)(2,1)S(1)} %get-tuple-element.84), channel_id=1, source_target_pairs={{0,4},{4,8},{8,12},{12,0},{1,5},{5,9},{9,13},{13,1},{2,6},{6,10},{... | collective-permute-start | bytes 1179656 | tf_op jit(solution)/shard_map/ppermute | solution.py:22
  214.8 8.6 %collective-permute-start.23 = (bf16[4,128,384]{2,1,0:T(8,128)(2,1)S(1)}, bf16[4,128,384]{2,1,0:T(8,128)(2,1)S(1)}, u32[]{:S(2)}, u32[]{:S(2)}) collective-permute-start(bf16[4,128,384]{2,1,0:T(8,128)(2,1)S(1)} %get-tuple-element.85), channel_id=1, source_target_pairs={{0,12},{4,0},{8,4},{12,8},{1,13},{5,1},{9,5},{13,9},{2,14},{6,2},{... | collective-permute-start | bytes 1179656 | tf_op jit(solution)/shard_map/ppermute | solution.py:22
  225.4 20.8 %all-to-all-start.4 = ((bf16[32,32,384]{2,1,0:T(8,128)(2,1)}), bf16[32,32,384]{2,1,0:T(8,128)(2,1)S(1)}, u32[]{:S(2)}, u32[]{:S(2)}) async-start(bf16[32,32,384]{2,1,0:T(8,128)(2,1)} %bitcast.68), calls=%async_computation.4 | async-start | bytes 1572864 | tf_op jit(solution)/shard_map/all_to_all | solution.py:365
  246.2 17.7 %all-to-all-start.5 = ((bf16[32,32,384]{2,1,0:T(8,128)(2,1)}), bf16[32,32,384]{2,1,0:T(8,128)(2,1)S(1)}, u32[]{:S(2)}, u32[]{:S(2)}) async-start(bf16[32,32,384]{2,1,0:T(8,128)(2,1)} %bitcast.27), calls=%async_computation.5 | async-start | bytes 1572864 | tf_op jit(solution)/shard_map/all_to_all | solution.py:365
  250.1 61.6 %all-gather.3.cloned.1.call-start = ((), (), s32[]{:S(2)}) async-start(), calls=%async_computation.7 | async-start | bytes 1671168 | tf_op jit(solution)/shard_map/all_gather | solution.py:392
  (22 other events, 70.0 us)
Sparse Core Ops, SparseCore 0:
  265.3 46.3 all-gather.2
where the time goes:
time: 328 us; the launch traced here: 322 us
  waiting for transfers between devices  114 us (35%)
  starting transfers between devices  73.1 us (22%)
  Pallas kernels  44.9 us (14%)
  local copies, waits for them, and re-layouts  31.8 us (10%)
  blocking collectives  28.7 us (9%)
  between operations  14.8 us (5%)
  matrix products  11.3 us (3%)
  other arithmetic  3.38 us (1%)
    ppermute x24, waiting for transfers between devices, shift(): lax.ppermute(rows, axis, [(i, (i + step) % RING) for i in range(RING)])  58.2 us
    ppermute x24, starting transfers between devices, shift(): lax.ppermute(rows, axis, [(i, (i + step) % RING) for i in range(RING)])  39.7 us
    all_to_all x1, blocking collectives, per_device(): lax.all_to_all(copies, AXES, split_axis=0, concat_axis=0, tiled=True)  28.7 us
    unnamed x48, local copies, waits for them, and re-layouts  27 us
    all_to_all x4, waiting for transfers between devices, go_home(): lax.all_to_all(total, axes, split_axis=0, concat_axis=0, tiled=True)  23.5 us
    pallas_call x2, Pallas kernels, ring_parts(): pl.pallas_call(functools.partial(parts_kernel, len(acts), transposed), ou...  23.3 us
    all_to_all x4, starting transfers between devices, go_home(): lax.all_to_all(total, axes, split_axis=0, concat_axis=0, tiled=True)  23.1 us
    all_to_all x2, waiting for transfers between devices, to_experts(): return lax.all_to_all(rows, EXPERT, split_axis=0, concat_axis=0, tiled=True)  17.1 us
  transfers between devices with their start and end apart: 31, of which 19 were waited for; matrix products, arithmetic and copies ran while one was open for 4% of the time, Pallas kernels for 14%

commit v1 on v0

v1 whole, which is shorter than its diff:
```python
import jax
import jax.numpy as jnp
from jax import lax
from jax.experimental import pallas as pl
from jax.experimental.pallas import tpu as pltpu
from jax.sharding import Mesh
from jax.sharding import PartitionSpec as P

F32 = jnp.float32
BF16 = jnp.bfloat16
EXPERT = ("z", "core")
AXES = ("x", "y")
RING = 4
GROUPS = 8
ROWS = 256
MIB = 1 << 20


def shift(rows, axis, step):
    return lax.ppermute(rows, axis, [(i, (i + step) % RING) for i in range(RING)])


def dot(a, b):
    return jnp.dot(a, b, preferred_element_type=F32)


def dot_t(a, b):
    return lax.dot_general(a, b, (((1,), (1,)), ((), ())), preferred_element_type=F32)


def slots_of(routes, per_expert):
    flat = routes.reshape(-1)
    order = jnp.arange(flat.shape[0], dtype=jnp.int32)
    earlier = (flat[:, None] == flat[None, :]) & (order[:, None] > order[None, :])
    before = jnp.sum(earlier.astype(jnp.int32), axis=1)
    return (flat * per_expert + before).reshape(routes.shape)


def whole(shape):
    return pl.BlockSpec(shape, lambda *_: (0,) * len(shape))


def halves_kernel(*refs):
    for source, to in zip(refs[:4], refs[4:]):
        to[...] = source[...]


def gathered(owns):
    rows, chunk = owns[0].shape
    half = rows // 2
    befores = [shift(own, axis, 1) for own, axis in zip(owns, AXES)]
    afters = [shift(own, axis, -1) for own, axis in zip(owns, AXES)]
    top = pl.BlockSpec((half, chunk), lambda i: (0, 0))
    bottom = pl.BlockSpec((half, chunk), lambda i: (1, 0))
    send = pl.pallas_call(
        halves_kernel,
        out_shape=[jax.ShapeDtypeStruct((half, chunk), BF16)] * 4,
        grid=(1,),
        in_specs=[top, top, bottom, bottom],
        out_specs=[whole((half, chunk))] * 4,
        compiler_params=params(),
        cost_estimate=cost(0, 16 * half * chunk),
        name="halves",
    )(*befores, *afters)
    near = [[owns[h], afters[h], befores[h]] for h in range(2)]
    far = [[shift(send[h], AXES[h], 1), shift(send[2 + h], AXES[h], -1)] for h in range(2)]
    return near, far


def forward_near_kernel(place, *refs):
    rows, (wg, wu), (gate, up) = refs[:6], refs[6:8], refs[8:]
    for h in range(2):
        for i in range(3):

            @pl.when((pl.program_id(0) == h) & (pl.program_id(1) == i))
            def _(h=h, i=i):
                block = rows[3 * h + i][...]
                for acc, w in ((gate, wg), (up, wu)):
                    value = dot(block, w[...])
                    acc[...] = value if i == 0 else acc[...] + value


def emit(at_step, distance, place, outs, product):
    part = outs[4].shape[-1]
    top, bottom = slice(0, ROWS // 2), slice(ROWS // 2, ROWS)
    for h in range(2):
        plus, minus, plus_later, minus_later, own = outs[5 * h : 5 * h + 5]
        chunk = (place[h] + distance) % RING
        columns = [
            pl.multiple_of((chunk * RING + j if h == 0 else j * RING + chunk) * part, part) for j in range(RING)
        ]
        values = product(h, columns).astype(BF16)
        for j in range(RING):
            value = values[:, j * part : (j + 1) * part]
            if at_step == 0:
                plus[0, j] = value[top]
                minus[0, j] = value[bottom]
            elif at_step == 1:
                plus_later[j] = value[top]
                plus[0, j] = value[bottom]
            elif at_step == 2:
                minus[0, j] = value[top]
                minus_later[j] = value[bottom]
            else:
                own[j] = value


def emitted(width, before, more):
    part = width // RING // RING
    half = (RING, ROWS // 2, part)
    shapes = [(2 + more, *half), (2 + more, *half), half, half, (RING, ROWS, part)]
    specs = [
        pl.BlockSpec((1, *half), lambda i, place: (jnp.clip(i - before, 0, 1 + more), 0, 0, 0)),
        pl.BlockSpec((1, *half), lambda i, place: (jnp.clip(i - before - 1, 0, 1 + more), 0, 0, 0)),
        whole(half),
        whole(half),
        whole((RING, ROWS, part)),
    ]
    return [jax.ShapeDtypeStruct(s, BF16) for s in shapes] * 2, specs * 2


DISTANCES = (2, 1, 3, 0)


def forward_far_kernel(place, *refs):
    rows, (wg, wu, gate, up, wd), (to_gate, to_up) = refs[:4], refs[4:9], refs[9:11]
    outs, (hidden, down, sem) = refs[11:21], refs[21:]
    step = pl.program_id(0)
    load = pltpu.make_async_copy(wd, down, sem)

    @pl.when(step == 0)
    def _():
        load.start()

    for h in range(2):

        @pl.when(step == h)
        def _(h=h):
            block = jnp.concatenate([rows[2 * h][...], rows[2 * h + 1][...]], axis=0)
            g = gate[...] + dot(block, wg[...])
            u = up[...] + dot(block, wu[...])
            s = 1.0 / (1.0 + jnp.exp(-g))
            hidden[h * ROWS : (h + 1) * ROWS] = (g * s * u).astype(BF16)
            to_gate[...] = u * s * (1.0 + g * (1.0 - s))
            to_up[...] = g * s

    @pl.when(step == 1)
    def _():
        load.wait()

    part = outs[4].shape[-1]

    def product(h, columns):
        weights = jnp.concatenate([down[:, pl.ds(at, part)] for at in columns], axis=1)
        return dot(hidden[h * ROWS : (h + 1) * ROWS], weights)

    for at_step, distance in enumerate(DISTANCES):

        @pl.when(step == 2 + at_step)
        def _(at_step=at_step, distance=distance):
            emit(at_step, distance, place, outs, product)


STEPS = 4


def backward_kernel(place, rows, wd, to_gate, to_up, wg, wu, *refs):
    waiting, outs, (acc, d_gate, d_up, gate, up, sems) = refs[:8], refs[8:18], refs[18:]
    step = pl.program_id(0)
    loads = [pltpu.make_async_copy(wg, gate, sems.at[0]), pltpu.make_async_copy(wu, up, sems.at[1])]

    @pl.when(step == 0)
    def _():
        for load in loads:
            load.start()

    @pl.when(step < STEPS)
    def _():
        value = dot_t(jnp.concatenate([rows[:, h].reshape(ROWS, rows.shape[-1]) for h in range(2)], axis=0), wd[...])

        @pl.when(step == 0)
        def _():
            acc[...] = value

        @pl.when(step > 0)
        def _():
            acc[...] += value

    @pl.when(step == STEPS - 1)
    def _():
        d_gate[...] = (acc[...] * to_gate[...]).astype(BF16)
        d_up[...] = (acc[...] * to_up[...]).astype(BF16)
        for load in loads:
            load.wait()

    part = outs[4].shape[-1]

    def product(h, columns):
        mine = slice(h * ROWS, (h + 1) * ROWS)
        gates, ups = (jnp.concatenate([w[pl.ds(at, part)] for at in columns], axis=0) for w in (gate, up))
        return dot_t(d_gate[mine], gates) + dot_t(d_up[mine], ups)

    for at_step, distance in enumerate(DISTANCES):

        @pl.when(step == STEPS + at_step)
        def _(at_step=at_step, distance=distance):
            emit(at_step, distance, place, outs, product)
            for h in range(2):
                if at_step >= 2:
                    own, got = waiting[2 * (at_step - 2) + h], waiting[4 + 2 * (at_step - 2) + h]
                    outs[5 * h + at_step - 2][0] = (own[...].astype(F32) + got[0].astype(F32)).astype(BF16)


def params(mib=58):
    return pltpu.CompilerParams(vmem_limit_bytes=mib * MIB)


def cost(flops, moved):
    return pl.CostEstimate(flops=int(flops), bytes_accessed=int(moved), transcendentals=0)


def forward(place, near, far, w_gate, w_up, w_down):
    width, hid = w_gate.shape
    chunk = width // RING

    def weights(distance):
        return pl.BlockSpec((chunk, hid), lambda *at: ((at[-1][at[0]] + distance(at)) % RING, 0))

    def by_half(*_):
        return pl.BlockSpec((ROWS, hid), lambda *at: (at[0], 0))

    near_w = weights(lambda at: jnp.where(at[1] == 2, 3, at[1]))
    rows = near[0] + near[1]
    gate, up = pl.pallas_call(
        forward_near_kernel,
        out_shape=[jax.ShapeDtypeStruct((2 * ROWS, hid), F32)] * 2,
        grid_spec=pltpu.PrefetchScalarGridSpec(
            num_scalar_prefetch=1,
            grid=(2, 3),
            in_specs=[whole(r.shape) for r in rows] + [near_w, near_w],
            out_specs=[by_half()] * 2,
        ),
        compiler_params=params(),
        cost_estimate=cost(6 * ROWS * width * hid, 3 * width * ROWS + 6 * width * hid),
        name="forward_near",
    )(place, *rows, w_gate, w_up)
    rows = far[0] + far[1]
    far_w = pl.BlockSpec((chunk, hid), lambda i, place: ((place[jnp.minimum(i, 1)] + 2) % RING, 0))
    half_rows = pl.BlockSpec((ROWS, hid), lambda i, place: (jnp.minimum(i, 1), 0))
    shapes, specs = emitted(width, 2, 0)
    outs = pl.pallas_call(
        forward_far_kernel,
        out_shape=[jax.ShapeDtypeStruct((2 * ROWS, hid), F32)] * 2 + shapes,
        grid_spec=pltpu.PrefetchScalarGridSpec(
            num_scalar_prefetch=1,
            grid=(6,),
            in_specs=[whole(r.shape) for r in rows]
            + [far_w, far_w, half_rows, half_rows, pl.BlockSpec(memory_space=pl.ANY)],
            out_specs=[half_rows] * 2 + specs,
            scratch_shapes=[
                pltpu.VMEM((2 * ROWS, hid), BF16),
                pltpu.VMEM((hid, width), BF16),
                pltpu.SemaphoreType.DMA,
            ],
        ),
        compiler_params=params(),
        cost_estimate=cost(6 * ROWS * width * hid, 2 * width * ROWS + 4 * width * hid + 16 * ROWS * hid),
        name="forward_far",
    )(place, *rows, w_gate, w_up, gate, up, w_down)
    return outs[0], outs[1], (outs[2:7], outs[7:])


def backward(place, rows, w_gate, w_up, w_down, to_gate, to_up, parts, first):
    hid, width = w_down.shape
    count = 2 * ROWS
    block = width // STEPS
    rows = rows.reshape(GROUPS, 2, ROWS // GROUPS, width)
    shapes, specs = emitted(width, STEPS, 1)
    anywhere = pl.BlockSpec(memory_space=pl.ANY)
    half = parts[0][2].shape
    waiting = [p[2] for p in parts] + [p[3] for p in parts]
    outs = pl.pallas_call(
        backward_kernel,
        out_shape=shapes,
        grid_spec=pltpu.PrefetchScalarGridSpec(
            num_scalar_prefetch=1,
            grid=(STEPS + 4,),
            in_specs=[
                pl.BlockSpec((*rows.shape[:3], block), lambda i, place: (0, 0, 0, jnp.minimum(i, STEPS - 1))),
                pl.BlockSpec((hid, block), lambda i, place: (0, jnp.minimum(i, STEPS - 1))),
                whole((count, hid)),
                whole((count, hid)),
                anywhere,
                anywhere,
            ]
            + [whole(half)] * 4
            + [pl.BlockSpec((1, *half), lambda i, place: (0, 0, 0, 0))] * 4,
            out_specs=specs,
            scratch_shapes=[
                pltpu.VMEM((count, hid), F32),
                pltpu.VMEM((count, hid), BF16),
                pltpu.VMEM((count, hid), BF16),
                pltpu.VMEM((width, hid), BF16),
                pltpu.VMEM((width, hid), BF16),
                pltpu.SemaphoreType.DMA((2,)),
            ],
        ),
        compiler_params=params(),
        cost_estimate=cost(6 * count * width * hid, 4 * width * count + 6 * width * hid),
        name="backward",
    )(place, rows, w_down, to_gate, to_up, w_gate, w_up, *waiting, *first)
    return outs[:5], outs[5:]


def combine_kernel(target, weights, *refs):
    homes, mixed = refs[:-1], refs[-1]
    tokens = target.shape[0]
    total = jnp.zeros((tokens, mixed.shape[-1]), F32)
    for h, home in enumerate(homes):
        at = lax.broadcasted_iota(jnp.int32, (tokens, home.shape[0]), 1)
        slot = ((at >> 5) & 7) * 64 + h * 32 + (at & 31)
        for k in range(2):
            choose = jnp.where(target[:, k : k + 1] == slot, 1.0, 0.0).astype(BF16)
            total += weights[:, k : k + 1] * dot(choose, home[...])
    for copy in range(mixed.shape[0]):
        mixed[copy] = total.astype(BF16)


def combine(homes, target, weights, copies):
    tokens = target.shape[0]
    part = homes[0].shape[-1]
    shape = (copies, tokens, part)
    return pl.pallas_call(
        combine_kernel,
        out_shape=jax.ShapeDtypeStruct(shape, BF16),
        grid=(1,),
        in_specs=[whole(target.shape), whole(weights.shape)] + [whole(h.shape) for h in homes],
        out_specs=whole(shape),
        compiler_params=params(),
        cost_estimate=cost(sum(4 * tokens * h.size for h in homes), 2 * (sum(h.size for h in homes) + copies * tokens * part)),
        name="combine",
    )(target, weights, *homes)


def add(*terms):
    return sum(t.astype(F32) for t in terms).astype(BF16)


def add_total(total, own, first_plus, first_minus, later_plus, later_minus):
    half = ROWS // 2
    total[:, :half] = add(own[:, :half], later_plus, first_minus)
    total[:, half:] = add(own[:, half:], first_plus, later_minus)


def middle_kernel(*refs):
    later, near, totals = refs[:8], refs[8:18], refs[22:]
    for own, got, send in zip(later[:4], later[4:], refs[18:22]):
        send[...] = add(own[...], got[0])
    for h in range(2):
        own, first_plus, first_minus, later_plus, later_minus = near[5 * h : 5 * h + 5]
        add_total(totals[h], own[...], first_plus[0], first_minus[0], later_plus[0], later_minus[0])


def total_kernel(after, *refs):
    for h in range(2):
        own, first_plus, first_minus, later_plus, later_minus = refs[5 * h : 5 * h + 5]
        add_total(refs[10 + h], own[...], first_plus[0], first_minus[0], later_plus[...], later_minus[...])


def both_ways(plus, minus):
    return [shift(p, axis, 1) for p, axis in zip(plus, AXES)] + [shift(m, axis, -1) for m, axis in zip(minus, AXES)]


def ring_middle(parts, got, out_parts, out_first):
    half, full = parts[0][2].shape, parts[0][4].shape
    blocks = [pl.BlockSpec((1, *half), lambda i, n=n: (n, 0, 0, 0)) for n in range(3)]
    operands = [p[2] for p in parts] + [p[3] for p in parts] + got
    specs = [whole(half)] * 4 + [blocks[0]] * 4
    for h in range(2):
        operands += [out_parts[h][4], out_first[h], out_first[2 + h], got[h], got[2 + h]]
        specs += [whole(full), blocks[1], blocks[1], blocks[2], blocks[2]]
    outs = pl.pallas_call(
        middle_kernel,
        out_shape=[jax.ShapeDtypeStruct(half, BF16)] * 4 + [jax.ShapeDtypeStruct(full, BF16)] * 2,
        grid=(1,),
        in_specs=specs,
        out_specs=[whole(half)] * 4 + [whole(full)] * 2,
        compiler_params=params(),
        cost_estimate=cost(0, 28 * ROWS * full[0] * full[2]),
        name="ring_middle",
    )(*operands)
    return outs[:4], outs[4:]


def ring_end(parts, first, later, after):
    half, full = parts[0][2].shape, parts[0][4].shape
    second = pl.BlockSpec((1, *half), lambda i: (1, 0, 0, 0))
    operands, specs = [after], [pl.BlockSpec(memory_space=pl.ANY)]
    for h in range(2):
        operands += [parts[h][4], first[h], first[2 + h], later[h], later[2 + h]]
        specs += [whole(full), second, second, whole(half), whole(half)]
    return pl.pallas_call(
        total_kernel,
        out_shape=[jax.ShapeDtypeStruct(full, BF16)] * 2,
        grid=(1,),
        in_specs=specs,
        out_specs=[whole(full)] * 2,
        compiler_params=params(),
        cost_estimate=cost(0, 16 * ROWS * full[0] * full[2]),
        name="ring_end",
    )(*operands)


def per_device(tokens, routes, route_weights, out_grad, w_gate, w_up, w_down):
    count_rows, width = tokens.shape
    per_expert = 4 * count_rows // GROUPS
    half = per_expert // 2
    chunk = width // RING
    part = chunk // RING
    w_gate, w_up, w_down = w_gate[0], w_up[0], w_down[0]
    place = [lax.axis_index(axis) for axis in AXES]
    places = jnp.stack(place).astype(jnp.int32)
    target = slots_of(routes, per_expert)
    slots = jnp.arange(GROUPS * per_expert, dtype=jnp.int32).reshape(GROUPS, 2, half)

    def placed(rows, h):
        mine = slots if h is None else slots[:, h]
        mine = mine.reshape(-1, 1)
        dispatch = ((mine == target[None, :, 0]) | (mine == target[None, :, 1])).astype(BF16)
        return dot(dispatch, rows).astype(BF16)

    def to_experts(rows):
        return lax.all_to_all(rows, EXPERT, split_axis=0, concat_axis=0, tiled=True)

    def quarter(h):
        return lax.dynamic_slice_in_dim(tokens, place[h] * chunk, chunk, axis=1)

    def go_home(totals):
        homes = []
        for h in range(2):
            total = totals[h].reshape(RING * GROUPS, half, part)
            axes = (AXES[1 - h], *EXPERT)
            homes.append(lax.all_to_all(total, axes, split_axis=0, concat_axis=0, tiled=True))
        return homes

    def ordered(slices):
        return slices.transpose(1, 0, 2).reshape(count_rows, width)

    quarters = jnp.stack([placed(quarter(h), h).reshape(GROUPS, half, chunk) for h in range(2)], axis=1)
    got = to_experts(quarters)
    rows_g = to_experts(placed(out_grad, None))
    near, far = gathered([got[:, h].reshape(ROWS, chunk) for h in range(2)])
    to_gate, to_up, out_parts = forward(places, near, far, w_gate, w_up, w_down)
    out_first = both_ways([p[0] for p in out_parts], [p[1] for p in out_parts])
    grad_parts = backward(places, rows_g, w_gate, w_up, w_down, to_gate, to_up, out_parts, out_first)
    got = both_ways([p[0] for p in grad_parts], [p[1] for p in grad_parts])
    send, out_totals = ring_middle(grad_parts, got, out_parts, out_first)
    grad_later = both_ways(send[:2], send[2:])
    mixed = combine([h.reshape(-1, part) for h in go_home(out_totals)], target, route_weights, 1)[0]
    moe_out = ordered(lax.all_gather(mixed, AXES, axis=0))
    grad_home = go_home(ring_end(grad_parts, got, grad_later, mixed))
    copies = combine([h.reshape(-1, part) for h in grad_home], target, route_weights, RING * RING)
    input_grad = ordered(lax.all_to_all(copies, AXES, split_axis=0, concat_axis=0, tiled=True))
    return moe_out, input_grad


def solution(mesh):
    fine = Mesh(mesh.devices.reshape(4, 2, 4, 4), ("z", "core", "y", "x"))
    row = P(EXPERT, None)
    wide = P(EXPERT, None, ("y", "x"))
    tall = P(EXPERT, ("y", "x"), None)
    return jax.shard_map(
        per_device,
        mesh=fine,
        in_specs=(row, row, row, row, wide, wide, tall),
        out_specs=(row, row),
        check_vma=False,
    )
```

time: 328 us -> 323 us (0.985); the launches traced: 322 us -> 322 us
  blocking collectives: 28.7 us -> 68.9 us
  Pallas kernels: 44.9 us -> 68 us
  starting transfers between devices: 73.1 us -> 50.2 us
  waiting for transfers between devices: 114 us -> 95.8 us
  local copies, waits for them, and re-layouts: 31.8 us -> 14.5 us
  matrix products: 11.3 us -> 7.27 us
    all_to_all x0 -> x2, blocking collectives: none -> 40.2 us  [go_home(): lax.all_to_all(total, axes, split_axis=0, concat_axis=0, tiled=True)]
    unnamed x48 -> x68, local copies, waits for them, and re-layouts: 27 us -> 10.8 us
    all_gather x1, waiting for transfers between devices: 15.1 us -> 0.01 us  [per_device(): moe_out = ordered(lax.all_gather(mixed, AXES, axis=0))]
    all_to_all x4 -> x2, starting transfers between devices: 23.1 us -> 9.55 us  [go_home(): lax.all_to_all(total, axes, split_axis=0, concat_axis=0, tiled=True)]
    pallas_call x1, Pallas kernels: 2.74 us -> 13.9 us  [forward(): pl.pallas_call(forward_far_kernel, out_shape=[jax.ShapeDtypeStruct((2 * R...]
    ppermute x24 -> x20, starting transfers between devices: 39.7 us -> 30.4 us  [shift(): lax.ppermute(rows, axis, [(i, (i + step) % RING) for i in range(RING)])]
    pallas_call x1, Pallas kernels: 6.7 us -> 13.3 us  [forward(): pl.pallas_call(forward_near_kernel, out_shape=[jax.ShapeDtypeStruct((2 *...]
    dot_general x7 -> x3, matrix products: 11.3 us -> 7.27 us  [dot(): return jnp.dot(a, b, preferred_element_type=F32)]
  transfers between devices with their start and end apart: 31 -> 25, of which waited for: 19 -> 14; matrix products, arithmetic and copies ran while one was open for 4% -> 3% of each run, Pallas kernels for 14% -> 11%
where the time goes in v1:
time: 323 us; the launch traced here: 322 us
  waiting for transfers between devices  95.8 us (30%)
  blocking collectives  68.9 us (21%)
  Pallas kernels  68 us (21%)
  starting transfers between devices  50.2 us (16%)
  local copies, waits for them, and re-layouts  14.5 us (4%)
  between operations  14.4 us (4%)
  matrix products  7.27 us (2%)
    ppermute x20, waiting for transfers between devices, shift(): lax.ppermute(rows, axis, [(i, (i + step) % RING) for i in range(RING)])  58.3 us
    all_to_all x2, blocking collectives, go_home(): lax.all_to_all(total, axes, split_axis=0, concat_axis=0, tiled=True)  40.2 us
    ppermute x20, starting transfers between devices, shift(): lax.ppermute(rows, axis, [(i, (i + step) % RING) for i in range(RING)])  30.4 us
    all_to_all x1, blocking collectives, per_device(): lax.all_to_all(copies, AXES, split_axis=0, concat_axis=0, tiled=True)  28.7 us
    pallas_call x1, Pallas kernels, backward(): pl.pallas_call(backward_kernel, out_shape=shapes, grid_spec=pltpu.Prefetc...  22.9 us
    all_to_all x2, waiting for transfers between devices, go_home(): lax.all_to_all(total, axes, split_axis=0, concat_axis=0, tiled=True)  19.6 us
    all_to_all x2, waiting for transfers between devices, to_experts(): return lax.all_to_all(rows, EXPERT, split_axis=0, concat_axis=0, tiled=True)  17.1 us
    pallas_call x1, Pallas kernels, forward(): pl.pallas_call(forward_far_kernel, out_shape=[jax.ShapeDtypeStruct((2 * R...  13.9 us
  transfers between devices with their start and end apart: 25, of which 14 were waited for; matrix products, arithmetic and copies ran while one was open for 3% of the time, Pallas kernels for 11%

profile of v1, /device:TPU:0, one launch (start us, length us, event | category | flops | bytes accessed | tf_op | source)
XLA Modules:
  0.0 321.8 jit_solution(1322492675176763898)
XLA Ops:
  13.9 5.4 %all-to-all-start.1 = ((bf16[8,2,32,1536]{3,2,1,0:T(8,128)(2,1)}), bf16[8,2,32,1536]{3,2,1,0:T(8,128)(2,1)S(1)}, u32[]{:S(2)}, u32[]{:S(2)}) async-start(bf16[8,2,32,1536]{3,2,1,0:T(8,128)(2,1)} %pad_maximum_fusion), calls=%async_computation.1 | async-start | bytes 3145728 | tf_op jit(solution)/shard_map/all_to_all | solution.py:433
  19.3 4.5 %convolution_convert_fusion = bf16[512,6144]{1,0:T(8,128)(2,1)} fusion(bf16[128,6144]{1,0:T(8,128)(2,1)S(1)} %copy-done, s32[128]{0:T(128)S(1)} %get-tuple-element.83, s32[128]{0:T(128)S(1)} %get-tuple-element.82), kind=kOutput, calls=%fused_computation | convolution fusion | flops 808648704 | bytes 7865344 | tf_op jit(solution)/shard_map/dot_general | solution.py:24
  23.7 17.1 %all-to-all-done.1 = bf16[8,2,32,1536]{3,2,1,0:T(8,128)(2,1)S(1)} async-done(((bf16[8,2,32,1536]{3,2,1,0:T(8,128)(2,1)}), bf16[8,2,32,1536]{3,2,1,0:T(8,128)(2,1)S(1)}, u32[]{:S(2)}, u32[]{:S(2)}) %all-to-all-start.1) | async-done | bytes 1572896 | tf_op jit(solution)/shard_map/all_to_all | solution.py:433
  40.9 4.8 %all-to-all-start = ((bf16[8,64,6144]{2,1,0:T(8,128)(2,1)}), bf16[8,64,6144]{2,1,0:T(8,128)(2,1)}, u32[]{:S(2)}, u32[]{:S(2)}) async-start(bf16[8,64,6144]{2,1,0:T(8,128)(2,1)} %bitcast.30), calls=%async_computation | async-start | bytes 12582912 | tf_op jit(solution)/shard_map/all_to_all | solution.py:433
  48.9 1.7 collective-permute-start.2
  52.9 13.9 %collective-permute-done.refs_0_.refs_2_ = bf16[256,1536]{1,0:T(8,128)(2,1)S(1)} collective-permute-done((bf16[256,1536]{1,0:T(8,128)(2,1)S(1)}, bf16[256,1536]{1,0:T(8,128)(2,1)S(1)}, u32[]{:S(2)}, u32[]{:S(2)}) %collective-permute-start) | collective-permute-done | bytes 786464 | tf_op jit(solution)/shard_map/ppermute | solution.py:20
  70.5 2.5 halves.1
  74.3 2.1 collective-permute-start.5
  79.6 13.3 %forward_near.1 = (f32[512,512]{1,0:T(8,128)}, f32[512,512]{1,0:T(8,128)}) custom-call(s32[2]{0:T(128)} %pad_add_fusion.place, bf16[256,1536]{1,0:T(8,128)(2,1)} %bitcast.57, bf16[256,1536]{1,0:T(8,128)(2,1)} %copy-done.14, bf16[256,1536]{1,0:T(8,128)(2,1)} %copy-done.12, bf16[256,1536]{1,0:T(8,128)(2,1)} %bitcast.54, bf16[256,1536]{1,0:T(8,128)(2,1)} %copy-done.15, ...), custom_call_target="tpu_custom_call" | custom-call | flops 4831838208 | bytes 23592960 | tf_op jit(solution)/shard_map/forward_near/pallas_call | solution.py:234
  94.1 13.9 %forward_far.1 = (f32[512,512]{1,0:T(8,128)}, f32[512,512]{1,0:T(8,128)}, bf16[2,4,128,384]{3,2,1,0:T(8,128)(2,1)}, bf16[2,4,128,384]{3,2,1,0:T(8,128)(2,1)}, bf...) custom-call(s32[2]{0:T(128)} %pad_add_fusion.place, ...), custom_call_target="tpu_custom_call" | custom-call | flops 4831838208 | bytes 17825792 | tf_op jit(solution)/shard_map/forward_far/pallas_call | solution.py:251
  110.3 1.9 collective-permute-start.8
  112.3 13.3 %collective-permute-done.10.refs_6_.refs_10_ = bf16[2,4,128,384]{3,2,1,0:T(8,128)(2,1)S(1)} collective-permute-done((bf16[2,4,128,384]{3,2,1,0:T(8,128)(2,1)}, bf16[2,4,128,384]{3,2,1,0:T(8,128)(2,1)S(1)}, u32[]{:S(2)}, u32[]{:S(2)}) %collective-permute-start.10) | collective-permute-done | bytes 786464 | tf_op jit(solution)/shard_map/ppermute | solution.py:20
  130.7 22.9 %backward.1 = (bf16[3,4,128,384]{3,2,1,0:T(8,128)(2,1)}, bf16[3,4,128,384]{3,2,1,0:T(8,128)(2,1)}, bf16[4,128,384]{2,1,0:T(8,128)(2,1)}, bf16[4,128,384]{2,1,0:T...) custom-call(s32[2]{0:T(128)} %pad_add_fusion.place, ...), custom_call_target="tpu_custom_call" | custom-call | flops 9663676416 | bytes 31457280 | tf_op jit(solution)/shard_map/backward/pallas_call | solution.py:282
  154.1 3.2 collective-permute-start.14
  157.3 3.0 collective-permute-start.15
  160.2 18.6 %collective-permute-done.12.refs_4_.refs_11_.refs_1_ = bf16[3,4,128,384]{3,2,1,0:T(8,128)(2,1)S(1)} collective-permute-done((bf16[3,4,128,384]{3,2,1,0:T(8,128)(2,1)}, bf16[3,4,128,384]{3,2,1,0:T(8,128)(2,1)S(1)}, u32[]{:S(2)}, u32[]{:S(2)}) %collective-permute-start.12) | collective-permute-done | bytes 1179680 | tf_op jit(solution)/shard_map/ppermute | solution.py:20
  179.1 1.8 collective-permute-done.15.refs_7_.refs_17_
  181.9 5.1 %ring_middle.1 = (bf16[4,128,384]{2,1,0:T(8,128)(2,1)}, bf16[4,128,384]{2,1,0:T(8,128)(2,1)}, bf16[4,128,384]{2,1,0:T(8,128)(2,1)}, bf16[4,128,384]{2,1,0:T(8,12...) custom-call(bf16[4,128,384]{2,1,0:T(8,128)(2,1)} %get-tuple-element.54.refs_0_, ...), custom_call_target="tpu_custom_call" | custom-call | bytes 11010048 | tf_op jit(solution)/shard_map/ring_middle/pallas_call | solution.py:382
  187.0 21.5 %all_to_all.39 = bf16[32,32,384]{2,1,0:T(8,128)(2,1)} all-to-all(bf16[32,32,384]{2,1,0:T(8,128)(2,1)} %bitcast.51), channel_id=1, replica_groups=mesh['z'=4,'core'=2,'y'=4,'x'=4] {'y','z','core'}, dimensions={0} | all-to-all | bytes 1572864 | tf_op jit(solution)/shard_map/all_to_all | solution.py:443
  208.5 3.9 %all-to-all-start.3 = ((bf16[32,32,384]{2,1,0:T(8,128)(2,1)}), bf16[32,32,384]{2,1,0:T(8,128)(2,1)S(1)}, u32[]{:S(2)}, u32[]{:S(2)}) async-start(bf16[32,32,384]{2,1,0:T(8,128)(2,1)} %bitcast.15), calls=%async_computation.3 | async-start | bytes 1572864 | tf_op jit(solution)/shard_map/all_to_all | solution.py:443
  212.5 1.8 collective-permute-start.16
  216.2 2.8 collective-permute-start.19
  219.7 6.5 %all-to-all-done.3 = bf16[32,32,384]{2,1,0:T(8,128)(2,1)S(1)} async-done(((bf16[32,32,384]{2,1,0:T(8,128)(2,1)}), bf16[32,32,384]{2,1,0:T(8,128)(2,1)S(1)}, u32[]{:S(2)}, u32[]{:S(2)}) %all-to-all-start.3) | async-done | bytes 786464 | tf_op jit(solution)/shard_map/all_to_all | solution.py:443
  227.2 2.9 combine.2
  230.0 3.4 %collective-permute-done.16.refs_3_ = bf16[4,128,384]{2,1,0:T(8,128)(2,1)S(1)} collective-permute-done((bf16[4,128,384]{2,1,0:T(8,128)(2,1)}, bf16[4,128,384]{2,1,0:T(8,128)(2,1)S(1)}, u32[]{:S(2)}, u32[]{:S(2)}) %collective-permute-start.16) | collective-permute-done | bytes 393248 | tf_op jit(solution)/shard_map/ppermute | solution.py:20
  234.6 3.8 %ring_end.1 = (bf16[4,256,384]{2,1,0:T(8,128)(2,1)}, bf16[4,256,384]{2,1,0:T(8,128)(2,1)}) custom-call(bf16[128,384]{1,0:T(8,128)(2,1)} %bitcast.48, bf16[4,256,384]{2,1,0:T(8,128)(2,1)} %get-tuple-element.66.refs_0_, bf16[3,4,128,384]{3,2,1,0:T(8,128)(2,1)} %copy-done.2, bf16[3,4,128,384]{3,2,1,0:T(8,128)(2,1)} %copy-done.4, ...), custom_call_target="tpu_custom_call" | custom-call | bytes 6291456 | tf_op jit(solution)/shard_map/ring_end/pallas_call | solution.py:402
  238.4 5.6 %all-to-all-start.4 = ((bf16[32,32,384]{2,1,0:T(8,128)(2,1)}), bf16[32,32,384]{2,1,0:T(8,128)(2,1)S(1)}, u32[]{:S(2)}, u32[]{:S(2)}) async-start(bf16[32,32,384]{2,1,0:T(8,128)(2,1)} %bitcast.50), calls=%async_computation.4 | async-start | bytes 1572864 | tf_op jit(solution)/shard_map/all_to_all | solution.py:443
  244.8 13.1 %all-to-all-done.4 = bf16[32,32,384]{2,1,0:T(8,128)(2,1)S(1)} async-done(((bf16[32,32,384]{2,1,0:T(8,128)(2,1)}), bf16[32,32,384]{2,1,0:T(8,128)(2,1)S(1)}, u32[]{:S(2)}, u32[]{:S(2)}) %all-to-all-start.4) | async-done | bytes 786464 | tf_op jit(solution)/shard_map/all_to_all | solution.py:443
  257.9 18.6 %all_to_all.40 = bf16[32,32,384]{2,1,0:T(8,128)(2,1)} all-to-all(bf16[32,32,384]{2,1,0:T(8,128)(2,1)S(1)} %bitcast.49), channel_id=1, replica_groups=mesh['z'=4,'core'=2,'y'=4,'x'=4] {'x','z','core'}, dimensions={0} | all-to-all | bytes 1572864 | tf_op jit(solution)/shard_map/all_to_all | solution.py:443
  276.5 3.7 %combine.3 = bf16[16,128,384]{2,1,0:T(8,128)(2,1)} custom-call(s32[128,2]{1,0:T(8,128)} %copy-done.8, f32[128,2]{1,0:T(8,128)} %copy.48.weights, bf16[1024,384]{1,0:T(8,128)(2,1)} %bitcast.44, bf16[1024,384]{1,0:T(8,128)(2,1)} %bitcast.45), custom_call_target="tpu_custom_call" | custom-call | flops 402653184 | bytes 3145728 | tf_op jit(solution)/shard_map/combine/pallas_call | solution.py:333
  280.2 28.7 %all_to_all.41 = bf16[16,128,384]{2,1,0:T(8,128)(2,1)S(1)} all-to-all(bf16[16,128,384]{2,1,0:T(8,128)(2,1)} %combine.3), channel_id=1, replica_groups=mesh['z'=4,'core'=2,'y'=4,'x'=4] {'x','y'}, dimensions={0} | all-to-all | bytes 3145728 | tf_op jit(solution)/shard_map/all_to_all | solution.py:463
  311.4 1.9 copy.49
  (117 shorter events, 40.1 us)
Async XLA Ops:
  13.9 27.0 %all-to-all-start.1 = ((bf16[8,2,32,1536]{3,2,1,0:T(8,128)(2,1)}), bf16[8,2,32,1536]{3,2,1,0:T(8,128)(2,1)S(1)}, u32[]{:S(2)}, u32[]{:S(2)}) async-start(bf16[8,2,32,1536]{3,2,1,0:T(8,128)(2,1)} %pad_maximum_fusion), calls=%async_computation.1 | async-start | bytes 3145728 | tf_op jit(solution)/shard_map/all_to_all | solution.py:433
  40.9 89.0 %all-to-all-start = ((bf16[8,64,6144]{2,1,0:T(8,128)(2,1)}), bf16[8,64,6144]{2,1,0:T(8,128)(2,1)}, u32[]{:S(2)}, u32[]{:S(2)}) async-start(bf16[8,64,6144]{2,1,0:T(8,128)(2,1)} %bitcast.30), calls=%async_computation | async-start | bytes 12582912 | tf_op jit(solution)/shard_map/all_to_all | solution.py:433
  45.8 27.3 %copy-start.10 = (bf16[8,1,32,1536]{3,2,1,0:T(8,128)(2,1)}, bf16[8,1,32,1536]{3,2,1,0:T(8,128)(2,1)S(1)}, u32[]{:S(2)}) copy-start(bf16[8,1,32,1536]{3,2,1,0:T(8,128)(2,1)S(1)} %get-tuple-element.86) | copy-start | bytes 2359300
  45.8 27.3 %copy-start.11 = (bf16[8,1,32,1536]{3,2,1,0:T(8,128)(2,1)}, bf16[8,1,32,1536]{3,2,1,0:T(8,128)(2,1)S(1)}, u32[]{:S(2)}) copy-start(bf16[8,1,32,1536]{3,2,1,0:T(8,128)(2,1)S(1)} %get-tuple-element.87) | copy-start | bytes 2359300
  45.8 21.1 %collective-permute-start = (bf16[256,1536]{1,0:T(8,128)(2,1)S(1)}, bf16[256,1536]{1,0:T(8,128)(2,1)S(1)}, u32[]{:S(2)}, u32[]{:S(2)}) collective-permute-start(bf16[256,1536]{1,0:T(8,128)(2,1)S(1)} %bitcast.55), channel_id=1, source_target_pairs={{0,1},{1,2},{2,3},{3,0},{4,5},{5,6},{6,7},{7,4},{8,9},{9,10},{10,1... | collective-permute-start | bytes 2359304 | tf_op jit(solution)/shard_map/ppermute | solution.py:20
  47.4 20.8 %collective-permute-start.1 = (bf16[256,1536]{1,0:T(8,128)(2,1)S(1)}, bf16[256,1536]{1,0:T(8,128)(2,1)S(1)}, u32[]{:S(2)}, u32[]{:S(2)}) collective-permute-start(bf16[256,1536]{1,0:T(8,128)(2,1)S(1)} %bitcast.52), channel_id=1, source_target_pairs={{0,4},{4,8},{8,12},{12,0},{1,5},{5,9},{9,13},{13,1},{2,6},{6,10},{... | collective-permute-start | bytes 2359304 | tf_op jit(solution)/shard_map/ppermute | solution.py:20
  48.9 19.2 %collective-permute-start.2 = (bf16[256,1536]{1,0:T(8,128)(2,1)S(1)}, bf16[256,1536]{1,0:T(8,128)(2,1)S(1)}, u32[]{:S(2)}, u32[]{:S(2)}) collective-permute-start(bf16[256,1536]{1,0:T(8,128)(2,1)S(1)} %bitcast.56), channel_id=1, source_target_pairs={{0,3},{1,0},{2,1},{3,2},{4,7},{5,4},{6,5},{7,6},{8,11},{9,8},{10,9... | collective-permute-start | bytes 2359304 | tf_op jit(solution)/shard_map/ppermute | solution.py:20
  50.7 19.0 %collective-permute-start.3 = (bf16[256,1536]{1,0:T(8,128)(2,1)S(1)}, bf16[256,1536]{1,0:T(8,128)(2,1)S(1)}, u32[]{:S(2)}, u32[]{:S(2)}) collective-permute-start(bf16[256,1536]{1,0:T(8,128)(2,1)S(1)} %bitcast.53), channel_id=1, source_target_pairs={{0,12},{4,0},{8,4},{12,8},{1,13},{5,1},{9,5},{13,9},{2,14},{6,2},{... | collective-permute-start | bytes 2359304 | tf_op jit(solution)/shard_map/ppermute | solution.py:20
  73.1 19.8 %collective-permute-start.4 = (bf16[128,1536]{1,0:T(8,128)(2,1)}, bf16[128,1536]{1,0:T(8,128)(2,1)S(1)}, u32[]{:S(2)}, u32[]{:S(2)}) collective-permute-start(bf16[128,1536]{1,0:T(8,128)(2,1)} %get-tuple-element.38), channel_id=1, source_target_pairs={{0,1},{1,2},{2,3},{3,0},{4,5},{5,6},{6,7},{7,4},{8,9},{9,10},{10,1... | collective-permute-start | bytes 1179656 | tf_op jit(solution)/shard_map/ppermute | solution.py:20
  74.3 18.6 %collective-permute-start.5 = (bf16[128,1536]{1,0:T(8,128)(2,1)}, bf16[128,1536]{1,0:T(8,128)(2,1)S(1)}, u32[]{:S(2)}, u32[]{:S(2)}) collective-permute-start(bf16[128,1536]{1,0:T(8,128)(2,1)} %get-tuple-element.39), channel_id=1, source_target_pairs={{0,3},{1,0},{2,1},{3,2},{4,7},{5,4},{6,5},{7,6},{8,11},{9,8},{10,9... | collective-permute-start | bytes 1179656 | tf_op jit(solution)/shard_map/ppermute | solution.py:20
  76.4 16.6 %collective-permute-start.6 = (bf16[128,1536]{1,0:T(8,128)(2,1)}, bf16[128,1536]{1,0:T(8,128)(2,1)S(1)}, u32[]{:S(2)}, u32[]{:S(2)}) collective-permute-start(bf16[128,1536]{1,0:T(8,128)(2,1)} %get-tuple-element.40), channel_id=1, source_target_pairs={{0,4},{4,8},{8,12},{12,0},{1,5},{5,9},{9,13},{13,1},{2,6},{6,10},{... | collective-permute-start | bytes 1179656 | tf_op jit(solution)/shard_map/ppermute | solution.py:20
  78.0 15.0 %collective-permute-start.7 = (bf16[128,1536]{1,0:T(8,128)(2,1)}, bf16[128,1536]{1,0:T(8,128)(2,1)S(1)}, u32[]{:S(2)}, u32[]{:S(2)}) collective-permute-start(bf16[128,1536]{1,0:T(8,128)(2,1)} %get-tuple-element.41), channel_id=1, source_target_pairs={{0,12},{4,0},{8,4},{12,8},{1,13},{5,1},{9,5},{13,9},{2,14},{6,2},{... | collective-permute-start | bytes 1179656 | tf_op jit(solution)/shard_map/ppermute | solution.py:20
  108.0 17.6 %collective-permute-start.10 = (bf16[2,4,128,384]{3,2,1,0:T(8,128)(2,1)}, bf16[2,4,128,384]{3,2,1,0:T(8,128)(2,1)S(1)}, u32[]{:S(2)}, u32[]{:S(2)}) collective-permute-start(bf16[2,4,128,384]{3,2,1,0:T(8,128)(2,1)} %get-tuple-element.52), channel_id=1, source_target_pairs={{0,3},{1,0},{2,1},{3,2},{4,7},{5,4},{6,5},{7,6},{8,11},{9,8},{10,9... | collective-permute-start | bytes 2359304 | tf_op jit(solution)/shard_map/ppermute | solution.py:20
  109.7 17.2 %collective-permute-start.11 = (bf16[2,4,128,384]{3,2,1,0:T(8,128)(2,1)}, bf16[2,4,128,384]{3,2,1,0:T(8,128)(2,1)S(1)}, u32[]{:S(2)}, u32[]{:S(2)}) collective-permute-start(bf16[2,4,128,384]{3,2,1,0:T(8,128)(2,1)} %get-tuple-element.53), channel_id=1, source_target_pairs={{0,12},{4,0},{8,4},{12,8},{1,13},{5,1},{9,5},{13,9},{2,14},{6,2},{... | collective-permute-start | bytes 2359304 | tf_op jit(solution)/shard_map/ppermute | solution.py:20
  110.3 18.1 %collective-permute-start.8 = (bf16[2,4,128,384]{3,2,1,0:T(8,128)(2,1)}, bf16[2,4,128,384]{3,2,1,0:T(8,128)(2,1)S(1)}, u32[]{:S(2)}, u32[]{:S(2)}) collective-permute-start(bf16[2,4,128,384]{3,2,1,0:T(8,128)(2,1)} %get-tuple-element.50), channel_id=1, source_target_pairs={{0,1},{1,2},{2,3},{3,0},{4,5},{5,6},{6,7},{7,4},{8,9},{9,10},{10,1... | collective-permute-start | bytes 2359304 | tf_op jit(solution)/shard_map/ppermute | solution.py:20
  112.3 17.6 %collective-permute-start.9 = (bf16[2,4,128,384]{3,2,1,0:T(8,128)(2,1)}, bf16[2,4,128,384]{3,2,1,0:T(8,128)(2,1)S(1)}, u32[]{:S(2)}, u32[]{:S(2)}) collective-permute-start(bf16[2,4,128,384]{3,2,1,0:T(8,128)(2,1)} %get-tuple-element.51), channel_id=1, source_target_pairs={{0,4},{4,8},{8,12},{12,0},{1,5},{5,9},{9,13},{13,1},{2,6},{6,10},{... | collective-permute-start | bytes 2359304 | tf_op jit(solution)/shard_map/ppermute | solution.py:20
  153.7 25.1 %collective-permute-start.12 = (bf16[3,4,128,384]{3,2,1,0:T(8,128)(2,1)}, bf16[3,4,128,384]{3,2,1,0:T(8,128)(2,1)S(1)}, u32[]{:S(2)}, u32[]{:S(2)}) collective-permute-start(bf16[3,4,128,384]{3,2,1,0:T(8,128)(2,1)} %get-tuple-element.58), channel_id=1, source_target_pairs={{0,1},{1,2},{2,3},{3,0},{4,5},{5,6},{6,7},{7,4},{8,9},{9,10},{10,1... | collective-permute-start | bytes 3538952 | tf_op jit(solution)/shard_map/ppermute | solution.py:20
  154.0 25.1 %collective-permute-start.13 = (bf16[3,4,128,384]{3,2,1,0:T(8,128)(2,1)}, bf16[3,4,128,384]{3,2,1,0:T(8,128)(2,1)S(1)}, u32[]{:S(2)}, u32[]{:S(2)}) collective-permute-start(bf16[3,4,128,384]{3,2,1,0:T(8,128)(2,1)} %get-tuple-element.59), channel_id=1, source_target_pairs={{0,4},{4,8},{8,12},{12,0},{1,5},{5,9},{9,13},{13,1},{2,6},{6,10},{... | collective-permute-start | bytes 3538952 | tf_op jit(solution)/shard_map/ppermute | solution.py:20
  154.1 25.0 %collective-permute-start.14 = (bf16[3,4,128,384]{3,2,1,0:T(8,128)(2,1)}, bf16[3,4,128,384]{3,2,1,0:T(8,128)(2,1)S(1)}, u32[]{:S(2)}, u32[]{:S(2)}) collective-permute-start(bf16[3,4,128,384]{3,2,1,0:T(8,128)(2,1)} %get-tuple-element.60), channel_id=1, source_target_pairs={{0,3},{1,0},{2,1},{3,2},{4,7},{5,4},{6,5},{7,6},{8,11},{9,8},{10,9... | collective-permute-start | bytes 3538952 | tf_op jit(solution)/shard_map/ppermute | solution.py:20
  157.3 23.6 %collective-permute-start.15 = (bf16[3,4,128,384]{3,2,1,0:T(8,128)(2,1)}, bf16[3,4,128,384]{3,2,1,0:T(8,128)(2,1)S(1)}, u32[]{:S(2)}, u32[]{:S(2)}) collective-permute-start(bf16[3,4,128,384]{3,2,1,0:T(8,128)(2,1)} %get-tuple-element.61), channel_id=1, source_target_pairs={{0,12},{4,0},{8,4},{12,8},{1,13},{5,1},{9,5},{13,9},{2,14},{6,2},{... | collective-permute-start | bytes 3538952 | tf_op jit(solution)/shard_map/ppermute | solution.py:20
  187.0 27.3 %copy-start.31 = (bf16[4,128,384]{2,1,0:T(8,128)(2,1)S(1)}, bf16[4,128,384]{2,1,0:T(8,128)(2,1)}, u32[]{:S(2)}) copy-start(bf16[4,128,384]{2,1,0:T(8,128)(2,1)} %get-tuple-element.68) | copy-start | bytes 1179652
  187.0 28.8 %copy-start.30 = (bf16[4,128,384]{2,1,0:T(8,128)(2,1)S(1)}, bf16[4,128,384]{2,1,0:T(8,128)(2,1)}, u32[]{:S(2)}) copy-start(bf16[4,128,384]{2,1,0:T(8,128)(2,1)} %get-tuple-element.70) | copy-start | bytes 1179652
  187.0 29.2 %copy-start.29 = (bf16[4,128,384]{2,1,0:T(8,128)(2,1)S(1)}, bf16[4,128,384]{2,1,0:T(8,128)(2,1)}, u32[]{:S(2)}) copy-start(bf16[4,128,384]{2,1,0:T(8,128)(2,1)} %get-tuple-element.71) | copy-start | bytes 1179652
  187.0 32.0 %copy-start.28 = (f32[128,2]{0,1:T(2,128)S(1)}, f32[128,2]{0,1:T(2,128)}, u32[]{:S(2)}) copy-start(f32[128,2]{0,1:T(2,128)} %param.9) | copy-start | bytes 3076
  208.5 17.7 %all-to-all-start.3 = ((bf16[32,32,384]{2,1,0:T(8,128)(2,1)}), bf16[32,32,384]{2,1,0:T(8,128)(2,1)S(1)}, u32[]{:S(2)}, u32[]{:S(2)}) async-start(bf16[32,32,384]{2,1,0:T(8,128)(2,1)} %bitcast.15), calls=%async_computation.3 | async-start | bytes 1572864 | tf_op jit(solution)/shard_map/all_to_all | solution.py:443
  212.5 21.0 %collective-permute-start.16 = (bf16[4,128,384]{2,1,0:T(8,128)(2,1)}, bf16[4,128,384]{2,1,0:T(8,128)(2,1)S(1)}, u32[]{:S(2)}, u32[]{:S(2)}) collective-permute-start(bf16[4,128,384]{2,1,0:T(8,128)(2,1)} %get-tuple-element.67), channel_id=1, source_target_pairs={{0,1},{1,2},{2,3},{3,0},{4,5},{5,6},{6,7},{7,4},{8,9},{9,10},{10,1... | collective-permute-start | bytes 1179656 | tf_op jit(solution)/shard_map/ppermute | solution.py:20
  214.3 19.2 %collective-permute-start.17 = (bf16[4,128,384]{2,1,0:T(8,128)(2,1)S(1)}, bf16[4,128,384]{2,1,0:T(8,128)(2,1)S(1)}, u32[]{:S(2)}, u32[]{:S(2)}) collective-permute-start(bf16[4,128,384]{2,1,0:T(8,128)(2,1)S(1)} %copy-done.31), channel_id=1, source_target_pairs={{0,3},{1,0},{2,1},{3,2},{4,7},{5,4},{6,5},{7,6},{8,11},{9,8},{10,9... | collective-permute-start | bytes 1179656 | tf_op jit(solution)/shard_map/ppermute | solution.py:20
  215.8 17.7 %collective-permute-start.18 = (bf16[4,128,384]{2,1,0:T(8,128)(2,1)S(1)}, bf16[4,128,384]{2,1,0:T(8,128)(2,1)S(1)}, u32[]{:S(2)}, u32[]{:S(2)}) collective-permute-start(bf16[4,128,384]{2,1,0:T(8,128)(2,1)S(1)} %copy-done.30), channel_id=1, source_target_pairs={{0,4},{4,8},{8,12},{12,0},{1,5},{5,9},{9,13},{13,1},{2,6},{6,10},{... | collective-permute-start | bytes 1179656 | tf_op jit(solution)/shard_map/ppermute | solution.py:20
  216.2 17.3 %collective-permute-start.19 = (bf16[4,128,384]{2,1,0:T(8,128)(2,1)S(1)}, bf16[4,128,384]{2,1,0:T(8,128)(2,1)S(1)}, u32[]{:S(2)}, u32[]{:S(2)}) collective-permute-start(bf16[4,128,384]{2,1,0:T(8,128)(2,1)S(1)} %copy-done.29), channel_id=1, source_target_pairs={{0,12},{4,0},{8,4},{12,8},{1,13},{5,1},{9,5},{13,9},{2,14},{6,2},{... | collective-permute-start | bytes 1179656 | tf_op jit(solution)/shard_map/ppermute | solution.py:20
  238.4 19.5 %copy-start.9 = (bf16[4,256,384]{2,1,0:T(8,128)(2,1)S(1)}, bf16[4,256,384]{2,1,0:T(8,128)(2,1)}, u32[]{:S(2)}) copy-start(bf16[4,256,384]{2,1,0:T(8,128)(2,1)} %get-tuple-element.73) | copy-start | bytes 2359300
  238.4 19.5 %all-to-all-start.4 = ((bf16[32,32,384]{2,1,0:T(8,128)(2,1)}), bf16[32,32,384]{2,1,0:T(8,128)(2,1)S(1)}, u32[]{:S(2)}, u32[]{:S(2)}) async-start(bf16[32,32,384]{2,1,0:T(8,128)(2,1)} %bitcast.50), calls=%async_computation.4 | async-start | bytes 1572864 | tf_op jit(solution)/shard_map/all_to_all | solution.py:443
  244.0 67.4 %all-gather.2.cloned.1.call-start = ((), (), s32[]{:S(2)}) async-start(), calls=%async_computation.7 | async-start | bytes 1671168 | tf_op jit(solution)/shard_map/all_gather | solution.py:460
  (25 other events, 68.1 us)
Sparse Core Ops, SparseCore 0:
  247.1 50.3 all-gather.1

commit v2 on v1

--- a/solution.py
+++ b/solution.py
@@ -110,8 +110,8 @@
     half = (RING, ROWS // 2, part)
     shapes = [(2 + more, *half), (2 + more, *half), half, half, (RING, ROWS, part)]
     specs = [
-        pl.BlockSpec((1, *half), lambda i, place: (jnp.clip(i - before, 0, 1 + more), 0, 0, 0)),
-        pl.BlockSpec((1, *half), lambda i, place: (jnp.clip(i - before - 1, 0, 1 + more), 0, 0, 0)),
+        pl.BlockSpec((1, *half), lambda i, place: (jnp.clip(i - before, 0, 1), 0, 0, 0)),
+        pl.BlockSpec((1, *half), lambda i, place: (jnp.clip(i - before - 1, 0, 1), 0, 0, 0)),
         whole(half),
         whole(half),
         whole((RING, ROWS, part)),
@@ -165,7 +165,7 @@
 
 
 def backward_kernel(place, rows, wd, to_gate, to_up, wg, wu, *refs):
-    waiting, outs, (acc, d_gate, d_up, gate, up, sems) = refs[:8], refs[8:18], refs[18:]
+    outs, (acc, d_gate, d_up, gate, up, sems) = refs[:10], refs[10:]
     step = pl.program_id(0)
     loads = [pltpu.make_async_copy(wg, gate, sems.at[0]), pltpu.make_async_copy(wu, up, sems.at[1])]
 
@@ -205,10 +205,6 @@
         @pl.when(step == STEPS + at_step)
         def _(at_step=at_step, distance=distance):
             emit(at_step, distance, place, outs, product)
-            for h in range(2):
-                if at_step >= 2:
-                    own, got = waiting[2 * (at_step - 2) + h], waiting[4 + 2 * (at_step - 2) + h]
-                    outs[5 * h + at_step - 2][0] = (own[...].astype(F32) + got[0].astype(F32)).astype(BF16)
 
 
 def params(mib=58):
@@ -270,15 +266,13 @@
     return outs[0], outs[1], (outs[2:7], outs[7:])
 
 
-def backward(place, rows, w_gate, w_up, w_down, to_gate, to_up, parts, first):
+def backward(place, rows, w_gate, w_up, w_down, to_gate, to_up):
     hid, width = w_down.shape
     count = 2 * ROWS
     block = width // STEPS
     rows = rows.reshape(GROUPS, 2, ROWS // GROUPS, width)
     shapes, specs = emitted(width, STEPS, 1)
     anywhere = pl.BlockSpec(memory_space=pl.ANY)
-    half = parts[0][2].shape
-    waiting = [p[2] for p in parts] + [p[3] for p in parts]
     outs = pl.pallas_call(
         backward_kernel,
         out_shape=shapes,
@@ -292,9 +286,7 @@
                 whole((count, hid)),
                 anywhere,
                 anywhere,
-            ]
-            + [whole(half)] * 4
-            + [pl.BlockSpec((1, *half), lambda i, place: (0, 0, 0, 0))] * 4,
+            ],
             out_specs=specs,
             scratch_shapes=[
                 pltpu.VMEM((count, hid), F32),
@@ -308,28 +300,30 @@
         compiler_params=params(),
         cost_estimate=cost(6 * count * width * hid, 4 * width * count + 6 * width * hid),
         name="backward",
-    )(place, rows, w_down, to_gate, to_up, w_gate, w_up, *waiting, *first)
+    )(place, rows, w_down, to_gate, to_up, w_gate, w_up)
     return outs[:5], outs[5:]
 
 
 def combine_kernel(target, weights, *refs):
     homes, mixed = refs[:-1], refs[-1]
-    tokens = target.shape[0]
-    total = jnp.zeros((tokens, mixed.shape[-1]), F32)
+    tokens, part = mixed.shape[2:]
+    totals = [jnp.zeros((tokens, part), F32) for _ in range(2)]
     for h, home in enumerate(homes):
-        at = lax.broadcasted_iota(jnp.int32, (tokens, home.shape[0]), 1)
+        rows = [home[:, n].reshape(-1, part) for n in range(2)]
+        at = lax.broadcasted_iota(jnp.int32, (tokens, rows[0].shape[0]), 1)
         slot = ((at >> 5) & 7) * 64 + h * 32 + (at & 31)
         for k in range(2):
             choose = jnp.where(target[:, k : k + 1] == slot, 1.0, 0.0).astype(BF16)
-            total += weights[:, k : k + 1] * dot(choose, home[...])
-    for copy in range(mixed.shape[0]):
-        mixed[copy] = total.astype(BF16)
+            for n in range(2):
+                totals[n] += weights[:, k : k + 1] * dot(choose, rows[n])
+    for n in range(2):
+        for copy in range(mixed.shape[0]):
+            mixed[copy, n] = totals[n].astype(BF16)
 
 
 def combine(homes, target, weights, copies):
     tokens = target.shape[0]
-    part = homes[0].shape[-1]
-    shape = (copies, tokens, part)
+    shape = (copies, 2, tokens, homes[0].shape[-1])
     return pl.pallas_call(
         combine_kernel,
         out_shape=jax.ShapeDtypeStruct(shape, BF16),
@@ -337,7 +331,7 @@
         in_specs=[whole(target.shape), whole(weights.shape)] + [whole(h.shape) for h in homes],
         out_specs=whole(shape),
         compiler_params=params(),
-        cost_estimate=cost(sum(4 * tokens * h.size for h in homes), 2 * (sum(h.size for h in homes) + copies * tokens * part)),
+        cost_estimate=cost(8 * tokens * homes[0].size, 4 * homes[0].size + 4 * copies * tokens * shape[-1]),
         name="combine",
     )(target, weights, *homes)
 
@@ -346,69 +340,111 @@
     return sum(t.astype(F32) for t in terms).astype(BF16)
 
 
-def add_total(total, own, first_plus, first_minus, later_plus, later_minus):
+def later_kernel(*refs):
+    for own, got, send in zip(refs[:4], refs[4:8], refs[-4:]):
+        send[...] = add(own[...], got[0]).reshape(send.shape)
+
+
+def total_kernel(*refs):
     half = ROWS // 2
-    total[:, :half] = add(own[:, :half], later_plus, first_minus)
-    total[:, half:] = add(own[:, half:], first_plus, later_minus)
-
-
-def middle_kernel(*refs):
-    later, near, totals = refs[:8], refs[8:18], refs[22:]
-    for own, got, send in zip(later[:4], later[4:], refs[18:22]):
-        send[...] = add(own[...], got[0])
-    for h in range(2):
-        own, first_plus, first_minus, later_plus, later_minus = near[5 * h : 5 * h + 5]
-        add_total(totals[h], own[...], first_plus[0], first_minus[0], later_plus[0], later_minus[0])
-
-
-def total_kernel(after, *refs):
-    for h in range(2):
-        own, first_plus, first_minus, later_plus, later_minus = refs[5 * h : 5 * h + 5]
-        add_total(refs[10 + h], own[...], first_plus[0], first_minus[0], later_plus[...], later_minus[...])
+    for n in range(2):
+        for h in range(2):
+            own, first_plus, first_minus, later_plus, later_minus = (r[...] for r in refs[10 * n + 5 * h : 10 * n + 5 * h + 5])
+            own = own[0]
+            first_plus, first_minus, later_plus, later_minus = (
+                r.reshape(half, r.shape[-1]) for r in (first_plus, first_minus, later_plus, later_minus)
+            )
+            top = add(own[:half], later_plus, first_minus)
+            bottom = add(own[half:], first_plus, later_minus)
+            total = refs[20 + h]
+            shape = (GROUPS // 2, *total.shape[3:])
+            total[0, : GROUPS // 2, n] = top.reshape(shape)
+            total[0, GROUPS // 2 :, n] = bottom.reshape(shape)
 
 
 def both_ways(plus, minus):
     return [shift(p, axis, 1) for p, axis in zip(plus, AXES)] + [shift(m, axis, -1) for m, axis in zip(minus, AXES)]
 
 
-def ring_middle(parts, got, out_parts, out_first):
-    half, full = parts[0][2].shape, parts[0][4].shape
-    blocks = [pl.BlockSpec((1, *half), lambda i, n=n: (n, 0, 0, 0)) for n in range(3)]
-    operands = [p[2] for p in parts] + [p[3] for p in parts] + got
-    specs = [whole(half)] * 4 + [blocks[0]] * 4
+def ring_join(parts, first, plus, minus):
+    half = parts[0][2].shape
+    block = pl.BlockSpec((1, *half), lambda i: (0, 0, 0, 0))
+    third = pl.BlockSpec((1, *half), lambda i: (2, 0, 0, 0))
+    buffers = [*plus, *minus]
+    outs = pl.pallas_call(
+        later_kernel,
+        out_shape=[jax.ShapeDtypeStruct(b.shape, BF16) for b in buffers],
+        grid=(1,),
+        in_specs=[whole(half)] * 4 + [block] * 4 + [pl.BlockSpec(memory_space=pl.ANY)] * 4,
+        out_specs=[third] * 4,
+        input_output_aliases={8 + n: n for n in range(4)},
+        compiler_params=params(),
+        cost_estimate=cost(0, 24 * half[0] * half[1] * half[2]),
+        name="ring_join",
+    )(*[p[2] for p in parts], *[p[3] for p in parts], *first, *buffers)
+    return outs[:2], outs[2:]
+
+
+def ring_later(parts, first):
+    half = parts[0][2].shape
+    block = pl.BlockSpec((1, *half), lambda i: (0, 0, 0, 0))
+    outs = pl.pallas_call(
+        later_kernel,
+        out_shape=[jax.ShapeDtypeStruct(half, BF16)] * 4,
+        grid=(1,),
+        in_specs=[whole(half)] * 4 + [block] * 4,
+        out_specs=[whole(half)] * 4,
+        compiler_params=params(),
+        cost_estimate=cost(0, 24 * half[0] * half[1] * half[2]),
+        name="ring_later",
+    )(*[p[2] for p in parts], *[p[3] for p in parts], *first)
+    return outs[:2], outs[2:]
+
+
+def ring_end(out_parts, out_first, got, grad_parts, grad_later):
+    _, rows, part = out_parts[0][4].shape
+    own = pl.BlockSpec((1, rows, part), lambda j: (j, 0, 0))
+    blocks = [pl.BlockSpec((1, 1, rows // 2, part), lambda j, n=n: (n, j, 0, 0)) for n in range(3)]
+    later = pl.BlockSpec((1, rows // 2, part), lambda j: (j, 0, 0))
+    operands, specs = [], []
     for h in range(2):
         operands += [out_parts[h][4], out_first[h], out_first[2 + h], got[h], got[2 + h]]
-        specs += [whole(full), blocks[1], blocks[1], blocks[2], blocks[2]]
-    outs = pl.pallas_call(
-        middle_kernel,
-        out_shape=[jax.ShapeDtypeStruct(half, BF16)] * 4 + [jax.ShapeDtypeStruct(full, BF16)] * 2,
-        grid=(1,),
-        in_specs=specs,
-        out_specs=[whole(half)] * 4 + [whole(full)] * 2,
-        compiler_params=params(),
-        cost_estimate=cost(0, 28 * ROWS * full[0] * full[2]),
-        name="ring_middle",
-    )(*operands)
-    return outs[:4], outs[4:]
-
-
-def ring_end(parts, first, later, after):
-    half, full = parts[0][2].shape, parts[0][4].shape
-    second = pl.BlockSpec((1, *half), lambda i: (1, 0, 0, 0))
-    operands, specs = [after], [pl.BlockSpec(memory_space=pl.ANY)]
+        specs += [own, blocks[1], blocks[1], blocks[2], blocks[2]]
     for h in range(2):
-        operands += [parts[h][4], first[h], first[2 + h], later[h], later[2 + h]]
-        specs += [whole(full), second, second, whole(half), whole(half)]
+        operands += [grad_parts[h][4], got[h], got[2 + h], grad_later[h], grad_later[2 + h]]
+        specs += [own, blocks[1], blocks[1], later, later]
+    shape = (RING, GROUPS, 2, rows // GROUPS, part)
     return pl.pallas_call(
         total_kernel,
-        out_shape=[jax.ShapeDtypeStruct(full, BF16)] * 2,
-        grid=(1,),
+        out_shape=[jax.ShapeDtypeStruct(shape, BF16)] * 2,
+        grid=(RING,),
         in_specs=specs,
-        out_specs=[whole(full)] * 2,
-        compiler_params=params(),
-        cost_estimate=cost(0, 16 * ROWS * full[0] * full[2]),
+        out_specs=[pl.BlockSpec((1, *shape[1:]), lambda j: (j, 0, 0, 0, 0))] * 2,
+        compiler_params=params(),
+        cost_estimate=cost(0, 32 * RING * rows * part),
         name="ring_end",
     )(*operands)
+
+
+def assemble_kernel(slices, *results):
+    count, _, _, part = slices.shape
+    for n, result in enumerate(results):
+        for c in range(count):
+            result[:, c * part : (c + 1) * part] = slices[c, n]
+
+
+def assemble(slices):
+    count, _, tokens, part = slices.shape
+    return pl.pallas_call(
+        assemble_kernel,
+        out_shape=[jax.ShapeDtypeStruct((tokens, count * part), BF16)] * 2,
+        grid=(RING,),
+        in_specs=[pl.BlockSpec((count // RING, 2, tokens, part), lambda i: (i, 0, 0, 0))],
+        out_specs=[pl.BlockSpec((tokens, count // RING * part), lambda i: (0, i))] * 2,
+        compiler_params=params(),
+        cost_estimate=cost(0, 4 * slices.size),
+        name="assemble",
+    )(slices)
 
 
 def per_device(tokens, routes, route_weights, out_grad, w_gate, w_up, w_down):
@@ -435,32 +471,24 @@
     def quarter(h):
         return lax.dynamic_slice_in_dim(tokens, place[h] * chunk, chunk, axis=1)
 
-    def go_home(totals):
-        homes = []
-        for h in range(2):
-            total = totals[h].reshape(RING * GROUPS, half, part)
-            axes = (AXES[1 - h], *EXPERT)
-            homes.append(lax.all_to_all(total, axes, split_axis=0, concat_axis=0, tiled=True))
-        return homes
-
-    def ordered(slices):
-        return slices.transpose(1, 0, 2).reshape(count_rows, width)
-
     quarters = jnp.stack([placed(quarter(h), h).reshape(GROUPS, half, chunk) for h in range(2)], axis=1)
     got = to_experts(quarters)
     rows_g = to_experts(placed(out_grad, None))
     near, far = gathered([got[:, h].reshape(ROWS, chunk) for h in range(2)])
     to_gate, to_up, out_parts = forward(places, near, far, w_gate, w_up, w_down)
     out_first = both_ways([p[0] for p in out_parts], [p[1] for p in out_parts])
-    grad_parts = backward(places, rows_g, w_gate, w_up, w_down, to_gate, to_up, out_parts, out_first)
-    got = both_ways([p[0] for p in grad_parts], [p[1] for p in grad_parts])
-    send, out_totals = ring_middle(grad_parts, got, out_parts, out_first)
-    grad_later = both_ways(send[:2], send[2:])
-    mixed = combine([h.reshape(-1, part) for h in go_home(out_totals)], target, route_weights, 1)[0]
-    moe_out = ordered(lax.all_gather(mixed, AXES, axis=0))
-    grad_home = go_home(ring_end(grad_parts, got, grad_later, mixed))
-    copies = combine([h.reshape(-1, part) for h in grad_home], target, route_weights, RING * RING)
-    input_grad = ordered(lax.all_to_all(copies, AXES, split_axis=0, concat_axis=0, tiled=True))
+    grad_parts = backward(places, rows_g, w_gate, w_up, w_down, to_gate, to_up)
+    plus, minus = ring_join(out_parts, out_first, [p[0] for p in grad_parts], [p[1] for p in grad_parts])
+    got = both_ways(plus, minus)
+    grad_later = both_ways(*ring_later(grad_parts, got))
+    totals = ring_end(out_parts, out_first, got, grad_parts, grad_later)
+    homes = []
+    for h in range(2):
+        pieces = totals[h].reshape(RING * GROUPS, 2, half, part)
+        axes = (AXES[1 - h], *EXPERT)
+        homes.append(lax.all_to_all(pieces, axes, split_axis=0, concat_axis=0, tiled=True))
+    copies = combine(homes, target, route_weights, RING * RING)
+    moe_out, input_grad = assemble(lax.all_to_all(copies, AXES, split_axis=0, concat_axis=0, tiled=True))
     return moe_out, input_grad
 
 

time: 323 us -> 305 us (0.944)
  between operations: 14.4 us -> 0.95 us
  local copies, waits for them, and re-layouts: 14.5 us -> 9.67 us
  Pallas kernels: 68 us -> 72.8 us
  waiting for transfers between devices: 95.8 us -> 91.5 us
  starting transfers between devices: 50.2 us -> 46.8 us
    all_to_all x1, blocking collectives: 28.7 us -> 44.5 us  [per_device(): lax.all_to_all(copies, AXES, split_axis=0, concat_axis=0, tiled=True)]
    all_to_all x2 -> x1, blocking collectives: 40.2 us -> 27.5 us  [per_device(): lax.all_to_all(pieces, axes, split_axis=0, concat_axis=0, tiled=True)]
    ppermute x20, waiting for transfers between devices: 58.3 us -> 48.8 us  [shift(): lax.ppermute(rows, axis, [(i, (i + step) % RING) for i in range(RING)])]
    pallas_call x2 -> x4, Pallas kernels: 8.83 us -> 16.4 us  [the longest x1 6 us: ring_end(): pl.pallas_call(total_kernel, out_shape=[jax.ShapeDtypeStruct(shape, BF16)...]
    all_to_all x2 -> x1, starting transfers between devices: 9.55 us -> 4.11 us  [per_device(): lax.all_to_all(pieces, axes, split_axis=0, concat_axis=0, tiled=True)]
    all_to_all x2 -> x1, waiting for transfers between devices: 19.6 us -> 22.4 us  [per_device(): lax.all_to_all(pieces, axes, split_axis=0, concat_axis=0, tiled=True)]
    unnamed x68 -> x56, local copies, waits for them, and re-layouts: 10.8 us -> 8.8 us
    pallas_call x2 -> x1, Pallas kernels: 6.52 us -> 5.2 us  [combine(): pl.pallas_call(combine_kernel, out_shape=jax.ShapeDtypeStruct(shape, BF16...]
  transfers between devices with their start and end apart: 25 -> 23, of which waited for: 14 -> 10; matrix products, arithmetic and copies ran while one was open for 3% -> 2% of each run, Pallas kernels for 11% -> 17%
where the time goes in v2:
time: 305 us; the launch traced here: 304 us
  waiting for transfers between devices  91.5 us (30%)
  Pallas kernels  72.8 us (24%)
  blocking collectives  72 us (24%)
  starting transfers between devices  46.8 us (15%)
  local copies, waits for them, and re-layouts  9.67 us (3%)
  matrix products  7.26 us (2%)
    ppermute x20, waiting for transfers between devices, shift(): lax.ppermute(rows, axis, [(i, (i + step) % RING) for i in range(RING)])  48.8 us
    all_to_all x1, blocking collectives, per_device(): lax.all_to_all(copies, AXES, split_axis=0, concat_axis=0, tiled=True)  44.5 us
    ppermute x20, starting transfers between devices, shift(): lax.ppermute(rows, axis, [(i, (i + step) % RING) for i in range(RING)])  32.6 us
    all_to_all x1, blocking collectives, per_device(): lax.all_to_all(pieces, axes, split_axis=0, concat_axis=0, tiled=True)  27.5 us
    all_to_all x1, waiting for transfers between devices, per_device(): lax.all_to_all(pieces, axes, split_axis=0, concat_axis=0, tiled=True)  22.4 us
    pallas_call x1, Pallas kernels, backward(): pl.pallas_call(backward_kernel, out_shape=shapes, grid_spec=pltpu.Prefetc...  21.4 us
    all_to_all x2, waiting for transfers between devices, to_experts(): return lax.all_to_all(rows, EXPERT, split_axis=0, concat_axis=0, tiled=True)  20.3 us
    pallas_call x1, Pallas kernels, forward(): pl.pallas_call(forward_far_kernel, out_shape=[jax.ShapeDtypeStruct((2 * R...  13.9 us
  transfers between devices with their start and end apart: 23, of which 10 were waited for; matrix products, arithmetic and copies ran while one was open for 2% of the time, Pallas kernels for 17%

profile of v2, /device:TPU:0, one launch (start us, length us, event | category | flops | bytes accessed | tf_op | source)
XLA Modules:
  0.0 303.8 jit_solution(10075746626146915821)
XLA Ops:
  7.3 5.4 %all-to-all-start = ((bf16[8,2,32,1536]{3,2,1,0:T(8,128)(2,1)}), bf16[8,2,32,1536]{3,2,1,0:T(8,128)(2,1)S(1)}, u32[]{:S(2)}, u32[]{:S(2)}) async-start(bf16[8,2,32,1536]{3,2,1,0:T(8,128)(2,1)} %pad_maximum_fusion), calls=%async_computation | async-start | bytes 3145728 | tf_op jit(solution)/shard_map/all_to_all | solution.py:469
  12.7 4.5 %convolution_convert_fusion = bf16[512,6144]{1,0:T(8,128)(2,1)} fusion(bf16[128,6144]{1,0:T(8,128)(2,1)S(1)} %copy-done, s32[128]{0:T(128)S(1)} %get-tuple-element.79, s32[128]{0:T(128)S(1)} %get-tuple-element.78), kind=kOutput, calls=%fused_computation | convolution fusion | flops 808648704 | bytes 7865344 | tf_op jit(solution)/shard_map/dot_general | solution.py:24
  17.2 17.1 %all-to-all-done = bf16[8,2,32,1536]{3,2,1,0:T(8,128)(2,1)S(1)} async-done(((bf16[8,2,32,1536]{3,2,1,0:T(8,128)(2,1)}), bf16[8,2,32,1536]{3,2,1,0:T(8,128)(2,1)S(1)}, u32[]{:S(2)}, u32[]{:S(2)}) %all-to-all-start) | async-done | bytes 1572896 | tf_op jit(solution)/shard_map/all_to_all | solution.py:469
  34.3 4.8 %all-to-all-start.1 = ((bf16[8,64,6144]{2,1,0:T(8,128)(2,1)}), bf16[8,64,6144]{2,1,0:T(8,128)(2,1)}, u32[]{:S(2)}, u32[]{:S(2)}) async-start(bf16[8,64,6144]{2,1,0:T(8,128)(2,1)} %bitcast.18), calls=%async_computation.1 | async-start | bytes 12582912 | tf_op jit(solution)/shard_map/all_to_all | solution.py:469
  42.4 1.7 collective-permute-start.2
  44.1 1.7 collective-permute-start.3
  46.4 13.9 %collective-permute-done.refs_0_.refs_2_ = bf16[256,1536]{1,0:T(8,128)(2,1)S(1)} collective-permute-done((bf16[256,1536]{1,0:T(8,128)(2,1)S(1)}, bf16[256,1536]{1,0:T(8,128)(2,1)S(1)}, u32[]{:S(2)}, u32[]{:S(2)}) %collective-permute-start) | collective-permute-done | bytes 786464 | tf_op jit(solution)/shard_map/ppermute | solution.py:20
  64.0 2.6 halves.1
  67.8 2.1 collective-permute-start.5
  71.5 1.7 collective-permute-start.7
  73.1 13.3 %forward_near.1 = (f32[512,512]{1,0:T(8,128)}, f32[512,512]{1,0:T(8,128)}) custom-call(s32[2]{0:T(128)} %pad_add_fusion.place, bf16[256,1536]{1,0:T(8,128)(2,1)} %bitcast.35, bf16[256,1536]{1,0:T(8,128)(2,1)} %copy-done.16, bf16[256,1536]{1,0:T(8,128)(2,1)} %copy-done.14, bf16[256,1536]{1,0:T(8,128)(2,1)} %bitcast.32, bf16[256,1536]{1,0:T(8,128)(2,1)} %copy-done.17, ...), custom_call_target="tpu_custom_call" | custom-call | flops 4831838208 | bytes 23592960 | tf_op jit(solution)/shard_map/forward_near/pallas_call | solution.py:230
  87.6 13.9 %forward_far.1 = (f32[512,512]{1,0:T(8,128)}, f32[512,512]{1,0:T(8,128)}, bf16[2,4,128,384]{3,2,1,0:T(8,128)(2,1)}, bf16[2,4,128,384]{3,2,1,0:T(8,128)(2,1)}, bf...) custom-call(s32[2]{0:T(128)} %pad_add_fusion.place, ...), custom_call_target="tpu_custom_call" | custom-call | flops 4831838208 | bytes 17825792 | tf_op jit(solution)/shard_map/forward_far/pallas_call | solution.py:247
  102.4 2.4 collective-permute-start.11
  105.1 2.9 collective-permute-start.9
  108.0 3.2 %all-to-all-done.1 = bf16[8,64,6144]{2,1,0:T(8,128)(2,1)} async-done(((bf16[8,64,6144]{2,1,0:T(8,128)(2,1)}), bf16[8,64,6144]{2,1,0:T(8,128)(2,1)}, u32[]{:S(2)}, u32[]{:S(2)}) %all-to-all-start.1) | async-done | bytes 6291488 | tf_op jit(solution)/shard_map/all_to_all | solution.py:469
  111.2 21.4 %backward.1 = (bf16[3,4,128,384]{3,2,1,0:T(8,128)(2,1)}, bf16[3,4,128,384]{3,2,1,0:T(8,128)(2,1)}, bf16[4,128,384]{2,1,0:T(8,128)(2,1)}, bf16[4,128,384]{2,1,0:T...) custom-call(s32[2]{0:T(128)} %pad_add_fusion.place, ...), custom_call_target="tpu_custom_call" | custom-call | flops 9663676416 | bytes 31457280 | tf_op jit(solution)/shard_map/backward/pallas_call | solution.py:276
  134.3 3.1 %ring_join.1 = (bf16[3,4,128,384]{3,2,1,0:T(8,128)(2,1)}, bf16[3,4,128,384]{3,2,1,0:T(8,128)(2,1)}, bf16[3,4,128,384]{3,2,1,0:T(8,128)(2,1)}, bf16[3,4,128,384]{3,2,1,0:T(8,128)(2,1)}) custom-call(bf16[4,128,384]{2,1,0:T(8,128)(2,1)} %get-tuple-element.49.refs_0_, ...), custom_call_target="tpu_custom_call", output_to_operand_aliasing={{0}: (8, {}), {1}: (9, {}), {2}: (10, {}), {3}: (11, {})} | custom-call | bytes 4718592 | tf_op jit(solution)/shard_map/ring_join/pallas_call | solution.py:374
  138.9 1.7 collective-permute-start.13
  143.9 22.5 %collective-permute-done.12.refs_4_.refs_3_.refs_11_ = bf16[3,4,128,384]{3,2,1,0:T(8,128)(2,1)S(1)} collective-permute-done((bf16[3,4,128,384]{3,2,1,0:T(8,128)(2,1)}, bf16[3,4,128,384]{3,2,1,0:T(8,128)(2,1)S(1)}, u32[]{:S(2)}, u32[]{:S(2)}) %collective-permute-start.12) | collective-permute-done | bytes 1179680 | tf_op jit(solution)/shard_map/ppermute | solution.py:20
  166.4 2.7 collective-permute-done.14.refs_5_.refs_8_.refs_16_
  170.5 3.1 %ring_later.1 = (bf16[4,128,384]{2,1,0:T(8,128)(2,1)}, bf16[4,128,384]{2,1,0:T(8,128)(2,1)}, bf16[4,128,384]{2,1,0:T(8,128)(2,1)}, bf16[4,128,384]{2,1,0:T(8,128)(2,1)}) custom-call(bf16[4,128,384]{2,1,0:T(8,128)(2,1)} %get-tuple-element.67.refs_0_, bf16[4,128,384]{2,1,0:T(8,128)(2,1)} %get-tuple-element.68.refs_1_, ...), custom_call_target="tpu_custom_call" | custom-call | bytes 4718592 | tf_op jit(solution)/shard_map/ring_later/pallas_call | solution.py:391
  173.9 3.0 collective-permute-start.17
  178.1 2.0 collective-permute-start.19
  180.1 4.2 %collective-permute-done.16.refs_13_ = bf16[4,128,384]{2,1,0:T(8,128)(2,1)S(1)} collective-permute-done((bf16[4,128,384]{2,1,0:T(8,128)(2,1)}, bf16[4,128,384]{2,1,0:T(8,128)(2,1)S(1)}, u32[]{:S(2)}, u32[]{:S(2)}) %collective-permute-start.16) | collective-permute-done | bytes 393248 | tf_op jit(solution)/shard_map/ppermute | solution.py:20
  184.3 2.7 collective-permute-done.18.refs_18_
  188.0 6.0 %ring_end.1 = (bf16[4,8,2,32,384]{4,3,2,1,0:T(8,128)(2,1)}, bf16[4,8,2,32,384]{4,3,2,1,0:T(8,128)(2,1)}) custom-call(bf16[4,256,384]{2,1,0:T(8,128)(2,1)} %get-tuple-element.46.refs_0_, bf16[2,4,128,384]{3,2,1,0:T(8,128)(2,1)} %copy-done.9, bf16[2,4,128,384]{3,2,1,0:T(8,128)(2,1)} %copy-done.10, bf16[3,4,128,384]{3,2,1,0:T(8,128)(2,1)} %copy-done.2, ...), custom_call_target="tpu_custom_call" | custom-call | bytes 12582912 | tf_op jit(solution)/shard_map/ring_end/pallas_call | solution.py:417
  194.0 27.5 %all_to_all.29.refs_0_ = bf16[32,2,32,384]{3,2,1,0:T(8,128)(2,1)} all-to-all(bf16[32,2,32,384]{3,2,1,0:T(8,128)(2,1)} %bitcast.29), channel_id=1, replica_groups=mesh['z'=4,'core'=2,'y'=4,'x'=4] {'y','z','core'}, dimensions={0} | all-to-all | bytes 3145728 | tf_op jit(solution)/shard_map/all_to_all | solution.py:489
  221.5 4.1 %all-to-all-start.3 = ((bf16[32,2,32,384]{3,2,1,0:T(8,128)(2,1)}), bf16[32,2,32,384]{3,2,1,0:T(8,128)(2,1)S(1)}, u32[]{:S(2)}, u32[]{:S(2)}) async-start(bf16[32,2,32,384]{3,2,1,0:T(8,128)(2,1)} %bitcast.14), calls=%async_computation.3 | async-start | bytes 3145728 | tf_op jit(solution)/shard_map/all_to_all | solution.py:489
  226.4 22.4 %all-to-all-done.3.refs_1_ = bf16[32,2,32,384]{3,2,1,0:T(8,128)(2,1)S(1)} async-done(((bf16[32,2,32,384]{3,2,1,0:T(8,128)(2,1)}), bf16[32,2,32,384]{3,2,1,0:T(8,128)(2,1)S(1)}, u32[]{:S(2)}, u32[]{:S(2)}) %all-to-all-start.3) | async-done | bytes 1572896 | tf_op jit(solution)/shard_map/all_to_all | solution.py:489
  249.9 5.2 %combine.1 = bf16[16,2,128,384]{3,2,1,0:T(8,128)(2,1)} custom-call(s32[128,2]{1,0:T(8,128)} %copy-done.11, f32[128,2]{1,0:T(8,128)} %copy.36.weights, bf16[32,2,32,384]{3,2,1,0:T(8,128)(2,1)} %all_to_all.29.refs_0_, bf16[32,2,32,384]{3,2,1,0:T(8,128)(2,1)} %copy-done.6), custom_call_target="tpu_custom_call" | custom-call | flops 805306368 | bytes 6291456 | tf_op jit(solution)/shard_map/combine/pallas_call | solution.py:327
  255.1 44.5 %all_to_all.30.slices = bf16[16,2,128,384]{3,2,1,0:T(8,128)(2,1)} all-to-all(bf16[16,2,128,384]{3,2,1,0:T(8,128)(2,1)} %combine.1), channel_id=1, replica_groups=mesh['z'=4,'core'=2,'y'=4,'x'=4] {'x','y'}, dimensions={0} | all-to-all | bytes 6291456 | tf_op jit(solution)/shard_map/all_to_all | solution.py:491
  299.6 4.2 %assemble.1 = (bf16[128,6144]{1,0:T(8,128)(2,1)}, bf16[128,6144]{1,0:T(8,128)(2,1)}) custom-call(bf16[16,2,128,384]{3,2,1,0:T(8,128)(2,1)} %all_to_all.30.slices), custom_call_target="tpu_custom_call" | custom-call | bytes 6291456 | tf_op jit(solution)/shard_map/assemble/pallas_call | solution.py:438
  (98 shorter events, 31.4 us)
Async XLA Ops:
  0.6 12.1 %copy-start = (bf16[128,6144]{1,0:T(8,128)(2,1)S(1)}, bf16[128,6144]{1,0:T(8,128)(2,1)}, u32[]{:S(2)}) copy-start(bf16[128,6144]{1,0:T(8,128)(2,1)} %param.10) | copy-start | bytes 4718596
  2.8 4.5 %copy-start.11 = (s32[128,2]{1,0:T(8,128)}, s32[128,2]{1,0:T(8,128)S(1)}, u32[]{:S(2)}) copy-start(s32[128,2]{1,0:T(8,128)S(1)} %add.12.target) | copy-start | bytes 3076
  7.3 27.0 %all-to-all-start = ((bf16[8,2,32,1536]{3,2,1,0:T(8,128)(2,1)}), bf16[8,2,32,1536]{3,2,1,0:T(8,128)(2,1)S(1)}, u32[]{:S(2)}, u32[]{:S(2)}) async-start(bf16[8,2,32,1536]{3,2,1,0:T(8,128)(2,1)} %pad_maximum_fusion), calls=%async_computation | async-start | bytes 3145728 | tf_op jit(solution)/shard_map/all_to_all | solution.py:469
  34.3 76.9 %all-to-all-start.1 = ((bf16[8,64,6144]{2,1,0:T(8,128)(2,1)}), bf16[8,64,6144]{2,1,0:T(8,128)(2,1)}, u32[]{:S(2)}, u32[]{:S(2)}) async-start(bf16[8,64,6144]{2,1,0:T(8,128)(2,1)} %bitcast.18), calls=%async_computation.1 | async-start | bytes 12582912 | tf_op jit(solution)/shard_map/all_to_all | solution.py:469
  39.2 27.4 %copy-start.12 = (bf16[8,1,32,1536]{3,2,1,0:T(8,128)(2,1)}, bf16[8,1,32,1536]{3,2,1,0:T(8,128)(2,1)S(1)}, u32[]{:S(2)}) copy-start(bf16[8,1,32,1536]{3,2,1,0:T(8,128)(2,1)S(1)} %get-tuple-element.82) | copy-start | bytes 2359300
  39.2 27.4 %copy-start.13 = (bf16[8,1,32,1536]{3,2,1,0:T(8,128)(2,1)}, bf16[8,1,32,1536]{3,2,1,0:T(8,128)(2,1)S(1)}, u32[]{:S(2)}) copy-start(bf16[8,1,32,1536]{3,2,1,0:T(8,128)(2,1)S(1)} %get-tuple-element.83) | copy-start | bytes 2359300
  39.2 21.1 %collective-permute-start = (bf16[256,1536]{1,0:T(8,128)(2,1)S(1)}, bf16[256,1536]{1,0:T(8,128)(2,1)S(1)}, u32[]{:S(2)}, u32[]{:S(2)}) collective-permute-start(bf16[256,1536]{1,0:T(8,128)(2,1)S(1)} %bitcast.33), channel_id=1, source_target_pairs={{0,1},{1,2},{2,3},{3,0},{4,5},{5,6},{6,7},{7,4},{8,9},{9,10},{10,1... | collective-permute-start | bytes 2359304 | tf_op jit(solution)/shard_map/ppermute | solution.py:20
  40.8 20.8 %collective-permute-start.1 = (bf16[256,1536]{1,0:T(8,128)(2,1)S(1)}, bf16[256,1536]{1,0:T(8,128)(2,1)S(1)}, u32[]{:S(2)}, u32[]{:S(2)}) collective-permute-start(bf16[256,1536]{1,0:T(8,128)(2,1)S(1)} %bitcast.30), channel_id=1, source_target_pairs={{0,4},{4,8},{8,12},{12,0},{1,5},{5,9},{9,13},{13,1},{2,6},{6,10},{... | collective-permute-start | bytes 2359304 | tf_op jit(solution)/shard_map/ppermute | solution.py:20
  42.4 19.2 %collective-permute-start.2 = (bf16[256,1536]{1,0:T(8,128)(2,1)S(1)}, bf16[256,1536]{1,0:T(8,128)(2,1)S(1)}, u32[]{:S(2)}, u32[]{:S(2)}) collective-permute-start(bf16[256,1536]{1,0:T(8,128)(2,1)S(1)} %bitcast.34), channel_id=1, source_target_pairs={{0,3},{1,0},{2,1},{3,2},{4,7},{5,4},{6,5},{7,6},{8,11},{9,8},{10,9... | collective-permute-start | bytes 2359304 | tf_op jit(solution)/shard_map/ppermute | solution.py:20
  44.1 19.0 %collective-permute-start.3 = (bf16[256,1536]{1,0:T(8,128)(2,1)S(1)}, bf16[256,1536]{1,0:T(8,128)(2,1)S(1)}, u32[]{:S(2)}, u32[]{:S(2)}) collective-permute-start(bf16[256,1536]{1,0:T(8,128)(2,1)S(1)} %bitcast.31), channel_id=1, source_target_pairs={{0,12},{4,0},{8,4},{12,8},{1,13},{5,1},{9,5},{13,9},{2,14},{6,2},{... | collective-permute-start | bytes 2359304 | tf_op jit(solution)/shard_map/ppermute | solution.py:20
  60.3 2.8 copy-start.14
  66.6 19.8 %collective-permute-start.4 = (bf16[128,1536]{1,0:T(8,128)(2,1)}, bf16[128,1536]{1,0:T(8,128)(2,1)S(1)}, u32[]{:S(2)}, u32[]{:S(2)}) collective-permute-start(bf16[128,1536]{1,0:T(8,128)(2,1)} %get-tuple-element.40), channel_id=1, source_target_pairs={{0,1},{1,2},{2,3},{3,0},{4,5},{5,6},{6,7},{7,4},{8,9},{9,10},{10,1... | collective-permute-start | bytes 1179656 | tf_op jit(solution)/shard_map/ppermute | solution.py:20
  67.8 18.6 %collective-permute-start.5 = (bf16[128,1536]{1,0:T(8,128)(2,1)}, bf16[128,1536]{1,0:T(8,128)(2,1)S(1)}, u32[]{:S(2)}, u32[]{:S(2)}) collective-permute-start(bf16[128,1536]{1,0:T(8,128)(2,1)} %get-tuple-element.41), channel_id=1, source_target_pairs={{0,3},{1,0},{2,1},{3,2},{4,7},{5,4},{6,5},{7,6},{8,11},{9,8},{10,9... | collective-permute-start | bytes 1179656 | tf_op jit(solution)/shard_map/ppermute | solution.py:20
  69.9 16.6 %collective-permute-start.6 = (bf16[128,1536]{1,0:T(8,128)(2,1)}, bf16[128,1536]{1,0:T(8,128)(2,1)S(1)}, u32[]{:S(2)}, u32[]{:S(2)}) collective-permute-start(bf16[128,1536]{1,0:T(8,128)(2,1)} %get-tuple-element.42), channel_id=1, source_target_pairs={{0,4},{4,8},{8,12},{12,0},{1,5},{5,9},{9,13},{13,1},{2,6},{6,10},{... | collective-permute-start | bytes 1179656 | tf_op jit(solution)/shard_map/ppermute | solution.py:20
  71.5 15.0 %collective-permute-start.7 = (bf16[128,1536]{1,0:T(8,128)(2,1)}, bf16[128,1536]{1,0:T(8,128)(2,1)S(1)}, u32[]{:S(2)}, u32[]{:S(2)}) collective-permute-start(bf16[128,1536]{1,0:T(8,128)(2,1)} %get-tuple-element.43), channel_id=1, source_target_pairs={{0,12},{4,0},{8,4},{12,8},{1,13},{5,1},{9,5},{13,9},{2,14},{6,2},{... | collective-permute-start | bytes 1179656 | tf_op jit(solution)/shard_map/ppermute | solution.py:20
  101.5 31.2 %collective-permute-start.10 = (bf16[2,4,128,384]{3,2,1,0:T(8,128)(2,1)}, bf16[2,4,128,384]{3,2,1,0:T(8,128)(2,1)S(1)}, u32[]{:S(2)}, u32[]{:S(2)}) collective-permute-start(bf16[2,4,128,384]{3,2,1,0:T(8,128)(2,1)} %get-tuple-element.53), channel_id=1, source_target_pairs={{0,4},{4,8},{8,12},{12,0},{1,5},{5,9},{9,13},{13,1},{2,6},{6,10},{... | collective-permute-start | bytes 2359304 | tf_op jit(solution)/shard_map/ppermute | solution.py:20
  102.4 30.3 %collective-permute-start.11 = (bf16[2,4,128,384]{3,2,1,0:T(8,128)(2,1)}, bf16[2,4,128,384]{3,2,1,0:T(8,128)(2,1)S(1)}, u32[]{:S(2)}, u32[]{:S(2)}) collective-permute-start(bf16[2,4,128,384]{3,2,1,0:T(8,128)(2,1)} %get-tuple-element.54), channel_id=1, source_target_pairs={{0,12},{4,0},{8,4},{12,8},{1,13},{5,1},{9,5},{13,9},{2,14},{6,2},{... | collective-permute-start | bytes 2359304 | tf_op jit(solution)/shard_map/ppermute | solution.py:20
  104.8 27.9 %collective-permute-start.8 = (bf16[2,4,128,384]{3,2,1,0:T(8,128)(2,1)}, bf16[2,4,128,384]{3,2,1,0:T(8,128)(2,1)S(1)}, u32[]{:S(2)}, u32[]{:S(2)}) collective-permute-start(bf16[2,4,128,384]{3,2,1,0:T(8,128)(2,1)} %get-tuple-element.47), channel_id=1, source_target_pairs={{0,1},{1,2},{2,3},{3,0},{4,5},{5,6},{6,7},{7,4},{8,9},{9,10},{10,1... | collective-permute-start | bytes 2359304 | tf_op jit(solution)/shard_map/ppermute | solution.py:20
  105.1 27.6 %collective-permute-start.9 = (bf16[2,4,128,384]{3,2,1,0:T(8,128)(2,1)}, bf16[2,4,128,384]{3,2,1,0:T(8,128)(2,1)S(1)}, u32[]{:S(2)}, u32[]{:S(2)}) collective-permute-start(bf16[2,4,128,384]{3,2,1,0:T(8,128)(2,1)} %get-tuple-element.48), channel_id=1, source_target_pairs={{0,3},{1,0},{2,1},{3,2},{4,7},{5,4},{6,5},{7,6},{8,11},{9,8},{10,9... | collective-permute-start | bytes 2359304 | tf_op jit(solution)/shard_map/ppermute | solution.py:20
  137.4 28.9 %collective-permute-start.12 = (bf16[3,4,128,384]{3,2,1,0:T(8,128)(2,1)}, bf16[3,4,128,384]{3,2,1,0:T(8,128)(2,1)S(1)}, u32[]{:S(2)}, u32[]{:S(2)}) collective-permute-start(bf16[3,4,128,384]{3,2,1,0:T(8,128)(2,1)} %get-tuple-element.61), channel_id=1, source_target_pairs={{0,1},{1,2},{2,3},{3,0},{4,5},{5,6},{6,7},{7,4},{8,9},{9,10},{10,1... | collective-permute-start | bytes 3538952 | tf_op jit(solution)/shard_map/ppermute | solution.py:20
  138.9 27.4 %collective-permute-start.13 = (bf16[3,4,128,384]{3,2,1,0:T(8,128)(2,1)}, bf16[3,4,128,384]{3,2,1,0:T(8,128)(2,1)S(1)}, u32[]{:S(2)}, u32[]{:S(2)}) collective-permute-start(bf16[3,4,128,384]{3,2,1,0:T(8,128)(2,1)} %get-tuple-element.62), channel_id=1, source_target_pairs={{0,3},{1,0},{2,1},{3,2},{4,7},{5,4},{6,5},{7,6},{8,11},{9,8},{10,9... | collective-permute-start | bytes 3538952 | tf_op jit(solution)/shard_map/ppermute | solution.py:20
  140.7 28.4 %collective-permute-start.14 = (bf16[3,4,128,384]{3,2,1,0:T(8,128)(2,1)}, bf16[3,4,128,384]{3,2,1,0:T(8,128)(2,1)S(1)}, u32[]{:S(2)}, u32[]{:S(2)}) collective-permute-start(bf16[3,4,128,384]{3,2,1,0:T(8,128)(2,1)} %get-tuple-element.64), channel_id=1, source_target_pairs={{0,4},{4,8},{8,12},{12,0},{1,5},{5,9},{9,13},{13,1},{2,6},{6,10},{... | collective-permute-start | bytes 3538952 | tf_op jit(solution)/shard_map/ppermute | solution.py:20
  142.2 26.9 %collective-permute-start.15 = (bf16[3,4,128,384]{3,2,1,0:T(8,128)(2,1)}, bf16[3,4,128,384]{3,2,1,0:T(8,128)(2,1)S(1)}, u32[]{:S(2)}, u32[]{:S(2)}) collective-permute-start(bf16[3,4,128,384]{3,2,1,0:T(8,128)(2,1)} %get-tuple-element.65), channel_id=1, source_target_pairs={{0,12},{4,0},{8,4},{12,8},{1,13},{5,1},{9,5},{13,9},{2,14},{6,2},{... | collective-permute-start | bytes 3538952 | tf_op jit(solution)/shard_map/ppermute | solution.py:20
  166.4 2.8 copy-start.2
  166.4 2.8 copy-start.3
  173.7 10.7 %collective-permute-start.16 = (bf16[4,128,384]{2,1,0:T(8,128)(2,1)}, bf16[4,128,384]{2,1,0:T(8,128)(2,1)S(1)}, u32[]{:S(2)}, u32[]{:S(2)}) collective-permute-start(bf16[4,128,384]{2,1,0:T(8,128)(2,1)} %get-tuple-element.71), channel_id=1, source_target_pairs={{0,1},{1,2},{2,3},{3,0},{4,5},{5,6},{6,7},{7,4},{8,9},{9,10},{10,1... | collective-permute-start | bytes 1179656 | tf_op jit(solution)/shard_map/ppermute | solution.py:20
  173.9 10.4 %collective-permute-start.17 = (bf16[4,128,384]{2,1,0:T(8,128)(2,1)}, bf16[4,128,384]{2,1,0:T(8,128)(2,1)S(1)}, u32[]{:S(2)}, u32[]{:S(2)}) collective-permute-start(bf16[4,128,384]{2,1,0:T(8,128)(2,1)} %get-tuple-element.72), channel_id=1, source_target_pairs={{0,3},{1,0},{2,1},{3,2},{4,7},{5,4},{6,5},{7,6},{8,11},{9,8},{10,9... | collective-permute-start | bytes 1179656 | tf_op jit(solution)/shard_map/ppermute | solution.py:20
  176.9 10.1 %collective-permute-start.18 = (bf16[4,128,384]{2,1,0:T(8,128)(2,1)}, bf16[4,128,384]{2,1,0:T(8,128)(2,1)S(1)}, u32[]{:S(2)}, u32[]{:S(2)}) collective-permute-start(bf16[4,128,384]{2,1,0:T(8,128)(2,1)} %get-tuple-element.74), channel_id=1, source_target_pairs={{0,4},{4,8},{8,12},{12,0},{1,5},{5,9},{9,13},{13,1},{2,6},{6,10},{... | collective-permute-start | bytes 1179656 | tf_op jit(solution)/shard_map/ppermute | solution.py:20
  178.1 8.9 %collective-permute-start.19 = (bf16[4,128,384]{2,1,0:T(8,128)(2,1)}, bf16[4,128,384]{2,1,0:T(8,128)(2,1)S(1)}, u32[]{:S(2)}, u32[]{:S(2)}) collective-permute-start(bf16[4,128,384]{2,1,0:T(8,128)(2,1)} %get-tuple-element.75), channel_id=1, source_target_pairs={{0,12},{4,0},{8,4},{12,8},{1,13},{5,1},{9,5},{13,9},{2,14},{6,2},{... | collective-permute-start | bytes 1179656 | tf_op jit(solution)/shard_map/ppermute | solution.py:20
  221.5 4.1 %copy-start.26 = (f32[128,2]{0,1:T(2,128)S(1)}, f32[128,2]{0,1:T(2,128)}, u32[]{:S(2)}) copy-start(f32[128,2]{0,1:T(2,128)} %param.9) | copy-start | bytes 3076
  221.5 27.2 %all-to-all-start.3 = ((bf16[32,2,32,384]{3,2,1,0:T(8,128)(2,1)}), bf16[32,2,32,384]{3,2,1,0:T(8,128)(2,1)S(1)}, u32[]{:S(2)}, u32[]{:S(2)}) async-start(bf16[32,2,32,384]{3,2,1,0:T(8,128)(2,1)} %bitcast.14), calls=%async_computation.3 | async-start | bytes 3145728 | tf_op jit(solution)/shard_map/all_to_all | solution.py:489
  255.1 48.7 %copy-start.1 = (bf16[128,6144]{1,0:T(8,128)(2,1)S(1)}, bf16[128,6144]{1,0:T(8,128)(2,1)}, u32[]{:S(2)}) copy-start(bf16[128,6144]{1,0:T(8,128)(2,1)} %param.10) | copy-start | bytes 4718596
  (18 other events, 23.4 us)

commit v3 on v2

--- a/solution.py
+++ b/solution.py
@@ -28,16 +28,60 @@
     return lax.dot_general(a, b, (((1,), (1,)), ((), ())), preferred_element_type=F32)
 
 
-def slots_of(routes, per_expert):
-    flat = routes.reshape(-1)
-    order = jnp.arange(flat.shape[0], dtype=jnp.int32)
-    earlier = (flat[:, None] == flat[None, :]) & (order[:, None] > order[None, :])
-    before = jnp.sum(earlier.astype(jnp.int32), axis=1)
-    return (flat * per_expert + before).reshape(routes.shape)
-
-
 def whole(shape):
     return pl.BlockSpec(shape, lambda *_: (0,) * len(shape))
+
+
+def params(mib=58):
+    return pltpu.CompilerParams(vmem_limit_bytes=mib * MIB)
+
+
+def cost(flops, moved):
+    return pl.CostEstimate(flops=int(flops), bytes_accessed=int(moved), transcendentals=0)
+
+
+def slot_at(at, h):
+    return (at >> 5) * 64 + h * 32 + (at & 31)
+
+
+def dispatch_kernel(place, routes, *refs):
+    columns, (placed, target) = refs[:2], refs[2:]
+    tokens = routes.shape[0]
+    row, lane = (lax.broadcasted_iota(jnp.int32, (tokens, tokens), d) for d in range(2))
+    picks = [jnp.where(routes[:, k : k + 1] == lane, 1.0, 0.0) for k in range(2)]
+    earlier = jnp.where(row > lane, 1.0, 0.0).astype(BF16)
+    before = dot(earlier, (picks[0] + picks[1]).astype(BF16))
+    targets = []
+    for k in range(2):
+        count = jnp.sum(picks[k] * before, axis=1, keepdims=True).astype(jnp.int32)
+        targets.append(routes[:, k : k + 1] * (2 * ROWS // GROUPS) + count)
+        target[:, k : k + 1] = targets[k]
+    slot_lane = lax.broadcasted_iota(jnp.int32, (tokens, ROWS), 1)
+    for h in range(2):
+        slot = slot_at(slot_lane, h)
+        chosen = jnp.where((targets[0] == slot) | (targets[1] == slot), 1.0, 0.0)
+        rows = dot(chosen.T.astype(BF16), columns[h][...]).astype(BF16)
+        placed[:, h] = rows.reshape(placed.shape[0], placed.shape[2], placed.shape[3])
+
+
+def dispatch(place, routes, rows):
+    tokens, width = rows.shape
+    chunk = width // RING
+    shape = (GROUPS, 2, ROWS // GROUPS, chunk)
+    return pl.pallas_call(
+        dispatch_kernel,
+        out_shape=[jax.ShapeDtypeStruct(shape, BF16), jax.ShapeDtypeStruct(routes.shape, jnp.int32)],
+        grid_spec=pltpu.PrefetchScalarGridSpec(
+            num_scalar_prefetch=1,
+            grid=(1,),
+            in_specs=[whole(routes.shape)]
+            + [pl.BlockSpec((tokens, chunk), lambda i, place, h=h: (0, place[h])) for h in range(2)],
+            out_specs=[whole(shape), whole(routes.shape)],
+        ),
+        compiler_params=params(16),
+        cost_estimate=cost(8 * ROWS * tokens * chunk, 8 * tokens * chunk + 4 * ROWS * chunk),
+        name="dispatch",
+    )(place, routes, rows, rows)
 
 
 def halves_kernel(*refs):
@@ -165,9 +209,10 @@
 
 
 def backward_kernel(place, rows, wd, to_gate, to_up, wg, wu, *refs):
-    outs, (acc, d_gate, d_up, gate, up, sems) = refs[:10], refs[10:]
+    outs, (acc, d_both, both, sems) = refs[:10], refs[10:]
+    hid = wd.shape[0]
     step = pl.program_id(0)
-    loads = [pltpu.make_async_copy(wg, gate, sems.at[0]), pltpu.make_async_copy(wu, up, sems.at[1])]
+    loads = [pltpu.make_async_copy(w, both.at[:, pl.ds(n * hid, hid)], sems.at[n]) for n, w in enumerate((wg, wu))]
 
     @pl.when(step == 0)
     def _():
@@ -188,31 +233,22 @@
 
     @pl.when(step == STEPS - 1)
     def _():
-        d_gate[...] = (acc[...] * to_gate[...]).astype(BF16)
-        d_up[...] = (acc[...] * to_up[...]).astype(BF16)
+        d_both[:, :hid] = (acc[...] * to_gate[...]).astype(BF16)
+        d_both[:, hid:] = (acc[...] * to_up[...]).astype(BF16)
         for load in loads:
             load.wait()
 
     part = outs[4].shape[-1]
 
     def product(h, columns):
-        mine = slice(h * ROWS, (h + 1) * ROWS)
-        gates, ups = (jnp.concatenate([w[pl.ds(at, part)] for at in columns], axis=0) for w in (gate, up))
-        return dot_t(d_gate[mine], gates) + dot_t(d_up[mine], ups)
+        weights = jnp.concatenate([both[pl.ds(at, part)] for at in columns], axis=0)
+        return dot_t(d_both[h * ROWS : (h + 1) * ROWS], weights)
 
     for at_step, distance in enumerate(DISTANCES):
 
         @pl.when(step == STEPS + at_step)
         def _(at_step=at_step, distance=distance):
             emit(at_step, distance, place, outs, product)
-
-
-def params(mib=58):
-    return pltpu.CompilerParams(vmem_limit_bytes=mib * MIB)
-
-
-def cost(flops, moved):
-    return pl.CostEstimate(flops=int(flops), bytes_accessed=int(moved), transcendentals=0)
 
 
 def forward(place, near, far, w_gate, w_up, w_down):
@@ -290,10 +326,8 @@
             out_specs=specs,
             scratch_shapes=[
                 pltpu.VMEM((count, hid), F32),
-                pltpu.VMEM((count, hid), BF16),
-                pltpu.VMEM((count, hid), BF16),
-                pltpu.VMEM((width, hid), BF16),
-                pltpu.VMEM((width, hid), BF16),
+                pltpu.VMEM((count, 2 * hid), BF16),
+                pltpu.VMEM((width, 2 * hid), BF16),
                 pltpu.SemaphoreType.DMA((2,)),
             ],
         ),
@@ -307,31 +341,29 @@
 def combine_kernel(target, weights, *refs):
     homes, mixed = refs[:-1], refs[-1]
     tokens, part = mixed.shape[2:]
-    totals = [jnp.zeros((tokens, part), F32) for _ in range(2)]
+    total = jnp.zeros((tokens, part), F32)
     for h, home in enumerate(homes):
-        rows = [home[:, n].reshape(-1, part) for n in range(2)]
-        at = lax.broadcasted_iota(jnp.int32, (tokens, rows[0].shape[0]), 1)
-        slot = ((at >> 5) & 7) * 64 + h * 32 + (at & 31)
+        rows = home[:, 0].reshape(-1, part)
+        slot = slot_at(lax.broadcasted_iota(jnp.int32, (tokens, rows.shape[0]), 1) & (ROWS - 1), h)
         for k in range(2):
             choose = jnp.where(target[:, k : k + 1] == slot, 1.0, 0.0).astype(BF16)
-            for n in range(2):
-                totals[n] += weights[:, k : k + 1] * dot(choose, rows[n])
-    for n in range(2):
-        for copy in range(mixed.shape[0]):
-            mixed[copy, n] = totals[n].astype(BF16)
+            total += weights[:, k : k + 1] * dot(choose, rows)
+    for copy in range(mixed.shape[0]):
+        mixed[copy, 0] = total.astype(BF16)
 
 
 def combine(homes, target, weights, copies):
     tokens = target.shape[0]
-    shape = (copies, 2, tokens, homes[0].shape[-1])
+    terms, _, slots, part = homes[0].shape
     return pl.pallas_call(
         combine_kernel,
-        out_shape=jax.ShapeDtypeStruct(shape, BF16),
-        grid=(1,),
-        in_specs=[whole(target.shape), whole(weights.shape)] + [whole(h.shape) for h in homes],
-        out_specs=whole(shape),
-        compiler_params=params(),
-        cost_estimate=cost(8 * tokens * homes[0].size, 4 * homes[0].size + 4 * copies * tokens * shape[-1]),
+        out_shape=jax.ShapeDtypeStruct((copies, 2, tokens, part), BF16),
+        grid=(2,),
+        in_specs=[whole(target.shape), whole(weights.shape)]
+        + [pl.BlockSpec((terms, 1, slots, part), lambda n: (0, n, 0, 0)) for _ in homes],
+        out_specs=pl.BlockSpec((copies, 1, tokens, part), lambda n: (0, n, 0, 0)),
+        compiler_params=params(24),
+        cost_estimate=cost(8 * tokens * homes[0].size, 4 * homes[0].size + 4 * copies * tokens * part),
         name="combine",
     )(target, weights, *homes)
 
@@ -449,31 +481,20 @@
 
 def per_device(tokens, routes, route_weights, out_grad, w_gate, w_up, w_down):
     count_rows, width = tokens.shape
-    per_expert = 4 * count_rows // GROUPS
-    half = per_expert // 2
+    half = ROWS // GROUPS
     chunk = width // RING
     part = chunk // RING
     w_gate, w_up, w_down = w_gate[0], w_up[0], w_down[0]
-    place = [lax.axis_index(axis) for axis in AXES]
-    places = jnp.stack(place).astype(jnp.int32)
-    target = slots_of(routes, per_expert)
-    slots = jnp.arange(GROUPS * per_expert, dtype=jnp.int32).reshape(GROUPS, 2, half)
-
-    def placed(rows, h):
-        mine = slots if h is None else slots[:, h]
-        mine = mine.reshape(-1, 1)
-        dispatch = ((mine == target[None, :, 0]) | (mine == target[None, :, 1])).astype(BF16)
-        return dot(dispatch, rows).astype(BF16)
+    places = jnp.stack([lax.axis_index(axis) for axis in AXES]).astype(jnp.int32)
 
     def to_experts(rows):
         return lax.all_to_all(rows, EXPERT, split_axis=0, concat_axis=0, tiled=True)
 
-    def quarter(h):
-        return lax.dynamic_slice_in_dim(tokens, place[h] * chunk, chunk, axis=1)
-
-    quarters = jnp.stack([placed(quarter(h), h).reshape(GROUPS, half, chunk) for h in range(2)], axis=1)
+    quarters, target = dispatch(places, routes, tokens)
     got = to_experts(quarters)
-    rows_g = to_experts(placed(out_grad, None))
+    every = jnp.arange(2 * ROWS, dtype=jnp.int32)[:, None]
+    chosen = ((every == target[None, :, 0]) | (every == target[None, :, 1])).astype(BF16)
+    rows_g = to_experts(dot(chosen, out_grad).astype(BF16))
     near, far = gathered([got[:, h].reshape(ROWS, chunk) for h in range(2)])
     to_gate, to_up, out_parts = forward(places, near, far, w_gate, w_up, w_down)
     out_first = both_ways([p[0] for p in out_parts], [p[1] for p in out_parts])

time: 305 us -> 298 us (0.977)
    dot_general x3 -> x1, matrix products: 7.26 us -> 4.48 us  [dot(): return jnp.dot(a, b, preferred_element_type=F32)]
where the time goes in v3:
time: 298 us; the launch traced here: 297 us
  waiting for transfers between devices  92.5 us (31%)
  Pallas kernels  72.8 us (24%)
  blocking collectives  70.8 us (24%)
  starting transfers between devices  46.9 us (16%)
  local copies, waits for them, and re-layouts  8.8 us (3%)
  matrix products  4.48 us (2%)
    ppermute x20, waiting for transfers between devices, shift(): lax.ppermute(rows, axis, [(i, (i + step) % RING) for i in range(RING)])  49.4 us
    all_to_all x1, blocking collectives, per_device(): lax.all_to_all(copies, AXES, split_axis=0, concat_axis=0, tiled=True)  43.4 us
    ppermute x20, starting transfers between devices, shift(): lax.ppermute(rows, axis, [(i, (i + step) % RING) for i in range(RING)])  32.6 us
    all_to_all x1, blocking collectives, per_device(): lax.all_to_all(pieces, axes, split_axis=0, concat_axis=0, tiled=True)  27.4 us
    all_to_all x1, waiting for transfers between devices, per_device(): lax.all_to_all(pieces, axes, split_axis=0, concat_axis=0, tiled=True)  23 us
    pallas_call x1, Pallas kernels, backward(): pl.pallas_call(backward_kernel, out_shape=shapes, grid_spec=pltpu.Prefetc...  21.4 us
    all_to_all x2, waiting for transfers between devices, to_experts(): return lax.all_to_all(rows, EXPERT, split_axis=0, concat_axis=0, tiled=True)  20.2 us
    pallas_call x1, Pallas kernels, forward(): pl.pallas_call(forward_far_kernel, out_shape=[jax.ShapeDtypeStruct((2 * R...  13.9 us
  transfers between devices with their start and end apart: 23, of which 10 were waited for; matrix products, arithmetic and copies ran while one was open for 2% of the time, Pallas kernels for 17%

profile of v3, /device:TPU:0, one launch (start us, length us, event | category | flops | bytes accessed | tf_op | source)
XLA Modules:
  0.0 297.2 jit_solution(1746370571006721811)
XLA Ops:
  3.0 2.7 dispatch.1
  5.8 5.4 %all-to-all-start = ((bf16[8,2,32,1536]{3,2,1,0:T(8,128)(2,1)}), bf16[8,2,32,1536]{3,2,1,0:T(8,128)(2,1)S(1)}, u32[]{:S(2)}, u32[]{:S(2)}) async-start(bf16[8,2,32,1536]{3,2,1,0:T(8,128)(2,1)} %get-tuple-element.43), calls=%async_computation | async-start | bytes 3145728 | tf_op jit(solution)/shard_map/all_to_all | solution.py:491
  11.3 4.5 %convolution_convert_fusion = bf16[512,6144]{1,0:T(8,128)(2,1)} fusion(bf16[128,6144]{1,0:T(8,128)(2,1)S(1)} %copy-done, s32[128]{0:T(128)S(1)} %get-tuple-element.83, s32[128]{0:T(128)S(1)} %get-tuple-element.82), kind=kOutput, calls=%fused_computation | convolution fusion | flops 808648704 | bytes 7865344 | tf_op jit(solution)/shard_map/dot_general | solution.py:24
  15.8 16.9 %all-to-all-done = bf16[8,2,32,1536]{3,2,1,0:T(8,128)(2,1)S(1)} async-done(((bf16[8,2,32,1536]{3,2,1,0:T(8,128)(2,1)}), bf16[8,2,32,1536]{3,2,1,0:T(8,128)(2,1)S(1)}, u32[]{:S(2)}, u32[]{:S(2)}) %all-to-all-start) | async-done | bytes 1572896 | tf_op jit(solution)/shard_map/all_to_all | solution.py:491
  32.7 4.8 %all-to-all-start.1 = ((bf16[8,64,6144]{2,1,0:T(8,128)(2,1)}), bf16[8,64,6144]{2,1,0:T(8,128)(2,1)}, u32[]{:S(2)}, u32[]{:S(2)}) async-start(bf16[8,64,6144]{2,1,0:T(8,128)(2,1)} %bitcast.12), calls=%async_computation.1 | async-start | bytes 12582912 | tf_op jit(solution)/shard_map/all_to_all | solution.py:491
  40.8 1.7 collective-permute-start.2
  42.6 1.7 collective-permute-start.3
  44.2 14.5 %collective-permute-done.refs_0_.refs_2_ = bf16[256,1536]{1,0:T(8,128)(2,1)S(1)} collective-permute-done((bf16[256,1536]{1,0:T(8,128)(2,1)S(1)}, bf16[256,1536]{1,0:T(8,128)(2,1)S(1)}, u32[]{:S(2)}, u32[]{:S(2)}) %collective-permute-start) | collective-permute-done | bytes 786464 | tf_op jit(solution)/shard_map/ppermute | solution.py:20
  62.5 2.5 halves.1
  66.2 2.1 collective-permute-start.5
  71.5 13.3 %forward_near.1 = (f32[512,512]{1,0:T(8,128)}, f32[512,512]{1,0:T(8,128)}) custom-call(s32[2]{0:T(128)} %copy-done.3, bf16[256,1536]{1,0:T(8,128)(2,1)} %bitcast.28, bf16[256,1536]{1,0:T(8,128)(2,1)} %copy-done.16, bf16[256,1536]{1,0:T(8,128)(2,1)} %copy-done.14, bf16[256,1536]{1,0:T(8,128)(2,1)} %bitcast.25, bf16[256,1536]{1,0:T(8,128)(2,1)} %copy-done.17, ...), custom_call_target="tpu_custom_call" | custom-call | flops 4831838208 | bytes 23592960 | tf_op jit(solution)/shard_map/forward_near/pallas_call | solution.py:266
  86.0 13.9 %forward_far.1 = (f32[512,512]{1,0:T(8,128)}, f32[512,512]{1,0:T(8,128)}, bf16[2,4,128,384]{3,2,1,0:T(8,128)(2,1)}, bf16[2,4,128,384]{3,2,1,0:T(8,128)(2,1)}, bf...) custom-call(s32[2]{0:T(128)} %copy-done.3, ...), custom_call_target="tpu_custom_call" | custom-call | flops 4831838208 | bytes 17825792 | tf_op jit(solution)/shard_map/forward_far/pallas_call | solution.py:283
  100.8 2.4 collective-permute-start.11
  103.5 2.9 collective-permute-start.9
  106.4 3.2 %all-to-all-done.1 = bf16[8,64,6144]{2,1,0:T(8,128)(2,1)} async-done(((bf16[8,64,6144]{2,1,0:T(8,128)(2,1)}), bf16[8,64,6144]{2,1,0:T(8,128)(2,1)}, u32[]{:S(2)}, u32[]{:S(2)}) %all-to-all-start.1) | async-done | bytes 6291488 | tf_op jit(solution)/shard_map/all_to_all | solution.py:491
  109.7 21.4 %backward.1 = (bf16[3,4,128,384]{3,2,1,0:T(8,128)(2,1)}, bf16[3,4,128,384]{3,2,1,0:T(8,128)(2,1)}, bf16[4,128,384]{2,1,0:T(8,128)(2,1)}, bf16[4,128,384]{2,1,0:T...) custom-call(s32[2]{0:T(128)} %copy-done.3, ...), custom_call_target="tpu_custom_call" | custom-call | flops 9663676416 | bytes 31457280 | tf_op jit(solution)/shard_map/backward/pallas_call | solution.py:312
  132.8 3.1 %ring_join.1 = (bf16[3,4,128,384]{3,2,1,0:T(8,128)(2,1)}, bf16[3,4,128,384]{3,2,1,0:T(8,128)(2,1)}, bf16[3,4,128,384]{3,2,1,0:T(8,128)(2,1)}, bf16[3,4,128,384]{3,2,1,0:T(8,128)(2,1)}) custom-call(bf16[4,128,384]{2,1,0:T(8,128)(2,1)} %get-tuple-element.53.refs_0_, ...), custom_call_target="tpu_custom_call", output_to_operand_aliasing={{0}: (8, {}), {1}: (9, {}), {2}: (10, {}), {3}: (11, {})} | custom-call | bytes 4718592 | tf_op jit(solution)/shard_map/ring_join/pallas_call | solution.py:406
  137.3 1.7 collective-permute-start.13
  142.3 22.5 %collective-permute-done.12.refs_4_.refs_3_.refs_11_ = bf16[3,4,128,384]{3,2,1,0:T(8,128)(2,1)S(1)} collective-permute-done((bf16[3,4,128,384]{3,2,1,0:T(8,128)(2,1)}, bf16[3,4,128,384]{3,2,1,0:T(8,128)(2,1)S(1)}, u32[]{:S(2)}, u32[]{:S(2)}) %collective-permute-start.12) | collective-permute-done | bytes 1179680 | tf_op jit(solution)/shard_map/ppermute | solution.py:20
  164.8 2.7 collective-permute-done.14.refs_5_.refs_8_.refs_16_
  169.0 3.1 %ring_later.1 = (bf16[4,128,384]{2,1,0:T(8,128)(2,1)}, bf16[4,128,384]{2,1,0:T(8,128)(2,1)}, bf16[4,128,384]{2,1,0:T(8,128)(2,1)}, bf16[4,128,384]{2,1,0:T(8,128)(2,1)}) custom-call(bf16[4,128,384]{2,1,0:T(8,128)(2,1)} %get-tuple-element.71.refs_0_, bf16[4,128,384]{2,1,0:T(8,128)(2,1)} %get-tuple-element.72.refs_1_, ...), custom_call_target="tpu_custom_call" | custom-call | bytes 4718592 | tf_op jit(solution)/shard_map/ring_later/pallas_call | solution.py:423
  172.4 3.0 collective-permute-start.17
  176.5 2.1 collective-permute-start.19
  178.6 4.2 %collective-permute-done.16.refs_13_ = bf16[4,128,384]{2,1,0:T(8,128)(2,1)S(1)} collective-permute-done((bf16[4,128,384]{2,1,0:T(8,128)(2,1)}, bf16[4,128,384]{2,1,0:T(8,128)(2,1)S(1)}, u32[]{:S(2)}, u32[]{:S(2)}) %collective-permute-start.16) | collective-permute-done | bytes 393248 | tf_op jit(solution)/shard_map/ppermute | solution.py:20
  182.8 2.7 collective-permute-done.18.refs_18_
  186.4 6.0 %ring_end.1 = (bf16[4,8,2,32,384]{4,3,2,1,0:T(8,128)(2,1)}, bf16[4,8,2,32,384]{4,3,2,1,0:T(8,128)(2,1)}) custom-call(bf16[4,256,384]{2,1,0:T(8,128)(2,1)} %get-tuple-element.50.refs_0_, bf16[2,4,128,384]{3,2,1,0:T(8,128)(2,1)} %copy-done.10, bf16[2,4,128,384]{3,2,1,0:T(8,128)(2,1)} %copy-done.11, bf16[3,4,128,384]{3,2,1,0:T(8,128)(2,1)} %copy-done.4, ...), custom_call_target="tpu_custom_call" | custom-call | bytes 12582912 | tf_op jit(solution)/shard_map/ring_end/pallas_call | solution.py:449
  192.4 27.4 %all_to_all.29.refs_0_ = bf16[32,2,32,384]{3,2,1,0:T(8,128)(2,1)S(1)} all-to-all(bf16[32,2,32,384]{3,2,1,0:T(8,128)(2,1)} %bitcast.22), channel_id=1, replica_groups=mesh['z'=4,'core'=2,'y'=4,'x'=4] {'y','z','core'}, dimensions={0} | all-to-all | bytes 3145728 | tf_op jit(solution)/shard_map/all_to_all | solution.py:510
  219.8 4.1 %all-to-all-start.3 = ((bf16[32,2,32,384]{3,2,1,0:T(8,128)(2,1)}), bf16[32,2,32,384]{3,2,1,0:T(8,128)(2,1)S(1)}, u32[]{:S(2)}, u32[]{:S(2)}) async-start(bf16[32,2,32,384]{3,2,1,0:T(8,128)(2,1)} %bitcast.21), calls=%async_computation.3 | async-start | bytes 3145728 | tf_op jit(solution)/shard_map/all_to_all | solution.py:510
  224.1 23.0 %all-to-all-done.3.refs_1_ = bf16[32,2,32,384]{3,2,1,0:T(8,128)(2,1)S(1)} async-done(((bf16[32,2,32,384]{3,2,1,0:T(8,128)(2,1)}), bf16[32,2,32,384]{3,2,1,0:T(8,128)(2,1)S(1)}, u32[]{:S(2)}, u32[]{:S(2)}) %all-to-all-start.3) | async-done | bytes 1572896 | tf_op jit(solution)/shard_map/all_to_all | solution.py:510
  247.1 2.5 combine.1
  249.6 43.4 %all_to_all.30.slices = bf16[16,2,128,384]{3,2,1,0:T(8,128)(2,1)} all-to-all(bf16[16,2,128,384]{3,2,1,0:T(8,128)(2,1)S(1)} %combine.1), channel_id=1, replica_groups=mesh['z'=4,'core'=2,'y'=4,'x'=4] {'x','y'}, dimensions={0} | all-to-all | bytes 6291456 | tf_op jit(solution)/shard_map/all_to_all | solution.py:512
  293.0 4.2 %assemble.1 = (bf16[128,6144]{1,0:T(8,128)(2,1)}, bf16[128,6144]{1,0:T(8,128)(2,1)}) custom-call(bf16[16,2,128,384]{3,2,1,0:T(8,128)(2,1)} %all_to_all.30.slices), custom_call_target="tpu_custom_call" | custom-call | bytes 6291456 | tf_op jit(solution)/shard_map/assemble/pallas_call | solution.py:470
  (86 shorter events, 26.7 us)
Async XLA Ops:
  0.6 10.7 %copy-start = (bf16[128,6144]{1,0:T(8,128)(2,1)S(1)}, bf16[128,6144]{1,0:T(8,128)(2,1)}, u32[]{:S(2)}) copy-start(bf16[128,6144]{1,0:T(8,128)(2,1)} %param.10) | copy-start | bytes 4718596
  3.0 2.7 copy-start.3
  5.8 27.0 %all-to-all-start = ((bf16[8,2,32,1536]{3,2,1,0:T(8,128)(2,1)}), bf16[8,2,32,1536]{3,2,1,0:T(8,128)(2,1)S(1)}, u32[]{:S(2)}, u32[]{:S(2)}) async-start(bf16[8,2,32,1536]{3,2,1,0:T(8,128)(2,1)} %get-tuple-element.43), calls=%async_computation | async-start | bytes 3145728 | tf_op jit(solution)/shard_map/all_to_all | solution.py:491
  32.7 76.9 %all-to-all-start.1 = ((bf16[8,64,6144]{2,1,0:T(8,128)(2,1)}), bf16[8,64,6144]{2,1,0:T(8,128)(2,1)}, u32[]{:S(2)}, u32[]{:S(2)}) async-start(bf16[8,64,6144]{2,1,0:T(8,128)(2,1)} %bitcast.12), calls=%async_computation.1 | async-start | bytes 12582912 | tf_op jit(solution)/shard_map/all_to_all | solution.py:491
  37.6 27.3 %copy-start.12 = (bf16[8,1,32,1536]{3,2,1,0:T(8,128)(2,1)}, bf16[8,1,32,1536]{3,2,1,0:T(8,128)(2,1)S(1)}, u32[]{:S(2)}) copy-start(bf16[8,1,32,1536]{3,2,1,0:T(8,128)(2,1)S(1)} %get-tuple-element.84) | copy-start | bytes 2359300
  37.6 27.3 %copy-start.13 = (bf16[8,1,32,1536]{3,2,1,0:T(8,128)(2,1)}, bf16[8,1,32,1536]{3,2,1,0:T(8,128)(2,1)S(1)}, u32[]{:S(2)}) copy-start(bf16[8,1,32,1536]{3,2,1,0:T(8,128)(2,1)S(1)} %get-tuple-element.85) | copy-start | bytes 2359300
  37.7 21.1 %collective-permute-start = (bf16[256,1536]{1,0:T(8,128)(2,1)S(1)}, bf16[256,1536]{1,0:T(8,128)(2,1)S(1)}, u32[]{:S(2)}, u32[]{:S(2)}) collective-permute-start(bf16[256,1536]{1,0:T(8,128)(2,1)S(1)} %bitcast.26), channel_id=1, source_target_pairs={{0,1},{1,2},{2,3},{3,0},{4,5},{5,6},{6,7},{7,4},{8,9},{9,10},{10,1... | collective-permute-start | bytes 2359304 | tf_op jit(solution)/shard_map/ppermute | solution.py:20
  39.2 20.8 %collective-permute-start.1 = (bf16[256,1536]{1,0:T(8,128)(2,1)S(1)}, bf16[256,1536]{1,0:T(8,128)(2,1)S(1)}, u32[]{:S(2)}, u32[]{:S(2)}) collective-permute-start(bf16[256,1536]{1,0:T(8,128)(2,1)S(1)} %bitcast.23), channel_id=1, source_target_pairs={{0,4},{4,8},{8,12},{12,0},{1,5},{5,9},{9,13},{13,1},{2,6},{6,10},{... | collective-permute-start | bytes 2359304 | tf_op jit(solution)/shard_map/ppermute | solution.py:20
  40.8 19.2 %collective-permute-start.2 = (bf16[256,1536]{1,0:T(8,128)(2,1)S(1)}, bf16[256,1536]{1,0:T(8,128)(2,1)S(1)}, u32[]{:S(2)}, u32[]{:S(2)}) collective-permute-start(bf16[256,1536]{1,0:T(8,128)(2,1)S(1)} %bitcast.27), channel_id=1, source_target_pairs={{0,3},{1,0},{2,1},{3,2},{4,7},{5,4},{6,5},{7,6},{8,11},{9,8},{10,9... | collective-permute-start | bytes 2359304 | tf_op jit(solution)/shard_map/ppermute | solution.py:20
  42.6 19.0 %collective-permute-start.3 = (bf16[256,1536]{1,0:T(8,128)(2,1)S(1)}, bf16[256,1536]{1,0:T(8,128)(2,1)S(1)}, u32[]{:S(2)}, u32[]{:S(2)}) collective-permute-start(bf16[256,1536]{1,0:T(8,128)(2,1)S(1)} %bitcast.24), channel_id=1, source_target_pairs={{0,12},{4,0},{8,4},{12,8},{1,13},{5,1},{9,5},{13,9},{2,14},{6,2},{... | collective-permute-start | bytes 2359304 | tf_op jit(solution)/shard_map/ppermute | solution.py:20
  58.8 2.8 copy-start.14
  65.0 19.8 %collective-permute-start.4 = (bf16[128,1536]{1,0:T(8,128)(2,1)}, bf16[128,1536]{1,0:T(8,128)(2,1)S(1)}, u32[]{:S(2)}, u32[]{:S(2)}) collective-permute-start(bf16[128,1536]{1,0:T(8,128)(2,1)} %get-tuple-element.44), channel_id=1, source_target_pairs={{0,1},{1,2},{2,3},{3,0},{4,5},{5,6},{6,7},{7,4},{8,9},{9,10},{10,1... | collective-permute-start | bytes 1179656 | tf_op jit(solution)/shard_map/ppermute | solution.py:20
  66.2 18.6 %collective-permute-start.5 = (bf16[128,1536]{1,0:T(8,128)(2,1)}, bf16[128,1536]{1,0:T(8,128)(2,1)S(1)}, u32[]{:S(2)}, u32[]{:S(2)}) collective-permute-start(bf16[128,1536]{1,0:T(8,128)(2,1)} %get-tuple-element.45), channel_id=1, source_target_pairs={{0,3},{1,0},{2,1},{3,2},{4,7},{5,4},{6,5},{7,6},{8,11},{9,8},{10,9... | collective-permute-start | bytes 1179656 | tf_op jit(solution)/shard_map/ppermute | solution.py:20
  68.3 16.6 %collective-permute-start.6 = (bf16[128,1536]{1,0:T(8,128)(2,1)}, bf16[128,1536]{1,0:T(8,128)(2,1)S(1)}, u32[]{:S(2)}, u32[]{:S(2)}) collective-permute-start(bf16[128,1536]{1,0:T(8,128)(2,1)} %get-tuple-element.46), channel_id=1, source_target_pairs={{0,4},{4,8},{8,12},{12,0},{1,5},{5,9},{9,13},{13,1},{2,6},{6,10},{... | collective-permute-start | bytes 1179656 | tf_op jit(solution)/shard_map/ppermute | solution.py:20
  69.9 15.0 %collective-permute-start.7 = (bf16[128,1536]{1,0:T(8,128)(2,1)}, bf16[128,1536]{1,0:T(8,128)(2,1)S(1)}, u32[]{:S(2)}, u32[]{:S(2)}) collective-permute-start(bf16[128,1536]{1,0:T(8,128)(2,1)} %get-tuple-element.47), channel_id=1, source_target_pairs={{0,12},{4,0},{8,4},{12,8},{1,13},{5,1},{9,5},{13,9},{2,14},{6,2},{... | collective-permute-start | bytes 1179656 | tf_op jit(solution)/shard_map/ppermute | solution.py:20
  99.9 31.2 %collective-permute-start.10 = (bf16[2,4,128,384]{3,2,1,0:T(8,128)(2,1)}, bf16[2,4,128,384]{3,2,1,0:T(8,128)(2,1)S(1)}, u32[]{:S(2)}, u32[]{:S(2)}) collective-permute-start(bf16[2,4,128,384]{3,2,1,0:T(8,128)(2,1)} %get-tuple-element.57), channel_id=1, source_target_pairs={{0,4},{4,8},{8,12},{12,0},{1,5},{5,9},{9,13},{13,1},{2,6},{6,10},{... | collective-permute-start | bytes 2359304 | tf_op jit(solution)/shard_map/ppermute | solution.py:20
  100.8 30.3 %collective-permute-start.11 = (bf16[2,4,128,384]{3,2,1,0:T(8,128)(2,1)}, bf16[2,4,128,384]{3,2,1,0:T(8,128)(2,1)S(1)}, u32[]{:S(2)}, u32[]{:S(2)}) collective-permute-start(bf16[2,4,128,384]{3,2,1,0:T(8,128)(2,1)} %get-tuple-element.58), channel_id=1, source_target_pairs={{0,12},{4,0},{8,4},{12,8},{1,13},{5,1},{9,5},{13,9},{2,14},{6,2},{... | collective-permute-start | bytes 2359304 | tf_op jit(solution)/shard_map/ppermute | solution.py:20
  103.2 27.9 %collective-permute-start.8 = (bf16[2,4,128,384]{3,2,1,0:T(8,128)(2,1)}, bf16[2,4,128,384]{3,2,1,0:T(8,128)(2,1)S(1)}, u32[]{:S(2)}, u32[]{:S(2)}) collective-permute-start(bf16[2,4,128,384]{3,2,1,0:T(8,128)(2,1)} %get-tuple-element.51), channel_id=1, source_target_pairs={{0,1},{1,2},{2,3},{3,0},{4,5},{5,6},{6,7},{7,4},{8,9},{9,10},{10,1... | collective-permute-start | bytes 2359304 | tf_op jit(solution)/shard_map/ppermute | solution.py:20
  103.5 27.6 %collective-permute-start.9 = (bf16[2,4,128,384]{3,2,1,0:T(8,128)(2,1)}, bf16[2,4,128,384]{3,2,1,0:T(8,128)(2,1)S(1)}, u32[]{:S(2)}, u32[]{:S(2)}) collective-permute-start(bf16[2,4,128,384]{3,2,1,0:T(8,128)(2,1)} %get-tuple-element.52), channel_id=1, source_target_pairs={{0,3},{1,0},{2,1},{3,2},{4,7},{5,4},{6,5},{7,6},{8,11},{9,8},{10,9... | collective-permute-start | bytes 2359304 | tf_op jit(solution)/shard_map/ppermute | solution.py:20
  135.8 28.9 %collective-permute-start.12 = (bf16[3,4,128,384]{3,2,1,0:T(8,128)(2,1)}, bf16[3,4,128,384]{3,2,1,0:T(8,128)(2,1)S(1)}, u32[]{:S(2)}, u32[]{:S(2)}) collective-permute-start(bf16[3,4,128,384]{3,2,1,0:T(8,128)(2,1)} %get-tuple-element.65), channel_id=1, source_target_pairs={{0,1},{1,2},{2,3},{3,0},{4,5},{5,6},{6,7},{7,4},{8,9},{9,10},{10,1... | collective-permute-start | bytes 3538952 | tf_op jit(solution)/shard_map/ppermute | solution.py:20
  137.3 27.4 %collective-permute-start.13 = (bf16[3,4,128,384]{3,2,1,0:T(8,128)(2,1)}, bf16[3,4,128,384]{3,2,1,0:T(8,128)(2,1)S(1)}, u32[]{:S(2)}, u32[]{:S(2)}) collective-permute-start(bf16[3,4,128,384]{3,2,1,0:T(8,128)(2,1)} %get-tuple-element.66), channel_id=1, source_target_pairs={{0,3},{1,0},{2,1},{3,2},{4,7},{5,4},{6,5},{7,6},{8,11},{9,8},{10,9... | collective-permute-start | bytes 3538952 | tf_op jit(solution)/shard_map/ppermute | solution.py:20
  139.1 28.4 %collective-permute-start.14 = (bf16[3,4,128,384]{3,2,1,0:T(8,128)(2,1)}, bf16[3,4,128,384]{3,2,1,0:T(8,128)(2,1)S(1)}, u32[]{:S(2)}, u32[]{:S(2)}) collective-permute-start(bf16[3,4,128,384]{3,2,1,0:T(8,128)(2,1)} %get-tuple-element.68), channel_id=1, source_target_pairs={{0,4},{4,8},{8,12},{12,0},{1,5},{5,9},{9,13},{13,1},{2,6},{6,10},{... | collective-permute-start | bytes 3538952 | tf_op jit(solution)/shard_map/ppermute | solution.py:20
  140.7 26.9 %collective-permute-start.15 = (bf16[3,4,128,384]{3,2,1,0:T(8,128)(2,1)}, bf16[3,4,128,384]{3,2,1,0:T(8,128)(2,1)S(1)}, u32[]{:S(2)}, u32[]{:S(2)}) collective-permute-start(bf16[3,4,128,384]{3,2,1,0:T(8,128)(2,1)} %get-tuple-element.69), channel_id=1, source_target_pairs={{0,12},{4,0},{8,4},{12,8},{1,13},{5,1},{9,5},{13,9},{2,14},{6,2},{... | collective-permute-start | bytes 3538952 | tf_op jit(solution)/shard_map/ppermute | solution.py:20
  164.8 2.8 copy-start.4
  164.8 2.8 copy-start.5
  172.1 10.7 %collective-permute-start.16 = (bf16[4,128,384]{2,1,0:T(8,128)(2,1)}, bf16[4,128,384]{2,1,0:T(8,128)(2,1)S(1)}, u32[]{:S(2)}, u32[]{:S(2)}) collective-permute-start(bf16[4,128,384]{2,1,0:T(8,128)(2,1)} %get-tuple-element.75), channel_id=1, source_target_pairs={{0,1},{1,2},{2,3},{3,0},{4,5},{5,6},{6,7},{7,4},{8,9},{9,10},{10,1... | collective-permute-start | bytes 1179656 | tf_op jit(solution)/shard_map/ppermute | solution.py:20
  172.4 10.4 %collective-permute-start.17 = (bf16[4,128,384]{2,1,0:T(8,128)(2,1)}, bf16[4,128,384]{2,1,0:T(8,128)(2,1)S(1)}, u32[]{:S(2)}, u32[]{:S(2)}) collective-permute-start(bf16[4,128,384]{2,1,0:T(8,128)(2,1)} %get-tuple-element.76), channel_id=1, source_target_pairs={{0,3},{1,0},{2,1},{3,2},{4,7},{5,4},{6,5},{7,6},{8,11},{9,8},{10,9... | collective-permute-start | bytes 1179656 | tf_op jit(solution)/shard_map/ppermute | solution.py:20
  175.3 10.1 %collective-permute-start.18 = (bf16[4,128,384]{2,1,0:T(8,128)(2,1)}, bf16[4,128,384]{2,1,0:T(8,128)(2,1)S(1)}, u32[]{:S(2)}, u32[]{:S(2)}) collective-permute-start(bf16[4,128,384]{2,1,0:T(8,128)(2,1)} %get-tuple-element.78), channel_id=1, source_target_pairs={{0,4},{4,8},{8,12},{12,0},{1,5},{5,9},{9,13},{13,1},{2,6},{6,10},{... | collective-permute-start | bytes 1179656 | tf_op jit(solution)/shard_map/ppermute | solution.py:20
  176.5 8.9 %collective-permute-start.19 = (bf16[4,128,384]{2,1,0:T(8,128)(2,1)}, bf16[4,128,384]{2,1,0:T(8,128)(2,1)S(1)}, u32[]{:S(2)}, u32[]{:S(2)}) collective-permute-start(bf16[4,128,384]{2,1,0:T(8,128)(2,1)} %get-tuple-element.79), channel_id=1, source_target_pairs={{0,12},{4,0},{8,4},{12,8},{1,13},{5,1},{9,5},{13,9},{2,14},{6,2},{... | collective-permute-start | bytes 1179656 | tf_op jit(solution)/shard_map/ppermute | solution.py:20
  219.8 4.1 %copy-start.26 = (f32[128,2]{0,1:T(2,128)S(1)}, f32[128,2]{0,1:T(2,128)}, u32[]{:S(2)}) copy-start(f32[128,2]{0,1:T(2,128)} %param.9) | copy-start | bytes 3076
  219.8 27.2 %all-to-all-start.3 = ((bf16[32,2,32,384]{3,2,1,0:T(8,128)(2,1)}), bf16[32,2,32,384]{3,2,1,0:T(8,128)(2,1)S(1)}, u32[]{:S(2)}, u32[]{:S(2)}) async-start(bf16[32,2,32,384]{3,2,1,0:T(8,128)(2,1)} %bitcast.21), calls=%async_computation.3 | async-start | bytes 3145728 | tf_op jit(solution)/shard_map/all_to_all | solution.py:510
  249.6 47.6 %copy-start.1 = (bf16[128,6144]{1,0:T(8,128)(2,1)S(1)}, bf16[128,6144]{1,0:T(8,128)(2,1)}, u32[]{:S(2)}) copy-start(bf16[128,6144]{1,0:T(8,128)(2,1)} %param.10) | copy-start | bytes 4718596
  (18 other events, 23.7 us)

commit v4 on v3

--- a/solution.py
+++ b/solution.py
@@ -1,3 +1,5 @@
+import functools
+
 import jax
 import jax.numpy as jnp
 from jax import lax
@@ -32,7 +34,7 @@
     return pl.BlockSpec(shape, lambda *_: (0,) * len(shape))
 
 
-def params(mib=58):
+def params(mib=63):
     return pltpu.CompilerParams(vmem_limit_bytes=mib * MIB)
 
 
@@ -78,15 +80,26 @@
             + [pl.BlockSpec((tokens, chunk), lambda i, place, h=h: (0, place[h])) for h in range(2)],
             out_specs=[whole(shape), whole(routes.shape)],
         ),
-        compiler_params=params(16),
+        compiler_params=params(),
         cost_estimate=cost(8 * ROWS * tokens * chunk, 8 * tokens * chunk + 4 * ROWS * chunk),
         name="dispatch",
     )(place, routes, rows, rows)
 
 
+ANYWHERE = pl.BlockSpec(memory_space=pl.ANY)
+
+
 def halves_kernel(*refs):
-    for source, to in zip(refs[:4], refs[4:]):
-        to[...] = source[...]
+    sources, ends, sems = refs[:4], refs[4:8], refs[8]
+    half = ends[0].shape[0]
+    copies = [
+        pltpu.make_async_copy(source.at[pl.ds(n // 2 * half, half)], end, sems.at[n])
+        for n, (source, end) in enumerate(zip(sources, ends))
+    ]
+    for copy in copies:
+        copy.start()
+    for copy in copies:
+        copy.wait()
 
 
 def gathered(owns):
@@ -94,14 +107,12 @@
     half = rows // 2
     befores = [shift(own, axis, 1) for own, axis in zip(owns, AXES)]
     afters = [shift(own, axis, -1) for own, axis in zip(owns, AXES)]
-    top = pl.BlockSpec((half, chunk), lambda i: (0, 0))
-    bottom = pl.BlockSpec((half, chunk), lambda i: (1, 0))
     send = pl.pallas_call(
         halves_kernel,
         out_shape=[jax.ShapeDtypeStruct((half, chunk), BF16)] * 4,
-        grid=(1,),
-        in_specs=[top, top, bottom, bottom],
-        out_specs=[whole((half, chunk))] * 4,
+        in_specs=[ANYWHERE] * 4,
+        out_specs=[ANYWHERE] * 4,
+        scratch_shapes=[pltpu.SemaphoreType.DMA((4,))],
         compiler_params=params(),
         cost_estimate=cost(0, 16 * half * chunk),
         name="halves",
@@ -308,7 +319,6 @@
     block = width // STEPS
     rows = rows.reshape(GROUPS, 2, ROWS // GROUPS, width)
     shapes, specs = emitted(width, STEPS, 1)
-    anywhere = pl.BlockSpec(memory_space=pl.ANY)
     outs = pl.pallas_call(
         backward_kernel,
         out_shape=shapes,
@@ -320,8 +330,8 @@
                 pl.BlockSpec((hid, block), lambda i, place: (0, jnp.minimum(i, STEPS - 1))),
                 whole((count, hid)),
                 whole((count, hid)),
-                anywhere,
-                anywhere,
+                ANYWHERE,
+                ANYWHERE,
             ],
             out_specs=specs,
             scratch_shapes=[
@@ -362,7 +372,7 @@
         in_specs=[whole(target.shape), whole(weights.shape)]
         + [pl.BlockSpec((terms, 1, slots, part), lambda n: (0, n, 0, 0)) for _ in homes],
         out_specs=pl.BlockSpec((copies, 1, tokens, part), lambda n: (0, n, 0, 0)),
-        compiler_params=params(24),
+        compiler_params=params(),
         cost_estimate=cost(8 * tokens * homes[0].size, 4 * homes[0].size + 4 * copies * tokens * part),
         name="combine",
     )(target, weights, *homes)
@@ -372,9 +382,31 @@
     return sum(t.astype(F32) for t in terms).astype(BF16)
 
 
-def later_kernel(*refs):
-    for own, got, send in zip(refs[:4], refs[4:8], refs[-4:]):
-        send[...] = add(own[...], got[0]).reshape(send.shape)
+def later_kernel(block, *refs):
+    owns, gots, sends, (mine, came, in_sems, out_sems) = refs[:4], refs[4:8], refs[-8:-4], refs[-4:]
+    loads, stores = [], []
+    for n in range(4):
+        loads.append(
+            [
+                pltpu.make_async_copy(owns[n], mine.at[n], in_sems.at[0, n]),
+                pltpu.make_async_copy(gots[n].at[0], came.at[n], in_sems.at[1, n]),
+            ]
+        )
+        to = sends[n] if block is None else sends[n].at[block]
+        stores.append(pltpu.make_async_copy(mine.at[n], to, out_sems.at[n]))
+        for load in loads[n]:
+            load.start()
+    for n in range(4):
+        for load in loads[n]:
+            load.wait()
+        mine[n] = add(mine[n], came[n])
+        stores[n].start()
+    for store in stores:
+        store.wait()
+
+
+def later_scratch(half):
+    return [pltpu.VMEM((4, *half), BF16)] * 2 + [pltpu.SemaphoreType.DMA((2, 4)), pltpu.SemaphoreType.DMA((4,))]
 
 
 def total_kernel(*refs):
@@ -400,15 +432,13 @@
 
 def ring_join(parts, first, plus, minus):
     half = parts[0][2].shape
-    block = pl.BlockSpec((1, *half), lambda i: (0, 0, 0, 0))
-    third = pl.BlockSpec((1, *half), lambda i: (2, 0, 0, 0))
     buffers = [*plus, *minus]
     outs = pl.pallas_call(
-        later_kernel,
+        functools.partial(later_kernel, 2),
         out_shape=[jax.ShapeDtypeStruct(b.shape, BF16) for b in buffers],
-        grid=(1,),
-        in_specs=[whole(half)] * 4 + [block] * 4 + [pl.BlockSpec(memory_space=pl.ANY)] * 4,
-        out_specs=[third] * 4,
+        in_specs=[ANYWHERE] * 12,
+        out_specs=[ANYWHERE] * 4,
+        scratch_shapes=later_scratch(half),
         input_output_aliases={8 + n: n for n in range(4)},
         compiler_params=params(),
         cost_estimate=cost(0, 24 * half[0] * half[1] * half[2]),
@@ -419,13 +449,12 @@
 
 def ring_later(parts, first):
     half = parts[0][2].shape
-    block = pl.BlockSpec((1, *half), lambda i: (0, 0, 0, 0))
     outs = pl.pallas_call(
-        later_kernel,
+        functools.partial(later_kernel, None),
         out_shape=[jax.ShapeDtypeStruct(half, BF16)] * 4,
-        grid=(1,),
-        in_specs=[whole(half)] * 4 + [block] * 4,
-        out_specs=[whole(half)] * 4,
+        in_specs=[ANYWHERE] * 8,
+        out_specs=[ANYWHERE] * 4,
+        scratch_shapes=later_scratch(half),
         compiler_params=params(),
         cost_estimate=cost(0, 24 * half[0] * half[1] * half[2]),
         name="ring_later",
@@ -458,11 +487,18 @@
     )(*operands)
 
 
-def assemble_kernel(slices, *results):
+def assemble_kernel(slices, *refs):
+    results, sems = refs[:2], refs[2]
     count, _, _, part = slices.shape
-    for n, result in enumerate(results):
-        for c in range(count):
-            result[:, c * part : (c + 1) * part] = slices[c, n]
+    copies = [
+        pltpu.make_async_copy(slices.at[c, n], result.at[:, pl.ds(c * part, part)], sems.at[c, n])
+        for c in range(count)
+        for n, result in enumerate(results)
+    ]
+    for copy in copies:
+        copy.start()
+    for copy in copies:
+        copy.wait()
 
 
 def assemble(slices):
@@ -470,9 +506,9 @@
     return pl.pallas_call(
         assemble_kernel,
         out_shape=[jax.ShapeDtypeStruct((tokens, count * part), BF16)] * 2,
-        grid=(RING,),
-        in_specs=[pl.BlockSpec((count // RING, 2, tokens, part), lambda i: (i, 0, 0, 0))],
-        out_specs=[pl.BlockSpec((tokens, count // RING * part), lambda i: (0, i))] * 2,
+        in_specs=[ANYWHERE],
+        out_specs=[ANYWHERE] * 2,
+        scratch_shapes=[pltpu.SemaphoreType.DMA((count, 2))],
         compiler_params=params(),
         cost_estimate=cost(0, 4 * slices.size),
         name="assemble",

time: 298 us -> 433 us (1.45)
  Pallas kernels: 72.8 us -> 214 us
  waiting for transfers between devices: 92.5 us -> 83.9 us
    pallas_call x1, Pallas kernels: 4.21 us -> 96.7 us  [assemble(): pl.pallas_call(assemble_kernel, out_shape=[jax.ShapeDtypeStruct((tokens,...]
    pallas_call x1, Pallas kernels: 2.53 us -> 48.8 us  [gathered(): pl.pallas_call(halves_kernel, out_shape=[jax.ShapeDtypeStruct((half, chun...]
    ppermute x20, waiting for transfers between devices: 49.4 us -> 44.6 us  [shift(): lax.ppermute(rows, axis, [(i, (i + step) % RING) for i in range(RING)])]
  transfers between devices with their start and end apart: 23 -> 23, of which waited for: 10 -> 8; matrix products, arithmetic and copies ran while one was open for 2% -> 1% of each run, Pallas kernels for 17% -> 23%
where the time goes in v4:
time: 433 us; the launch traced here: 432 us
  Pallas kernels  214 us (49%)
  waiting for transfers between devices  83.9 us (19%)
  blocking collectives  74.1 us (17%)
  starting transfers between devices  47.8 us (11%)
  local copies, waits for them, and re-layouts  5.96 us (1%)
  matrix products  4.44 us (1%)
    pallas_call x1, Pallas kernels, assemble(): pl.pallas_call(assemble_kernel, out_shape=[jax.ShapeDtypeStruct((tokens,...  96.7 us
    pallas_call x1, Pallas kernels, gathered(): pl.pallas_call(halves_kernel, out_shape=[jax.ShapeDtypeStruct((half, chun...  48.8 us
    ppermute x20, waiting for transfers between devices, shift(): lax.ppermute(rows, axis, [(i, (i + step) % RING) for i in range(RING)])  44.6 us
    all_to_all x1, blocking collectives, per_device(): lax.all_to_all(copies, AXES, split_axis=0, concat_axis=0, tiled=True)  44.3 us
    ppermute x20, starting transfers between devices, shift(): lax.ppermute(rows, axis, [(i, (i + step) % RING) for i in range(RING)])  32.7 us
    all_to_all x1, blocking collectives, per_device(): lax.all_to_all(pieces, axes, split_axis=0, concat_axis=0, tiled=True)  29.8 us
    all_to_all x1, waiting for transfers between devices, per_device(): lax.all_to_all(pieces, axes, split_axis=0, concat_axis=0, tiled=True)  22.3 us
    pallas_call x1, Pallas kernels, backward(): pl.pallas_call(backward_kernel, out_shape=shapes, grid_spec=pltpu.Prefetc...  21.4 us
  transfers between devices with their start and end apart: 23, of which 8 were waited for; matrix products, arithmetic and copies ran while one was open for 1% of the time, Pallas kernels for 23%

profile of v4, /device:TPU:0, one launch (start us, length us, event | category | flops | bytes accessed | tf_op | source)
XLA Modules:
  0.0 431.8 jit_solution(17972917250078575772)
XLA Ops:
  2.6 4.0 dispatch.1
  6.6 5.5 %all-to-all-start = ((bf16[8,2,32,1536]{3,2,1,0:T(8,128)(2,1)}), bf16[8,2,32,1536]{3,2,1,0:T(8,128)(2,1)S(1)}, u32[]{:S(2)}, u32[]{:S(2)}) async-start(bf16[8,2,32,1536]{3,2,1,0:T(8,128)(2,1)} %get-tuple-element.43), calls=%async_computation | async-start | bytes 3145728 | tf_op jit(solution)/shard_map/all_to_all | solution.py:527
  12.3 4.4 %convolution_convert_fusion = bf16[512,6144]{1,0:T(8,128)(2,1)} fusion(bf16[128,6144]{1,0:T(8,128)(2,1)S(1)} %copy-done.1, s32[128]{0:T(128)S(1)} %get-tuple-element.83, s32[128]{0:T(128)S(1)} %get-tuple-element.82), kind=kOutput, calls=%fused_computation | convolution fusion | flops 808648704 | bytes 7865344 | tf_op jit(solution)/shard_map/dot_general | solution.py:26
  16.8 17.0 %all-to-all-done = bf16[8,2,32,1536]{3,2,1,0:T(8,128)(2,1)S(1)} async-done(((bf16[8,2,32,1536]{3,2,1,0:T(8,128)(2,1)}), bf16[8,2,32,1536]{3,2,1,0:T(8,128)(2,1)S(1)}, u32[]{:S(2)}, u32[]{:S(2)}) %all-to-all-start) | async-done | bytes 1572896 | tf_op jit(solution)/shard_map/all_to_all | solution.py:527
  33.7 4.8 %all-to-all-start.1 = ((bf16[8,64,6144]{2,1,0:T(8,128)(2,1)}), bf16[8,64,6144]{2,1,0:T(8,128)(2,1)}, u32[]{:S(2)}, u32[]{:S(2)}) async-start(bf16[8,64,6144]{2,1,0:T(8,128)(2,1)} %bitcast.12), calls=%async_computation.1 | async-start | bytes 12582912 | tf_op jit(solution)/shard_map/all_to_all | solution.py:527
  41.8 1.7 collective-permute-start.2
  45.2 14.5 %collective-permute-done.refs_0_.refs_2_ = bf16[256,1536]{1,0:T(8,128)(2,1)S(1)} collective-permute-done((bf16[256,1536]{1,0:T(8,128)(2,1)S(1)}, bf16[256,1536]{1,0:T(8,128)(2,1)S(1)}, u32[]{:S(2)}, u32[]{:S(2)}) %collective-permute-start) | collective-permute-done | bytes 786464 | tf_op jit(solution)/shard_map/ppermute | solution.py:22
  62.8 48.8 %halves.1 = (bf16[128,1536]{1,0:T(8,128)(2,1)}, bf16[128,1536]{1,0:T(8,128)(2,1)}, bf16[128,1536]{1,0:T(8,128)(2,1)}, bf16[128,1536]{1,0:T(8,128)(2,1)}) custom-call(bf16[256,1536]{1,0:T(8,128)(2,1)} %copy-done.4, bf16[256,1536]{1,0:T(8,128)(2,1)} %copy-done.5, bf16[256,1536]{1,0:T(8,128)(2,1)} %copy-done.6, ...), custom_call_target="tpu_custom_call" | custom-call | bytes 3145728 | tf_op jit(solution)/shard_map/halves/pallas_call | solution.py:110
  113.2 1.7 collective-permute-start.5
  116.3 1.8 collective-permute-start.7
  118.1 13.3 %forward_near.1 = (f32[512,512]{1,0:T(8,128)}, f32[512,512]{1,0:T(8,128)}) custom-call(s32[2]{0:T(128)} %pad_add_fusion.place, bf16[256,1536]{1,0:T(8,128)(2,1)} %bitcast.27, bf16[256,1536]{1,0:T(8,128)(2,1)} %copy-done.6, bf16[256,1536]{1,0:T(8,128)(2,1)} %copy-done.4, bf16[256,1536]{1,0:T(8,128)(2,1)} %bitcast.24, ...), custom_call_target="tpu_custom_call" | custom-call | flops 4831838208 | bytes 23592960 | tf_op jit(solution)/shard_map/forward_near/pallas_call | solution.py:277
  132.3 13.8 %forward_far.1 = (f32[512,512]{1,0:T(8,128)}, f32[512,512]{1,0:T(8,128)}, bf16[2,4,128,384]{3,2,1,0:T(8,128)(2,1)}, bf16[2,4,128,384]{3,2,1,0:T(8,128)(2,1)}, bf...) custom-call(s32[2]{0:T(128)} %pad_add_fusion.place, ...), custom_call_target="tpu_custom_call" | custom-call | flops 4831838208 | bytes 17825792 | tf_op jit(solution)/shard_map/forward_far/pallas_call | solution.py:294
  146.9 2.6 collective-permute-start.11
  150.2 2.5 collective-permute-start.9
  152.7 21.4 %backward.1 = (bf16[3,4,128,384]{3,2,1,0:T(8,128)(2,1)}, bf16[3,4,128,384]{3,2,1,0:T(8,128)(2,1)}, bf16[4,128,384]{2,1,0:T(8,128)(2,1)}, bf16[4,128,384]{2,1,0:T...) custom-call(s32[2]{0:T(128)} %pad_add_fusion.place, ...), custom_call_target="tpu_custom_call" | custom-call | flops 9663676416 | bytes 31457280 | tf_op jit(solution)/shard_map/backward/pallas_call | solution.py:322
  175.1 2.8 ring_join.1
  178.0 3.2 collective-permute-start.13
  181.2 3.2 collective-permute-start.15
  184.4 20.0 %collective-permute-done.12.refs_4_.refs_3_.refs_11_ = bf16[3,4,128,384]{3,2,1,0:T(8,128)(2,1)} collective-permute-done((bf16[3,4,128,384]{3,2,1,0:T(8,128)(2,1)}, bf16[3,4,128,384]{3,2,1,0:T(8,128)(2,1)}, u32[]{:S(2)}, u32[]{:S(2)}) %collective-permute-start.12) | collective-permute-done | bytes 1179680 | tf_op jit(solution)/shard_map/ppermute | solution.py:22
  204.4 2.7 collective-permute-done.14.refs_5_.refs_8_.refs_16_
  207.1 2.8 ring_later.1
  210.0 3.2 collective-permute-start.17
  213.2 3.2 collective-permute-start.19
  216.4 2.7 collective-permute-done.16.refs_13_
  219.2 3.3 collective-permute-done.18.refs_18_
  222.5 6.0 %ring_end.1 = (bf16[4,8,2,32,384]{4,3,2,1,0:T(8,128)(2,1)}, bf16[4,8,2,32,384]{4,3,2,1,0:T(8,128)(2,1)}) custom-call(bf16[4,256,384]{2,1,0:T(8,128)(2,1)} %get-tuple-element.50.refs_0_, bf16[2,4,128,384]{3,2,1,0:T(8,128)(2,1)} %collective-permute-done.8.refs_4_.refs_1_, bf16[2,4,128,384]{3,2,1,0:T(8,128)(2,1)} %collective-permute-done.9.refs_6_.refs_2_, ...), custom_call_target="tpu_custom_call" | custom-call | bytes 12582912 | tf_op jit(solution)/shard_map/ring_end/pallas_call | solution.py:478
  228.5 29.8 %all_to_all.29.refs_0_ = bf16[32,2,32,384]{3,2,1,0:T(8,128)(2,1)} all-to-all(bf16[32,2,32,384]{3,2,1,0:T(8,128)(2,1)} %bitcast.21), channel_id=1, replica_groups=mesh['z'=4,'core'=2,'y'=4,'x'=4] {'y','z','core'}, dimensions={0} | all-to-all | bytes 3145728 | tf_op jit(solution)/shard_map/all_to_all | solution.py:546
  258.3 4.8 %all-to-all-start.3 = ((bf16[32,2,32,384]{3,2,1,0:T(8,128)(2,1)}), bf16[32,2,32,384]{3,2,1,0:T(8,128)(2,1)}, u32[]{:S(2)}, u32[]{:S(2)}) async-start(bf16[32,2,32,384]{3,2,1,0:T(8,128)(2,1)} %bitcast.10), calls=%async_computation.3 | async-start | bytes 3145728 | tf_op jit(solution)/shard_map/all_to_all | solution.py:546
  263.9 22.3 %all-to-all-done.3.refs_1_ = bf16[32,2,32,384]{3,2,1,0:T(8,128)(2,1)} async-done(((bf16[32,2,32,384]{3,2,1,0:T(8,128)(2,1)}), bf16[32,2,32,384]{3,2,1,0:T(8,128)(2,1)}, u32[]{:S(2)}, u32[]{:S(2)}) %all-to-all-start.3) | async-done | bytes 1572896 | tf_op jit(solution)/shard_map/all_to_all | solution.py:546
  286.2 4.4 %combine.1 = bf16[16,2,128,384]{3,2,1,0:T(8,128)(2,1)} custom-call(s32[128,2]{1,0:T(8,128)} %get-tuple-element.42.target, f32[128,2]{1,0:T(8,128)} %copy.16.weights, bf16[32,2,32,384]{3,2,1,0:T(8,128)(2,1)} %all_to_all.29.refs_0_, bf16[32,2,32,384]{3,2,1,0:T(8,128)(2,1)} %all-to-all-done.3.refs_1_), custom_call_target="tpu_custom_call" | custom-call | flops 805306368 | bytes 6291456 | tf_op jit(solution)/shard_map/combine/pallas_call | solution.py:368
  290.6 44.3 %all_to_all.30.slices = bf16[16,2,128,384]{3,2,1,0:T(8,128)(2,1)} all-to-all(bf16[16,2,128,384]{3,2,1,0:T(8,128)(2,1)} %combine.1), channel_id=1, replica_groups=mesh['z'=4,'core'=2,'y'=4,'x'=4] {'x','y'}, dimensions={0} | all-to-all | bytes 6291456 | tf_op jit(solution)/shard_map/all_to_all | solution.py:548
  335.0 96.7 %assemble.1 = (bf16[128,6144]{1,0:T(8,128)(2,1)}, bf16[128,6144]{1,0:T(8,128)(2,1)}) custom-call(bf16[16,2,128,384]{3,2,1,0:T(8,128)(2,1)} %all_to_all.30.slices), custom_call_target="tpu_custom_call" | custom-call | bytes 6291456 | tf_op jit(solution)/shard_map/assemble/pallas_call | solution.py:506
  (58 shorter events, 17.3 us)
Async XLA Ops:
  6.6 5.5 %copy-start.7 = (s32[128,2]{1,0:T(8,128)S(1)}, s32[128,2]{1,0:T(8,128)}, u32[]{:S(2)}) copy-start(s32[128,2]{1,0:T(8,128)} %get-tuple-element.42.target) | copy-start | bytes 3076
  6.6 5.7 %copy-start.1 = (bf16[128,6144]{1,0:T(8,128)(2,1)S(1)}, bf16[128,6144]{1,0:T(8,128)(2,1)}, u32[]{:S(2)}) copy-start(bf16[128,6144]{1,0:T(8,128)(2,1)} %param.10) | copy-start | bytes 4718596
  6.6 27.1 %all-to-all-start = ((bf16[8,2,32,1536]{3,2,1,0:T(8,128)(2,1)}), bf16[8,2,32,1536]{3,2,1,0:T(8,128)(2,1)S(1)}, u32[]{:S(2)}, u32[]{:S(2)}) async-start(bf16[8,2,32,1536]{3,2,1,0:T(8,128)(2,1)} %get-tuple-element.43), calls=%async_computation | async-start | bytes 3145728 | tf_op jit(solution)/shard_map/all_to_all | solution.py:527
  33.7 119.0 %all-to-all-start.1 = ((bf16[8,64,6144]{2,1,0:T(8,128)(2,1)}), bf16[8,64,6144]{2,1,0:T(8,128)(2,1)}, u32[]{:S(2)}, u32[]{:S(2)}) async-start(bf16[8,64,6144]{2,1,0:T(8,128)(2,1)} %bitcast.12), calls=%async_computation.1 | async-start | bytes 12582912 | tf_op jit(solution)/shard_map/all_to_all | solution.py:527
  38.6 22.4 %copy-start.3 = (bf16[8,1,32,1536]{3,2,1,0:T(8,128)(2,1)}, bf16[8,1,32,1536]{3,2,1,0:T(8,128)(2,1)S(1)}, u32[]{:S(2)}) copy-start(bf16[8,1,32,1536]{3,2,1,0:T(8,128)(2,1)S(1)} %get-tuple-element.85) | copy-start | bytes 2359300
  38.7 72.9 %copy-start.2 = (bf16[8,1,32,1536]{3,2,1,0:T(8,128)(2,1)}, bf16[8,1,32,1536]{3,2,1,0:T(8,128)(2,1)S(1)}, u32[]{:S(2)}) copy-start(bf16[8,1,32,1536]{3,2,1,0:T(8,128)(2,1)S(1)} %get-tuple-element.84) | copy-start | bytes 2359300
  38.7 21.1 %collective-permute-start = (bf16[256,1536]{1,0:T(8,128)(2,1)S(1)}, bf16[256,1536]{1,0:T(8,128)(2,1)S(1)}, u32[]{:S(2)}, u32[]{:S(2)}) collective-permute-start(bf16[256,1536]{1,0:T(8,128)(2,1)S(1)} %bitcast.25), channel_id=1, source_target_pairs={{0,1},{1,2},{2,3},{3,0},{4,5},{5,6},{6,7},{7,4},{8,9},{9,10},{10,1... | collective-permute-start | bytes 2359304 | tf_op jit(solution)/shard_map/ppermute | solution.py:22
  40.2 20.8 %collective-permute-start.1 = (bf16[256,1536]{1,0:T(8,128)(2,1)S(1)}, bf16[256,1536]{1,0:T(8,128)(2,1)S(1)}, u32[]{:S(2)}, u32[]{:S(2)}) collective-permute-start(bf16[256,1536]{1,0:T(8,128)(2,1)S(1)} %bitcast.22), channel_id=1, source_target_pairs={{0,4},{4,8},{8,12},{12,0},{1,5},{5,9},{9,13},{13,1},{2,6},{6,10},{... | collective-permute-start | bytes 2359304 | tf_op jit(solution)/shard_map/ppermute | solution.py:22
  41.8 19.2 %collective-permute-start.2 = (bf16[256,1536]{1,0:T(8,128)(2,1)S(1)}, bf16[256,1536]{1,0:T(8,128)(2,1)S(1)}, u32[]{:S(2)}, u32[]{:S(2)}) collective-permute-start(bf16[256,1536]{1,0:T(8,128)(2,1)S(1)} %bitcast.26), channel_id=1, source_target_pairs={{0,3},{1,0},{2,1},{3,2},{4,7},{5,4},{6,5},{7,6},{8,11},{9,8},{10,9... | collective-permute-start | bytes 2359304 | tf_op jit(solution)/shard_map/ppermute | solution.py:22
  43.6 19.2 %collective-permute-start.3 = (bf16[256,1536]{1,0:T(8,128)(2,1)S(1)}, bf16[256,1536]{1,0:T(8,128)(2,1)}, u32[]{:S(2)}, u32[]{:S(2)}) collective-permute-start(bf16[256,1536]{1,0:T(8,128)(2,1)S(1)} %bitcast.23), channel_id=1, source_target_pairs={{0,12},{4,0},{8,4},{12,8},{1,13},{5,1},{9,5},{13,9},{2,14},{6,2},{... | collective-permute-start | bytes 2359304 | tf_op jit(solution)/shard_map/ppermute | solution.py:22
  59.8 1.3 copy-start.4
  111.6 19.8 %collective-permute-start.4 = (bf16[128,1536]{1,0:T(8,128)(2,1)}, bf16[128,1536]{1,0:T(8,128)(2,1)S(1)}, u32[]{:S(2)}, u32[]{:S(2)}) collective-permute-start(bf16[128,1536]{1,0:T(8,128)(2,1)} %get-tuple-element.44), channel_id=1, source_target_pairs={{0,1},{1,2},{2,3},{3,0},{4,5},{5,6},{6,7},{7,4},{8,9},{9,10},{10,1... | collective-permute-start | bytes 1179656 | tf_op jit(solution)/shard_map/ppermute | solution.py:22
  113.2 18.3 %collective-permute-start.5 = (bf16[128,1536]{1,0:T(8,128)(2,1)}, bf16[128,1536]{1,0:T(8,128)(2,1)S(1)}, u32[]{:S(2)}, u32[]{:S(2)}) collective-permute-start(bf16[128,1536]{1,0:T(8,128)(2,1)} %get-tuple-element.45), channel_id=1, source_target_pairs={{0,3},{1,0},{2,1},{3,2},{4,7},{5,4},{6,5},{7,6},{8,11},{9,8},{10,9... | collective-permute-start | bytes 1179656 | tf_op jit(solution)/shard_map/ppermute | solution.py:22
  114.9 16.6 %collective-permute-start.6 = (bf16[128,1536]{1,0:T(8,128)(2,1)}, bf16[128,1536]{1,0:T(8,128)(2,1)}, u32[]{:S(2)}, u32[]{:S(2)}) collective-permute-start(bf16[128,1536]{1,0:T(8,128)(2,1)} %get-tuple-element.46), channel_id=1, source_target_pairs={{0,4},{4,8},{8,12},{12,0},{1,5},{5,9},{9,13},{13,1},{2,6},{6,10},{... | collective-permute-start | bytes 1179656 | tf_op jit(solution)/shard_map/ppermute | solution.py:22
  116.3 15.2 %collective-permute-start.7 = (bf16[128,1536]{1,0:T(8,128)(2,1)}, bf16[128,1536]{1,0:T(8,128)(2,1)}, u32[]{:S(2)}, u32[]{:S(2)}) collective-permute-start(bf16[128,1536]{1,0:T(8,128)(2,1)} %get-tuple-element.47), channel_id=1, source_target_pairs={{0,12},{4,0},{8,4},{12,8},{1,13},{5,1},{9,5},{13,9},{2,14},{6,2},{... | collective-permute-start | bytes 1179656 | tf_op jit(solution)/shard_map/ppermute | solution.py:22
  146.2 28.0 %collective-permute-start.10 = (bf16[2,4,128,384]{3,2,1,0:T(8,128)(2,1)}, bf16[2,4,128,384]{3,2,1,0:T(8,128)(2,1)S(1)}, u32[]{:S(2)}, u32[]{:S(2)}) collective-permute-start(bf16[2,4,128,384]{3,2,1,0:T(8,128)(2,1)} %get-tuple-element.57), channel_id=1, source_target_pairs={{0,4},{4,8},{8,12},{12,0},{1,5},{5,9},{9,13},{13,1},{2,6},{6,10},{... | collective-permute-start | bytes 2359304 | tf_op jit(solution)/shard_map/ppermute | solution.py:22
  146.9 27.3 %collective-permute-start.11 = (bf16[2,4,128,384]{3,2,1,0:T(8,128)(2,1)}, bf16[2,4,128,384]{3,2,1,0:T(8,128)(2,1)}, u32[]{:S(2)}, u32[]{:S(2)}) collective-permute-start(bf16[2,4,128,384]{3,2,1,0:T(8,128)(2,1)} %get-tuple-element.58), channel_id=1, source_target_pairs={{0,12},{4,0},{8,4},{12,8},{1,13},{5,1},{9,5},{13,9},{2,14},{6,2},{... | collective-permute-start | bytes 2359304 | tf_op jit(solution)/shard_map/ppermute | solution.py:22
  149.5 24.7 %collective-permute-start.8 = (bf16[2,4,128,384]{3,2,1,0:T(8,128)(2,1)}, bf16[2,4,128,384]{3,2,1,0:T(8,128)(2,1)}, u32[]{:S(2)}, u32[]{:S(2)}) collective-permute-start(bf16[2,4,128,384]{3,2,1,0:T(8,128)(2,1)} %get-tuple-element.51), channel_id=1, source_target_pairs={{0,1},{1,2},{2,3},{3,0},{4,5},{5,6},{6,7},{7,4},{8,9},{9,10},{10,1... | collective-permute-start | bytes 2359304 | tf_op jit(solution)/shard_map/ppermute | solution.py:22
  150.2 24.0 %collective-permute-start.9 = (bf16[2,4,128,384]{3,2,1,0:T(8,128)(2,1)}, bf16[2,4,128,384]{3,2,1,0:T(8,128)(2,1)}, u32[]{:S(2)}, u32[]{:S(2)}) collective-permute-start(bf16[2,4,128,384]{3,2,1,0:T(8,128)(2,1)} %get-tuple-element.52), channel_id=1, source_target_pairs={{0,3},{1,0},{2,1},{3,2},{4,7},{5,4},{6,5},{7,6},{8,11},{9,8},{10,9... | collective-permute-start | bytes 2359304 | tf_op jit(solution)/shard_map/ppermute | solution.py:22
  174.2 0.9 copy-start
  177.9 26.5 %collective-permute-start.12 = (bf16[3,4,128,384]{3,2,1,0:T(8,128)(2,1)}, bf16[3,4,128,384]{3,2,1,0:T(8,128)(2,1)}, u32[]{:S(2)}, u32[]{:S(2)}) collective-permute-start(bf16[3,4,128,384]{3,2,1,0:T(8,128)(2,1)} %get-tuple-element.65), channel_id=1, source_target_pairs={{0,1},{1,2},{2,3},{3,0},{4,5},{5,6},{6,7},{7,4},{8,9},{9,10},{10,1... | collective-permute-start | bytes 3538952 | tf_op jit(solution)/shard_map/ppermute | solution.py:22
  178.0 26.5 %collective-permute-start.13 = (bf16[3,4,128,384]{3,2,1,0:T(8,128)(2,1)}, bf16[3,4,128,384]{3,2,1,0:T(8,128)(2,1)}, u32[]{:S(2)}, u32[]{:S(2)}) collective-permute-start(bf16[3,4,128,384]{3,2,1,0:T(8,128)(2,1)} %get-tuple-element.66), channel_id=1, source_target_pairs={{0,3},{1,0},{2,1},{3,2},{4,7},{5,4},{6,5},{7,6},{8,11},{9,8},{10,9... | collective-permute-start | bytes 3538952 | tf_op jit(solution)/shard_map/ppermute | solution.py:22
  181.2 25.9 %collective-permute-start.14 = (bf16[3,4,128,384]{3,2,1,0:T(8,128)(2,1)}, bf16[3,4,128,384]{3,2,1,0:T(8,128)(2,1)}, u32[]{:S(2)}, u32[]{:S(2)}) collective-permute-start(bf16[3,4,128,384]{3,2,1,0:T(8,128)(2,1)} %get-tuple-element.68), channel_id=1, source_target_pairs={{0,4},{4,8},{8,12},{12,0},{1,5},{5,9},{9,13},{13,1},{2,6},{6,10},{... | collective-permute-start | bytes 3538952 | tf_op jit(solution)/shard_map/ppermute | solution.py:22
  181.2 25.9 %collective-permute-start.15 = (bf16[3,4,128,384]{3,2,1,0:T(8,128)(2,1)}, bf16[3,4,128,384]{3,2,1,0:T(8,128)(2,1)}, u32[]{:S(2)}, u32[]{:S(2)}) collective-permute-start(bf16[3,4,128,384]{3,2,1,0:T(8,128)(2,1)} %get-tuple-element.69), channel_id=1, source_target_pairs={{0,12},{4,0},{8,4},{12,8},{1,13},{5,1},{9,5},{13,9},{2,14},{6,2},{... | collective-permute-start | bytes 3538952 | tf_op jit(solution)/shard_map/ppermute | solution.py:22
  209.9 9.3 %collective-permute-start.16 = (bf16[4,128,384]{2,1,0:T(8,128)(2,1)}, bf16[4,128,384]{2,1,0:T(8,128)(2,1)S(1)}, u32[]{:S(2)}, u32[]{:S(2)}) collective-permute-start(bf16[4,128,384]{2,1,0:T(8,128)(2,1)} %get-tuple-element.75), channel_id=1, source_target_pairs={{0,1},{1,2},{2,3},{3,0},{4,5},{5,6},{6,7},{7,4},{8,9},{9,10},{10,1... | collective-permute-start | bytes 1179656 | tf_op jit(solution)/shard_map/ppermute | solution.py:22
  210.0 9.2 %collective-permute-start.17 = (bf16[4,128,384]{2,1,0:T(8,128)(2,1)}, bf16[4,128,384]{2,1,0:T(8,128)(2,1)S(1)}, u32[]{:S(2)}, u32[]{:S(2)}) collective-permute-start(bf16[4,128,384]{2,1,0:T(8,128)(2,1)} %get-tuple-element.76), channel_id=1, source_target_pairs={{0,3},{1,0},{2,1},{3,2},{4,7},{5,4},{6,5},{7,6},{8,11},{9,8},{10,9... | collective-permute-start | bytes 1179656 | tf_op jit(solution)/shard_map/ppermute | solution.py:22
  213.2 9.3 %collective-permute-start.18 = (bf16[4,128,384]{2,1,0:T(8,128)(2,1)}, bf16[4,128,384]{2,1,0:T(8,128)(2,1)}, u32[]{:S(2)}, u32[]{:S(2)}) collective-permute-start(bf16[4,128,384]{2,1,0:T(8,128)(2,1)} %get-tuple-element.78), channel_id=1, source_target_pairs={{0,4},{4,8},{8,12},{12,0},{1,5},{5,9},{9,13},{13,1},{2,6},{6,10},{... | collective-permute-start | bytes 1179656 | tf_op jit(solution)/shard_map/ppermute | solution.py:22
  213.2 9.3 %collective-permute-start.19 = (bf16[4,128,384]{2,1,0:T(8,128)(2,1)}, bf16[4,128,384]{2,1,0:T(8,128)(2,1)}, u32[]{:S(2)}, u32[]{:S(2)}) collective-permute-start(bf16[4,128,384]{2,1,0:T(8,128)(2,1)} %get-tuple-element.79), channel_id=1, source_target_pairs={{0,12},{4,0},{8,4},{12,8},{1,13},{5,1},{9,5},{13,9},{2,14},{6,2},{... | collective-permute-start | bytes 1179656 | tf_op jit(solution)/shard_map/ppermute | solution.py:22
  219.2 3.3 copy-start.10
  219.2 3.3 copy-start.11
  258.3 4.8 %copy-start.12 = (f32[128,2]{0,1:T(2,128)S(1)}, f32[128,2]{0,1:T(2,128)}, u32[]{:S(2)}) copy-start(f32[128,2]{0,1:T(2,128)} %param.9) | copy-start | bytes 3076
  258.3 27.9 %all-to-all-start.3 = ((bf16[32,2,32,384]{3,2,1,0:T(8,128)(2,1)}), bf16[32,2,32,384]{3,2,1,0:T(8,128)(2,1)}, u32[]{:S(2)}, u32[]{:S(2)}) async-start(bf16[32,2,32,384]{3,2,1,0:T(8,128)(2,1)} %bitcast.10), calls=%async_computation.3 | async-start | bytes 3145728 | tf_op jit(solution)/shard_map/all_to_all | solution.py:546
  (4 other events, 3.4 us)

commit v5 on v4

--- a/solution.py
+++ b/solution.py
@@ -80,7 +80,7 @@
             + [pl.BlockSpec((tokens, chunk), lambda i, place, h=h: (0, place[h])) for h in range(2)],
             out_specs=[whole(shape), whole(routes.shape)],
         ),
-        compiler_params=params(),
+        compiler_params=params(16),
         cost_estimate=cost(8 * ROWS * tokens * chunk, 8 * tokens * chunk + 4 * ROWS * chunk),
         name="dispatch",
     )(place, routes, rows, rows)
@@ -90,16 +90,8 @@
 
 
 def halves_kernel(*refs):
-    sources, ends, sems = refs[:4], refs[4:8], refs[8]
-    half = ends[0].shape[0]
-    copies = [
-        pltpu.make_async_copy(source.at[pl.ds(n // 2 * half, half)], end, sems.at[n])
-        for n, (source, end) in enumerate(zip(sources, ends))
-    ]
-    for copy in copies:
-        copy.start()
-    for copy in copies:
-        copy.wait()
+    for source, to in zip(refs[:4], refs[4:]):
+        to[...] = source[...]
 
 
 def gathered(owns):
@@ -107,13 +99,15 @@
     half = rows // 2
     befores = [shift(own, axis, 1) for own, axis in zip(owns, AXES)]
     afters = [shift(own, axis, -1) for own, axis in zip(owns, AXES)]
+    top = pl.BlockSpec((half, chunk), lambda i: (0, 0))
+    bottom = pl.BlockSpec((half, chunk), lambda i: (1, 0))
     send = pl.pallas_call(
         halves_kernel,
         out_shape=[jax.ShapeDtypeStruct((half, chunk), BF16)] * 4,
-        in_specs=[ANYWHERE] * 4,
-        out_specs=[ANYWHERE] * 4,
-        scratch_shapes=[pltpu.SemaphoreType.DMA((4,))],
-        compiler_params=params(),
+        grid=(1,),
+        in_specs=[top, top, bottom, bottom],
+        out_specs=[whole((half, chunk))] * 4,
+        compiler_params=params(58),
         cost_estimate=cost(0, 16 * half * chunk),
         name="halves",
     )(*befores, *afters)
@@ -216,7 +210,7 @@
             emit(at_step, distance, place, outs, product)
 
 
-STEPS = 4
+STEPS = 2
 
 
 def backward_kernel(place, rows, wd, to_gate, to_up, wg, wu, *refs):
@@ -283,7 +277,7 @@
             in_specs=[whole(r.shape) for r in rows] + [near_w, near_w],
             out_specs=[by_half()] * 2,
         ),
-        compiler_params=params(),
+        compiler_params=params(63),
         cost_estimate=cost(6 * ROWS * width * hid, 3 * width * ROWS + 6 * width * hid),
         name="forward_near",
     )(place, *rows, w_gate, w_up)
@@ -306,7 +300,7 @@
                 pltpu.SemaphoreType.DMA,
             ],
         ),
-        compiler_params=params(),
+        compiler_params=params(63),
         cost_estimate=cost(6 * ROWS * width * hid, 2 * width * ROWS + 4 * width * hid + 16 * ROWS * hid),
         name="forward_far",
     )(place, *rows, w_gate, w_up, gate, up, w_down)
@@ -372,7 +366,7 @@
         in_specs=[whole(target.shape), whole(weights.shape)]
         + [pl.BlockSpec((terms, 1, slots, part), lambda n: (0, n, 0, 0)) for _ in homes],
         out_specs=pl.BlockSpec((copies, 1, tokens, part), lambda n: (0, n, 0, 0)),
-        compiler_params=params(),
+        compiler_params=params(24),
         cost_estimate=cost(8 * tokens * homes[0].size, 4 * homes[0].size + 4 * copies * tokens * part),
         name="combine",
     )(target, weights, *homes)
@@ -414,16 +408,16 @@
     for n in range(2):
         for h in range(2):
             own, first_plus, first_minus, later_plus, later_minus = (r[...] for r in refs[10 * n + 5 * h : 10 * n + 5 * h + 5])
-            own = own[0]
+            total = refs[20 + h]
             first_plus, first_minus, later_plus, later_minus = (
-                r.reshape(half, r.shape[-1]) for r in (first_plus, first_minus, later_plus, later_minus)
+                r.reshape(-1, half, r.shape[-1]) for r in (first_plus, first_minus, later_plus, later_minus)
             )
-            top = add(own[:half], later_plus, first_minus)
-            bottom = add(own[half:], first_plus, later_minus)
-            total = refs[20 + h]
             shape = (GROUPS // 2, *total.shape[3:])
-            total[0, : GROUPS // 2, n] = top.reshape(shape)
-            total[0, GROUPS // 2 :, n] = bottom.reshape(shape)
+            for j in range(own.shape[0]):
+                top = add(own[j, :half], later_plus[j], first_minus[j])
+                bottom = add(own[j, half:], first_plus[j], later_minus[j])
+                total[j, : GROUPS // 2, n] = top.reshape(shape)
+                total[j, GROUPS // 2 :, n] = bottom.reshape(shape)
 
 
 def both_ways(plus, minus):
@@ -464,9 +458,9 @@
 
 def ring_end(out_parts, out_first, got, grad_parts, grad_later):
     _, rows, part = out_parts[0][4].shape
-    own = pl.BlockSpec((1, rows, part), lambda j: (j, 0, 0))
-    blocks = [pl.BlockSpec((1, 1, rows // 2, part), lambda j, n=n: (n, j, 0, 0)) for n in range(3)]
-    later = pl.BlockSpec((1, rows // 2, part), lambda j: (j, 0, 0))
+    own = pl.BlockSpec((2, rows, part), lambda j: (j, 0, 0))
+    blocks = [pl.BlockSpec((1, 2, rows // 2, part), lambda j, n=n: (n, j, 0, 0)) for n in range(3)]
+    later = pl.BlockSpec((2, rows // 2, part), lambda j: (j, 0, 0))
     operands, specs = [], []
     for h in range(2):
         operands += [out_parts[h][4], out_first[h], out_first[2 + h], got[h], got[2 + h]]
@@ -478,27 +472,20 @@
     return pl.pallas_call(
         total_kernel,
         out_shape=[jax.ShapeDtypeStruct(shape, BF16)] * 2,
-        grid=(RING,),
+        grid=(2,),
         in_specs=specs,
-        out_specs=[pl.BlockSpec((1, *shape[1:]), lambda j: (j, 0, 0, 0, 0))] * 2,
+        out_specs=[pl.BlockSpec((2, *shape[1:]), lambda j: (j, 0, 0, 0, 0))] * 2,
         compiler_params=params(),
         cost_estimate=cost(0, 32 * RING * rows * part),
         name="ring_end",
     )(*operands)
 
 
-def assemble_kernel(slices, *refs):
-    results, sems = refs[:2], refs[2]
+def assemble_kernel(slices, *results):
     count, _, _, part = slices.shape
-    copies = [
-        pltpu.make_async_copy(slices.at[c, n], result.at[:, pl.ds(c * part, part)], sems.at[c, n])
-        for c in range(count)
-        for n, result in enumerate(results)
-    ]
-    for copy in copies:
-        copy.start()
-    for copy in copies:
-        copy.wait()
+    for n, result in enumerate(results):
+        for c in range(count):
+            result[:, c * part : (c + 1) * part] = slices[c, n]
 
 
 def assemble(slices):
@@ -506,10 +493,10 @@
     return pl.pallas_call(
         assemble_kernel,
         out_shape=[jax.ShapeDtypeStruct((tokens, count * part), BF16)] * 2,
-        in_specs=[ANYWHERE],
-        out_specs=[ANYWHERE] * 2,
-        scratch_shapes=[pltpu.SemaphoreType.DMA((count, 2))],
-        compiler_params=params(),
+        grid=(2,),
+        in_specs=[pl.BlockSpec((count // 2, 2, tokens, part), lambda i: (i, 0, 0, 0))],
+        out_specs=[pl.BlockSpec((tokens, count // 2 * part), lambda i: (0, i))] * 2,
+        compiler_params=params(58),
         cost_estimate=cost(0, 4 * slices.size),
         name="assemble",
     )(slices)

time: 433 us -> 291 us (0.67)
  Pallas kernels: 214 us -> 68.8 us
  waiting for transfers between devices: 83.9 us -> 93 us
    pallas_call x1, Pallas kernels: 96.7 us -> 3.2 us  [assemble(): pl.pallas_call(assemble_kernel, out_shape=[jax.ShapeDtypeStruct((tokens,...]
    pallas_call x1, Pallas kernels: 48.8 us -> 2.53 us  [gathered(): pl.pallas_call(halves_kernel, out_shape=[jax.ShapeDtypeStruct((half, chun...]
    ppermute x20, waiting for transfers between devices: 44.6 us -> 49.6 us  [shift(): lax.ppermute(rows, axis, [(i, (i + step) % RING) for i in range(RING)])]
  transfers between devices with their start and end apart: 23 -> 23, of which waited for: 8 -> 10; matrix products, arithmetic and copies ran while one was open for 1% -> 2% of each run, Pallas kernels for 23% -> 17%
where the time goes in v5:
time: 291 us; the launch traced here: 290 us
  waiting for transfers between devices  93 us (32%)
  blocking collectives  70.8 us (24%)
  Pallas kernels  68.8 us (24%)
  starting transfers between devices  47.1 us (16%)
  local copies, waits for them, and re-layouts  5.31 us (2%)
  matrix products  4.44 us (2%)
    ppermute x20, waiting for transfers between devices, shift(): lax.ppermute(rows, axis, [(i, (i + step) % RING) for i in range(RING)])  49.6 us
    all_to_all x1, blocking collectives, per_device(): lax.all_to_all(copies, AXES, split_axis=0, concat_axis=0, tiled=True)  43.3 us
    ppermute x20, starting transfers between devices, shift(): lax.ppermute(rows, axis, [(i, (i + step) % RING) for i in range(RING)])  32.7 us
    all_to_all x1, blocking collectives, per_device(): lax.all_to_all(pieces, axes, split_axis=0, concat_axis=0, tiled=True)  27.6 us
    all_to_all x1, waiting for transfers between devices, per_device(): lax.all_to_all(pieces, axes, split_axis=0, concat_axis=0, tiled=True)  23 us
    all_to_all x2, waiting for transfers between devices, to_experts(): return lax.all_to_all(rows, EXPERT, split_axis=0, concat_axis=0, tiled=True)  20.4 us
    pallas_call x1, Pallas kernels, backward(): pl.pallas_call(backward_kernel, out_shape=shapes, grid_spec=pltpu.Prefetc...  19.7 us
    pallas_call x1, Pallas kernels, forward(): pl.pallas_call(forward_far_kernel, out_shape=[jax.ShapeDtypeStruct((2 * R...  13.9 us
  transfers between devices with their start and end apart: 23, of which 10 were waited for; matrix products, arithmetic and copies ran while one was open for 2% of the time, Pallas kernels for 17%

profile of v5, /device:TPU:0, one launch (start us, length us, event | category | flops | bytes accessed | tf_op | source)
XLA Modules:
  0.0 290.5 jit_solution(4024023220531545567)
XLA Ops:
  2.9 2.7 dispatch.1
  5.6 5.5 %all-to-all-start = ((bf16[8,2,32,1536]{3,2,1,0:T(8,128)(2,1)}), bf16[8,2,32,1536]{3,2,1,0:T(8,128)(2,1)S(1)}, u32[]{:S(2)}, u32[]{:S(2)}) async-start(bf16[8,2,32,1536]{3,2,1,0:T(8,128)(2,1)} %get-tuple-element.43), calls=%async_computation | async-start | bytes 3145728 | tf_op jit(solution)/shard_map/all_to_all | solution.py:514
  11.3 4.4 %convolution_convert_fusion = bf16[512,6144]{1,0:T(8,128)(2,1)} fusion(bf16[128,6144]{1,0:T(8,128)(2,1)S(1)} %copy-done.3, s32[128]{0:T(128)S(1)} %get-tuple-element.83, s32[128]{0:T(128)S(1)} %get-tuple-element.82), kind=kOutput, calls=%fused_computation | convolution fusion | flops 808648704 | bytes 7865344 | tf_op jit(solution)/shard_map/dot_general | solution.py:26
  15.8 17.0 %all-to-all-done = bf16[8,2,32,1536]{3,2,1,0:T(8,128)(2,1)S(1)} async-done(((bf16[8,2,32,1536]{3,2,1,0:T(8,128)(2,1)}), bf16[8,2,32,1536]{3,2,1,0:T(8,128)(2,1)S(1)}, u32[]{:S(2)}, u32[]{:S(2)}) %all-to-all-start) | async-done | bytes 1572896 | tf_op jit(solution)/shard_map/all_to_all | solution.py:514
  32.7 4.8 %all-to-all-start.1 = ((bf16[8,64,6144]{2,1,0:T(8,128)(2,1)}), bf16[8,64,6144]{2,1,0:T(8,128)(2,1)}, u32[]{:S(2)}, u32[]{:S(2)}) async-start(bf16[8,64,6144]{2,1,0:T(8,128)(2,1)} %bitcast.12), calls=%async_computation.1 | async-start | bytes 12582912 | tf_op jit(solution)/shard_map/all_to_all | solution.py:514
  40.8 1.7 collective-permute-start.2
  44.2 14.5 %collective-permute-done.refs_0_.refs_2_ = bf16[256,1536]{1,0:T(8,128)(2,1)S(1)} collective-permute-done((bf16[256,1536]{1,0:T(8,128)(2,1)S(1)}, bf16[256,1536]{1,0:T(8,128)(2,1)S(1)}, u32[]{:S(2)}, u32[]{:S(2)}) %collective-permute-start) | collective-permute-done | bytes 786464 | tf_op jit(solution)/shard_map/ppermute | solution.py:22
  62.4 2.5 halves.1
  66.2 2.1 collective-permute-start.5
  71.5 13.3 %forward_near.1 = (f32[512,512]{1,0:T(8,128)}, f32[512,512]{1,0:T(8,128)}) custom-call(s32[2]{0:T(128)} %copy-done.1, bf16[256,1536]{1,0:T(8,128)(2,1)} %bitcast.28, bf16[256,1536]{1,0:T(8,128)(2,1)} %copy-done.8, bf16[256,1536]{1,0:T(8,128)(2,1)} %copy-done.6, bf16[256,1536]{1,0:T(8,128)(2,1)} %bitcast.25, bf16[256,1536]{1,0:T(8,128)(2,1)} %copy-done.9, ...), custom_call_target="tpu_custom_call" | custom-call | flops 4831838208 | bytes 23592960 | tf_op jit(solution)/shard_map/forward_near/pallas_call | solution.py:271
  85.7 13.9 %forward_far.1 = (f32[512,512]{1,0:T(8,128)}, f32[512,512]{1,0:T(8,128)}, bf16[2,4,128,384]{3,2,1,0:T(8,128)(2,1)}, bf16[2,4,128,384]{3,2,1,0:T(8,128)(2,1)}, bf...) custom-call(s32[2]{0:T(128)} %copy-done.1, ...), custom_call_target="tpu_custom_call" | custom-call | flops 4831838208 | bytes 17825792 | tf_op jit(solution)/shard_map/forward_far/pallas_call | solution.py:288
  100.5 2.4 collective-permute-start.11
  103.3 2.9 collective-permute-start.9
  106.2 3.5 %all-to-all-done.1 = bf16[8,64,6144]{2,1,0:T(8,128)(2,1)} async-done(((bf16[8,64,6144]{2,1,0:T(8,128)(2,1)}), bf16[8,64,6144]{2,1,0:T(8,128)(2,1)}, u32[]{:S(2)}, u32[]{:S(2)}) %all-to-all-start.1) | async-done | bytes 6291488 | tf_op jit(solution)/shard_map/all_to_all | solution.py:514
  109.6 19.7 %backward.1 = (bf16[3,4,128,384]{3,2,1,0:T(8,128)(2,1)}, bf16[3,4,128,384]{3,2,1,0:T(8,128)(2,1)}, bf16[4,128,384]{2,1,0:T(8,128)(2,1)}, bf16[4,128,384]{2,1,0:T...) custom-call(s32[2]{0:T(128)} %copy-done.1, ...), custom_call_target="tpu_custom_call" | custom-call | flops 9663676416 | bytes 31457280 | tf_op jit(solution)/shard_map/backward/pallas_call | solution.py:316
  130.3 2.8 ring_join.1
  134.6 1.7 collective-permute-start.13
  138.0 1.7 collective-permute-start.15
  139.6 22.6 %collective-permute-done.12.refs_4_.refs_3_.refs_11_ = bf16[3,4,128,384]{3,2,1,0:T(8,128)(2,1)} collective-permute-done((bf16[3,4,128,384]{3,2,1,0:T(8,128)(2,1)}, bf16[3,4,128,384]{3,2,1,0:T(8,128)(2,1)}, u32[]{:S(2)}, u32[]{:S(2)}) %collective-permute-start.12) | collective-permute-done | bytes 1179680 | tf_op jit(solution)/shard_map/ppermute | solution.py:22
  162.2 2.7 collective-permute-done.14.refs_5_.refs_8_.refs_16_
  165.0 2.8 ring_later.1
  168.1 3.0 %collective-permute-start.17 = (bf16[4,128,384]{2,1,0:T(8,128)(2,1)}, bf16[4,128,384]{2,1,0:T(8,128)(2,1)S(1)}, u32[]{:S(2)}, u32[]{:S(2)}) collective-permute-start(bf16[4,128,384]{2,1,0:T(8,128)(2,1)} %get-tuple-element.76), channel_id=1, source_target_pairs={{0,3},{1,0},{2,1},{3,2},{4,7},{5,4},{6,5},{7,6},{8,11},{9,8},{10,9... | collective-permute-start | bytes 1179656 | tf_op jit(solution)/shard_map/ppermute | solution.py:22
  172.6 1.7 collective-permute-start.19
  174.3 4.2 %collective-permute-done.16.refs_13_ = bf16[4,128,384]{2,1,0:T(8,128)(2,1)S(1)} collective-permute-done((bf16[4,128,384]{2,1,0:T(8,128)(2,1)}, bf16[4,128,384]{2,1,0:T(8,128)(2,1)S(1)}, u32[]{:S(2)}, u32[]{:S(2)}) %collective-permute-start.16) | collective-permute-done | bytes 393248 | tf_op jit(solution)/shard_map/ppermute | solution.py:22
  178.4 2.8 collective-permute-done.18.refs_18_
  181.2 5.4 %ring_end.1 = (bf16[4,8,2,32,384]{4,3,2,1,0:T(8,128)(2,1)}, bf16[4,8,2,32,384]{4,3,2,1,0:T(8,128)(2,1)}) custom-call(bf16[4,256,384]{2,1,0:T(8,128)(2,1)} %get-tuple-element.50.refs_0_, bf16[2,4,128,384]{3,2,1,0:T(8,128)(2,1)} %collective-permute-done.8.refs_4_.refs_1_, bf16[2,4,128,384]{3,2,1,0:T(8,128)(2,1)} %collective-permute-done.9.refs_6_.refs_2_, ...), custom_call_target="tpu_custom_call" | custom-call | bytes 12582912 | tf_op jit(solution)/shard_map/ring_end/pallas_call | solution.py:472
  186.7 27.6 %all_to_all.29.refs_0_ = bf16[32,2,32,384]{3,2,1,0:T(8,128)(2,1)S(1)} all-to-all(bf16[32,2,32,384]{3,2,1,0:T(8,128)(2,1)} %bitcast.22), channel_id=1, replica_groups=mesh['z'=4,'core'=2,'y'=4,'x'=4] {'y','z','core'}, dimensions={0} | all-to-all | bytes 3145728 | tf_op jit(solution)/shard_map/all_to_all | solution.py:533
  214.2 4.1 %all-to-all-start.3 = ((bf16[32,2,32,384]{3,2,1,0:T(8,128)(2,1)}), bf16[32,2,32,384]{3,2,1,0:T(8,128)(2,1)S(1)}, u32[]{:S(2)}, u32[]{:S(2)}) async-start(bf16[32,2,32,384]{3,2,1,0:T(8,128)(2,1)} %bitcast.21), calls=%async_computation.3 | async-start | bytes 3145728 | tf_op jit(solution)/shard_map/all_to_all | solution.py:533
  218.5 23.0 %all-to-all-done.3.refs_1_ = bf16[32,2,32,384]{3,2,1,0:T(8,128)(2,1)S(1)} async-done(((bf16[32,2,32,384]{3,2,1,0:T(8,128)(2,1)}), bf16[32,2,32,384]{3,2,1,0:T(8,128)(2,1)S(1)}, u32[]{:S(2)}, u32[]{:S(2)}) %all-to-all-start.3) | async-done | bytes 1572896 | tf_op jit(solution)/shard_map/all_to_all | solution.py:533
  241.5 2.6 combine.1
  244.0 43.3 %all_to_all.30.slices = bf16[16,2,128,384]{3,2,1,0:T(8,128)(2,1)} all-to-all(bf16[16,2,128,384]{3,2,1,0:T(8,128)(2,1)S(1)} %combine.1), channel_id=1, replica_groups=mesh['z'=4,'core'=2,'y'=4,'x'=4] {'x','y'}, dimensions={0} | all-to-all | bytes 6291456 | tf_op jit(solution)/shard_map/all_to_all | solution.py:535
  287.3 3.2 %assemble.1 = (bf16[128,6144]{1,0:T(8,128)(2,1)}, bf16[128,6144]{1,0:T(8,128)(2,1)}) custom-call(bf16[16,2,128,384]{3,2,1,0:T(8,128)(2,1)} %all_to_all.30.slices), custom_call_target="tpu_custom_call" | custom-call | bytes 6291456 | tf_op jit(solution)/shard_map/assemble/pallas_call | solution.py:493
  (62 shorter events, 23.7 us)
Async XLA Ops:
  2.9 2.7 copy-start.1
  5.6 5.7 %copy-start.3 = (bf16[128,6144]{1,0:T(8,128)(2,1)S(1)}, bf16[128,6144]{1,0:T(8,128)(2,1)}, u32[]{:S(2)}) copy-start(bf16[128,6144]{1,0:T(8,128)(2,1)} %param.10) | copy-start | bytes 4718596
  5.6 27.1 %all-to-all-start = ((bf16[8,2,32,1536]{3,2,1,0:T(8,128)(2,1)}), bf16[8,2,32,1536]{3,2,1,0:T(8,128)(2,1)S(1)}, u32[]{:S(2)}, u32[]{:S(2)}) async-start(bf16[8,2,32,1536]{3,2,1,0:T(8,128)(2,1)} %get-tuple-element.43), calls=%async_computation | async-start | bytes 3145728 | tf_op jit(solution)/shard_map/all_to_all | solution.py:514
  32.7 76.9 %all-to-all-start.1 = ((bf16[8,64,6144]{2,1,0:T(8,128)(2,1)}), bf16[8,64,6144]{2,1,0:T(8,128)(2,1)}, u32[]{:S(2)}, u32[]{:S(2)}) async-start(bf16[8,64,6144]{2,1,0:T(8,128)(2,1)} %bitcast.12), calls=%async_computation.1 | async-start | bytes 12582912 | tf_op jit(solution)/shard_map/all_to_all | solution.py:514
  37.6 27.3 %copy-start.4 = (bf16[8,1,32,1536]{3,2,1,0:T(8,128)(2,1)}, bf16[8,1,32,1536]{3,2,1,0:T(8,128)(2,1)S(1)}, u32[]{:S(2)}) copy-start(bf16[8,1,32,1536]{3,2,1,0:T(8,128)(2,1)S(1)} %get-tuple-element.84) | copy-start | bytes 2359300
  37.6 27.3 %copy-start.5 = (bf16[8,1,32,1536]{3,2,1,0:T(8,128)(2,1)}, bf16[8,1,32,1536]{3,2,1,0:T(8,128)(2,1)S(1)}, u32[]{:S(2)}) copy-start(bf16[8,1,32,1536]{3,2,1,0:T(8,128)(2,1)S(1)} %get-tuple-element.85) | copy-start | bytes 2359300
  37.6 21.1 %collective-permute-start = (bf16[256,1536]{1,0:T(8,128)(2,1)S(1)}, bf16[256,1536]{1,0:T(8,128)(2,1)S(1)}, u32[]{:S(2)}, u32[]{:S(2)}) collective-permute-start(bf16[256,1536]{1,0:T(8,128)(2,1)S(1)} %bitcast.26), channel_id=1, source_target_pairs={{0,1},{1,2},{2,3},{3,0},{4,5},{5,6},{6,7},{7,4},{8,9},{9,10},{10,1... | collective-permute-start | bytes 2359304 | tf_op jit(solution)/shard_map/ppermute | solution.py:22
  39.2 20.8 %collective-permute-start.1 = (bf16[256,1536]{1,0:T(8,128)(2,1)S(1)}, bf16[256,1536]{1,0:T(8,128)(2,1)S(1)}, u32[]{:S(2)}, u32[]{:S(2)}) collective-permute-start(bf16[256,1536]{1,0:T(8,128)(2,1)S(1)} %bitcast.23), channel_id=1, source_target_pairs={{0,4},{4,8},{8,12},{12,0},{1,5},{5,9},{9,13},{13,1},{2,6},{6,10},{... | collective-permute-start | bytes 2359304 | tf_op jit(solution)/shard_map/ppermute | solution.py:22
  40.8 19.2 %collective-permute-start.2 = (bf16[256,1536]{1,0:T(8,128)(2,1)S(1)}, bf16[256,1536]{1,0:T(8,128)(2,1)S(1)}, u32[]{:S(2)}, u32[]{:S(2)}) collective-permute-start(bf16[256,1536]{1,0:T(8,128)(2,1)S(1)} %bitcast.27), channel_id=1, source_target_pairs={{0,3},{1,0},{2,1},{3,2},{4,7},{5,4},{6,5},{7,6},{8,11},{9,8},{10,9... | collective-permute-start | bytes 2359304 | tf_op jit(solution)/shard_map/ppermute | solution.py:22
  42.5 19.0 %collective-permute-start.3 = (bf16[256,1536]{1,0:T(8,128)(2,1)S(1)}, bf16[256,1536]{1,0:T(8,128)(2,1)S(1)}, u32[]{:S(2)}, u32[]{:S(2)}) collective-permute-start(bf16[256,1536]{1,0:T(8,128)(2,1)S(1)} %bitcast.24), channel_id=1, source_target_pairs={{0,12},{4,0},{8,4},{12,8},{1,13},{5,1},{9,5},{13,9},{2,14},{6,2},{... | collective-permute-start | bytes 2359304 | tf_op jit(solution)/shard_map/ppermute | solution.py:22
  58.8 2.8 copy-start.6
  60.0 1.5 copy-start.7
  65.0 19.8 %collective-permute-start.4 = (bf16[128,1536]{1,0:T(8,128)(2,1)}, bf16[128,1536]{1,0:T(8,128)(2,1)S(1)}, u32[]{:S(2)}, u32[]{:S(2)}) collective-permute-start(bf16[128,1536]{1,0:T(8,128)(2,1)} %get-tuple-element.44), channel_id=1, source_target_pairs={{0,1},{1,2},{2,3},{3,0},{4,5},{5,6},{6,7},{7,4},{8,9},{9,10},{10,1... | collective-permute-start | bytes 1179656 | tf_op jit(solution)/shard_map/ppermute | solution.py:22
  66.2 18.7 %collective-permute-start.5 = (bf16[128,1536]{1,0:T(8,128)(2,1)}, bf16[128,1536]{1,0:T(8,128)(2,1)S(1)}, u32[]{:S(2)}, u32[]{:S(2)}) collective-permute-start(bf16[128,1536]{1,0:T(8,128)(2,1)} %get-tuple-element.45), channel_id=1, source_target_pairs={{0,3},{1,0},{2,1},{3,2},{4,7},{5,4},{6,5},{7,6},{8,11},{9,8},{10,9... | collective-permute-start | bytes 1179656 | tf_op jit(solution)/shard_map/ppermute | solution.py:22
  68.3 16.6 %collective-permute-start.6 = (bf16[128,1536]{1,0:T(8,128)(2,1)}, bf16[128,1536]{1,0:T(8,128)(2,1)}, u32[]{:S(2)}, u32[]{:S(2)}) collective-permute-start(bf16[128,1536]{1,0:T(8,128)(2,1)} %get-tuple-element.46), channel_id=1, source_target_pairs={{0,4},{4,8},{8,12},{12,0},{1,5},{5,9},{9,13},{13,1},{2,6},{6,10},{... | collective-permute-start | bytes 1179656 | tf_op jit(solution)/shard_map/ppermute | solution.py:22
  69.9 15.0 %collective-permute-start.7 = (bf16[128,1536]{1,0:T(8,128)(2,1)}, bf16[128,1536]{1,0:T(8,128)(2,1)}, u32[]{:S(2)}, u32[]{:S(2)}) collective-permute-start(bf16[128,1536]{1,0:T(8,128)(2,1)} %get-tuple-element.47), channel_id=1, source_target_pairs={{0,12},{4,0},{8,4},{12,8},{1,13},{5,1},{9,5},{13,9},{2,14},{6,2},{... | collective-permute-start | bytes 1179656 | tf_op jit(solution)/shard_map/ppermute | solution.py:22
  99.6 29.7 %collective-permute-start.10 = (bf16[2,4,128,384]{3,2,1,0:T(8,128)(2,1)}, bf16[2,4,128,384]{3,2,1,0:T(8,128)(2,1)S(1)}, u32[]{:S(2)}, u32[]{:S(2)}) collective-permute-start(bf16[2,4,128,384]{3,2,1,0:T(8,128)(2,1)} %get-tuple-element.57), channel_id=1, source_target_pairs={{0,4},{4,8},{8,12},{12,0},{1,5},{5,9},{9,13},{13,1},{2,6},{6,10},{... | collective-permute-start | bytes 2359304 | tf_op jit(solution)/shard_map/ppermute | solution.py:22
  100.5 28.8 %collective-permute-start.11 = (bf16[2,4,128,384]{3,2,1,0:T(8,128)(2,1)}, bf16[2,4,128,384]{3,2,1,0:T(8,128)(2,1)}, u32[]{:S(2)}, u32[]{:S(2)}) collective-permute-start(bf16[2,4,128,384]{3,2,1,0:T(8,128)(2,1)} %get-tuple-element.58), channel_id=1, source_target_pairs={{0,12},{4,0},{8,4},{12,8},{1,13},{5,1},{9,5},{13,9},{2,14},{6,2},{... | collective-permute-start | bytes 2359304 | tf_op jit(solution)/shard_map/ppermute | solution.py:22
  102.9 26.4 %collective-permute-start.8 = (bf16[2,4,128,384]{3,2,1,0:T(8,128)(2,1)}, bf16[2,4,128,384]{3,2,1,0:T(8,128)(2,1)}, u32[]{:S(2)}, u32[]{:S(2)}) collective-permute-start(bf16[2,4,128,384]{3,2,1,0:T(8,128)(2,1)} %get-tuple-element.51), channel_id=1, source_target_pairs={{0,1},{1,2},{2,3},{3,0},{4,5},{5,6},{6,7},{7,4},{8,9},{9,10},{10,1... | collective-permute-start | bytes 2359304 | tf_op jit(solution)/shard_map/ppermute | solution.py:22
  103.3 26.1 %collective-permute-start.9 = (bf16[2,4,128,384]{3,2,1,0:T(8,128)(2,1)}, bf16[2,4,128,384]{3,2,1,0:T(8,128)(2,1)}, u32[]{:S(2)}, u32[]{:S(2)}) collective-permute-start(bf16[2,4,128,384]{3,2,1,0:T(8,128)(2,1)} %get-tuple-element.52), channel_id=1, source_target_pairs={{0,3},{1,0},{2,1},{3,2},{4,7},{5,4},{6,5},{7,6},{8,11},{9,8},{10,9... | collective-permute-start | bytes 2359304 | tf_op jit(solution)/shard_map/ppermute | solution.py:22
  133.1 29.1 %collective-permute-start.12 = (bf16[3,4,128,384]{3,2,1,0:T(8,128)(2,1)}, bf16[3,4,128,384]{3,2,1,0:T(8,128)(2,1)}, u32[]{:S(2)}, u32[]{:S(2)}) collective-permute-start(bf16[3,4,128,384]{3,2,1,0:T(8,128)(2,1)} %get-tuple-element.65), channel_id=1, source_target_pairs={{0,1},{1,2},{2,3},{3,0},{4,5},{5,6},{6,7},{7,4},{8,9},{9,10},{10,1... | collective-permute-start | bytes 3538952 | tf_op jit(solution)/shard_map/ppermute | solution.py:22
  134.6 27.5 %collective-permute-start.13 = (bf16[3,4,128,384]{3,2,1,0:T(8,128)(2,1)}, bf16[3,4,128,384]{3,2,1,0:T(8,128)(2,1)}, u32[]{:S(2)}, u32[]{:S(2)}) collective-permute-start(bf16[3,4,128,384]{3,2,1,0:T(8,128)(2,1)} %get-tuple-element.66), channel_id=1, source_target_pairs={{0,3},{1,0},{2,1},{3,2},{4,7},{5,4},{6,5},{7,6},{8,11},{9,8},{10,9... | collective-permute-start | bytes 3538952 | tf_op jit(solution)/shard_map/ppermute | solution.py:22
  136.4 28.5 %collective-permute-start.14 = (bf16[3,4,128,384]{3,2,1,0:T(8,128)(2,1)}, bf16[3,4,128,384]{3,2,1,0:T(8,128)(2,1)}, u32[]{:S(2)}, u32[]{:S(2)}) collective-permute-start(bf16[3,4,128,384]{3,2,1,0:T(8,128)(2,1)} %get-tuple-element.68), channel_id=1, source_target_pairs={{0,4},{4,8},{8,12},{12,0},{1,5},{5,9},{9,13},{13,1},{2,6},{6,10},{... | collective-permute-start | bytes 3538952 | tf_op jit(solution)/shard_map/ppermute | solution.py:22
  138.0 27.0 %collective-permute-start.15 = (bf16[3,4,128,384]{3,2,1,0:T(8,128)(2,1)}, bf16[3,4,128,384]{3,2,1,0:T(8,128)(2,1)}, u32[]{:S(2)}, u32[]{:S(2)}) collective-permute-start(bf16[3,4,128,384]{3,2,1,0:T(8,128)(2,1)} %get-tuple-element.69), channel_id=1, source_target_pairs={{0,12},{4,0},{8,4},{12,8},{1,13},{5,1},{9,5},{13,9},{2,14},{6,2},{... | collective-permute-start | bytes 3538952 | tf_op jit(solution)/shard_map/ppermute | solution.py:22
  167.7 10.7 %collective-permute-start.16 = (bf16[4,128,384]{2,1,0:T(8,128)(2,1)}, bf16[4,128,384]{2,1,0:T(8,128)(2,1)S(1)}, u32[]{:S(2)}, u32[]{:S(2)}) collective-permute-start(bf16[4,128,384]{2,1,0:T(8,128)(2,1)} %get-tuple-element.75), channel_id=1, source_target_pairs={{0,1},{1,2},{2,3},{3,0},{4,5},{5,6},{6,7},{7,4},{8,9},{9,10},{10,1... | collective-permute-start | bytes 1179656 | tf_op jit(solution)/shard_map/ppermute | solution.py:22
  168.1 10.4 %collective-permute-start.17 = (bf16[4,128,384]{2,1,0:T(8,128)(2,1)}, bf16[4,128,384]{2,1,0:T(8,128)(2,1)S(1)}, u32[]{:S(2)}, u32[]{:S(2)}) collective-permute-start(bf16[4,128,384]{2,1,0:T(8,128)(2,1)} %get-tuple-element.76), channel_id=1, source_target_pairs={{0,3},{1,0},{2,1},{3,2},{4,7},{5,4},{6,5},{7,6},{8,11},{9,8},{10,9... | collective-permute-start | bytes 1179656 | tf_op jit(solution)/shard_map/ppermute | solution.py:22
  171.0 10.2 %collective-permute-start.18 = (bf16[4,128,384]{2,1,0:T(8,128)(2,1)}, bf16[4,128,384]{2,1,0:T(8,128)(2,1)}, u32[]{:S(2)}, u32[]{:S(2)}) collective-permute-start(bf16[4,128,384]{2,1,0:T(8,128)(2,1)} %get-tuple-element.78), channel_id=1, source_target_pairs={{0,4},{4,8},{8,12},{12,0},{1,5},{5,9},{9,13},{13,1},{2,6},{6,10},{... | collective-permute-start | bytes 1179656 | tf_op jit(solution)/shard_map/ppermute | solution.py:22
  172.6 8.6 %collective-permute-start.19 = (bf16[4,128,384]{2,1,0:T(8,128)(2,1)}, bf16[4,128,384]{2,1,0:T(8,128)(2,1)}, u32[]{:S(2)}, u32[]{:S(2)}) collective-permute-start(bf16[4,128,384]{2,1,0:T(8,128)(2,1)} %get-tuple-element.79), channel_id=1, source_target_pairs={{0,12},{4,0},{8,4},{12,8},{1,13},{5,1},{9,5},{13,9},{2,14},{6,2},{... | collective-permute-start | bytes 1179656 | tf_op jit(solution)/shard_map/ppermute | solution.py:22
  178.4 2.8 copy-start.12
  178.4 2.8 copy-start.13
  214.2 4.1 %copy-start.14 = (f32[128,2]{0,1:T(2,128)S(1)}, f32[128,2]{0,1:T(2,128)}, u32[]{:S(2)}) copy-start(f32[128,2]{0,1:T(2,128)} %param.9) | copy-start | bytes 3076
  214.2 27.2 %all-to-all-start.3 = ((bf16[32,2,32,384]{3,2,1,0:T(8,128)(2,1)}), bf16[32,2,32,384]{3,2,1,0:T(8,128)(2,1)S(1)}, u32[]{:S(2)}, u32[]{:S(2)}) async-start(bf16[32,2,32,384]{3,2,1,0:T(8,128)(2,1)} %bitcast.21), calls=%async_computation.3 | async-start | bytes 3145728 | tf_op jit(solution)/shard_map/all_to_all | solution.py:533
  (6 other events, 6.4 us)

commit v6 on v5

--- a/solution.py
+++ b/solution.py
@@ -405,19 +405,18 @@
 
 def total_kernel(*refs):
     half = ROWS // 2
-    for n in range(2):
-        for h in range(2):
-            own, first_plus, first_minus, later_plus, later_minus = (r[...] for r in refs[10 * n + 5 * h : 10 * n + 5 * h + 5])
-            total = refs[20 + h]
-            first_plus, first_minus, later_plus, later_minus = (
-                r.reshape(-1, half, r.shape[-1]) for r in (first_plus, first_minus, later_plus, later_minus)
-            )
-            shape = (GROUPS // 2, *total.shape[3:])
-            for j in range(own.shape[0]):
-                top = add(own[j, :half], later_plus[j], first_minus[j])
-                bottom = add(own[j, half:], first_plus[j], later_minus[j])
-                total[j, : GROUPS // 2, n] = top.reshape(shape)
-                total[j, GROUPS // 2 :, n] = bottom.reshape(shape)
+    for h in range(2):
+        own, first_plus, first_minus, later_plus, later_minus = (r[...] for r in refs[5 * h : 5 * h + 5])
+        total = refs[-2 + h]
+        first_plus, first_minus, later_plus, later_minus = (
+            r.reshape(-1, half, r.shape[-1]) for r in (first_plus, first_minus, later_plus, later_minus)
+        )
+        shape = (GROUPS // 2, *total.shape[3:])
+        for j in range(own.shape[0]):
+            top = add(own[j, :half], later_plus[j], first_minus[j])
+            bottom = add(own[j, half:], first_plus[j], later_minus[j])
+            total[j, : GROUPS // 2, 0] = top.reshape(shape)
+            total[j, GROUPS // 2 :, 0] = bottom.reshape(shape)
 
 
 def both_ways(plus, minus):
@@ -456,29 +455,28 @@
     return outs[:2], outs[2:]
 
 
-def ring_end(out_parts, out_first, got, grad_parts, grad_later):
-    _, rows, part = out_parts[0][4].shape
+def ring_end(parts, first, later, totals):
+    _, rows, part = parts[0][4].shape
     own = pl.BlockSpec((2, rows, part), lambda j: (j, 0, 0))
     blocks = [pl.BlockSpec((1, 2, rows // 2, part), lambda j, n=n: (n, j, 0, 0)) for n in range(3)]
-    later = pl.BlockSpec((2, rows // 2, part), lambda j: (j, 0, 0))
+    last = blocks[2] if totals is None else pl.BlockSpec((2, rows // 2, part), lambda j: (j, 0, 0))
     operands, specs = [], []
     for h in range(2):
-        operands += [out_parts[h][4], out_first[h], out_first[2 + h], got[h], got[2 + h]]
-        specs += [own, blocks[1], blocks[1], blocks[2], blocks[2]]
-    for h in range(2):
-        operands += [grad_parts[h][4], got[h], got[2 + h], grad_later[h], grad_later[2 + h]]
-        specs += [own, blocks[1], blocks[1], later, later]
+        operands += [parts[h][4], first[h], first[2 + h], later[h], later[2 + h]]
+        specs += [own, blocks[1], blocks[1], last, last]
+    number = 0 if totals is None else 1
     shape = (RING, GROUPS, 2, rows // GROUPS, part)
     return pl.pallas_call(
         total_kernel,
         out_shape=[jax.ShapeDtypeStruct(shape, BF16)] * 2,
         grid=(2,),
-        in_specs=specs,
-        out_specs=[pl.BlockSpec((2, *shape[1:]), lambda j: (j, 0, 0, 0, 0))] * 2,
+        in_specs=specs + [ANYWHERE] * (2 * number),
+        out_specs=[pl.BlockSpec((2, GROUPS, 1, *shape[3:]), lambda j: (j, 0, number, 0, 0))] * 2,
+        input_output_aliases={10 + h: h for h in range(2 * number)},
         compiler_params=params(),
-        cost_estimate=cost(0, 32 * RING * rows * part),
+        cost_estimate=cost(0, 16 * RING * rows * part),
         name="ring_end",
-    )(*operands)
+    )(*operands, *(totals or ()))
 
 
 def assemble_kernel(slices, *results):
@@ -525,7 +523,8 @@
     plus, minus = ring_join(out_parts, out_first, [p[0] for p in grad_parts], [p[1] for p in grad_parts])
     got = both_ways(plus, minus)
     grad_later = both_ways(*ring_later(grad_parts, got))
-    totals = ring_end(out_parts, out_first, got, grad_parts, grad_later)
+    totals = ring_end(out_parts, out_first, got, None)
+    totals = ring_end(grad_parts, got, grad_later, totals)
     homes = []
     for h in range(2):
         pieces = totals[h].reshape(RING * GROUPS, 2, half, part)

time: 291 us -> 289 us (level)
    ppermute x20, waiting for transfers between devices: 49.6 us -> 46 us  [shift(): lax.ppermute(rows, axis, [(i, (i + step) % RING) for i in range(RING)])]
    pallas_call x1 -> x2, Pallas kernels: 5.42 us -> 7.14 us  [ring_end(): pl.pallas_call(total_kernel, out_shape=[jax.ShapeDtypeStruct(shape, BF16)...]
  transfers between devices with their start and end apart: 23 -> 23, of which waited for: 10 -> 10; matrix products, arithmetic and copies ran while one was open for 2% -> 2% of each run, Pallas kernels for 17% -> 18%
where the time goes in v6:
time: 289 us
  waiting for transfers between devices  91.8 us (32%)
  blocking collectives  70.9 us (25%)
  Pallas kernels  70.5 us (24%)
  starting transfers between devices  44.8 us (16%)
  local copies, waits for them, and re-layouts  5.28 us (2%)
  matrix products  4.45 us (2%)
    ppermute x20, waiting for transfers between devices, shift(): lax.ppermute(rows, axis, [(i, (i + step) % RING) for i in range(RING)])  46 us
    all_to_all x1, blocking collectives, per_device(): lax.all_to_all(copies, AXES, split_axis=0, concat_axis=0, tiled=True)  43.3 us
    ppermute x20, starting transfers between devices, shift(): lax.ppermute(rows, axis, [(i, (i + step) % RING) for i in range(RING)])  30.4 us
    all_to_all x1, blocking collectives, per_device(): lax.all_to_all(pieces, axes, split_axis=0, concat_axis=0, tiled=True)  27.6 us
    all_to_all x1, waiting for transfers between devices, per_device(): lax.all_to_all(pieces, axes, split_axis=0, concat_axis=0, tiled=True)  23 us
    all_to_all x2, waiting for transfers between devices, to_experts(): return lax.all_to_all(rows, EXPERT, split_axis=0, concat_axis=0, tiled=True)  22.8 us
    pallas_call x1, Pallas kernels, backward(): pl.pallas_call(backward_kernel, out_shape=shapes, grid_spec=pltpu.Prefetc...  19.7 us
    pallas_call x1, Pallas kernels, forward(): pl.pallas_call(forward_far_kernel, out_shape=[jax.ShapeDtypeStruct((2 * R...  13.9 us
  transfers between devices with their start and end apart: 23, of which 10 were waited for; matrix products, arithmetic and copies ran while one was open for 2% of the time, Pallas kernels for 18%

profile of v6, /device:TPU:0, one launch (start us, length us, event | category | flops | bytes accessed | tf_op | source)
XLA Modules:
  0.0 288.6 jit_solution(15982465973295323287)
XLA Ops:
  2.9 2.7 dispatch.1
  5.6 5.5 %all-to-all-start.1 = ((bf16[8,2,32,1536]{3,2,1,0:T(8,128)(2,1)}), bf16[8,2,32,1536]{3,2,1,0:T(8,128)(2,1)S(1)}, u32[]{:S(2)}, u32[]{:S(2)}) async-start(bf16[8,2,32,1536]{3,2,1,0:T(8,128)(2,1)} %get-tuple-element.45), calls=%async_computation.1 | async-start | bytes 3145728 | tf_op jit(solution)/shard_map/all_to_all | solution.py:512
  11.3 4.5 %convolution_convert_fusion = bf16[512,6144]{1,0:T(8,128)(2,1)} fusion(bf16[128,6144]{1,0:T(8,128)(2,1)S(1)} %copy-done.3, s32[128]{0:T(128)S(1)} %get-tuple-element.87, s32[128]{0:T(128)S(1)} %get-tuple-element.86), kind=kOutput, calls=%fused_computation | convolution fusion | flops 808648704 | bytes 7865344 | tf_op jit(solution)/shard_map/dot_general | solution.py:26
  15.8 16.9 %all-to-all-done.1 = bf16[8,2,32,1536]{3,2,1,0:T(8,128)(2,1)S(1)} async-done(((bf16[8,2,32,1536]{3,2,1,0:T(8,128)(2,1)}), bf16[8,2,32,1536]{3,2,1,0:T(8,128)(2,1)S(1)}, u32[]{:S(2)}, u32[]{:S(2)}) %all-to-all-start.1) | async-done | bytes 1572896 | tf_op jit(solution)/shard_map/all_to_all | solution.py:512
  32.7 4.8 %all-to-all-start = ((bf16[8,64,6144]{2,1,0:T(8,128)(2,1)}), bf16[8,64,6144]{2,1,0:T(8,128)(2,1)}, u32[]{:S(2)}, u32[]{:S(2)}) async-start(bf16[8,64,6144]{2,1,0:T(8,128)(2,1)} %bitcast.12), calls=%async_computation | async-start | bytes 12582912 | tf_op jit(solution)/shard_map/all_to_all | solution.py:512
  40.8 1.7 collective-permute-start.2
  42.5 1.7 collective-permute-start.3
  44.2 14.5 %collective-permute-done.refs_0_.refs_2_ = bf16[256,1536]{1,0:T(8,128)(2,1)S(1)} collective-permute-done((bf16[256,1536]{1,0:T(8,128)(2,1)S(1)}, bf16[256,1536]{1,0:T(8,128)(2,1)S(1)}, u32[]{:S(2)}, u32[]{:S(2)}) %collective-permute-start) | collective-permute-done | bytes 786464 | tf_op jit(solution)/shard_map/ppermute | solution.py:22
  62.4 2.5 halves.1
  66.2 2.1 collective-permute-start.5
  71.5 13.3 %forward_near.1 = (f32[512,512]{1,0:T(8,128)}, f32[512,512]{1,0:T(8,128)}) custom-call(s32[2]{0:T(128)} %copy-done.1, bf16[256,1536]{1,0:T(8,128)(2,1)} %bitcast.28, bf16[256,1536]{1,0:T(8,128)(2,1)} %copy-done.8, bf16[256,1536]{1,0:T(8,128)(2,1)} %copy-done.6, bf16[256,1536]{1,0:T(8,128)(2,1)} %bitcast.25, bf16[256,1536]{1,0:T(8,128)(2,1)} %copy-done.9, ...), custom_call_target="tpu_custom_call" | custom-call | flops 4831838208 | bytes 23592960 | tf_op jit(solution)/shard_map/forward_near/pallas_call | solution.py:271
  85.7 13.9 %forward_far.1 = (f32[512,512]{1,0:T(8,128)}, f32[512,512]{1,0:T(8,128)}, bf16[2,4,128,384]{3,2,1,0:T(8,128)(2,1)}, bf16[2,4,128,384]{3,2,1,0:T(8,128)(2,1)}, bf...) custom-call(s32[2]{0:T(128)} %copy-done.1, ...), custom_call_target="tpu_custom_call" | custom-call | flops 4831838208 | bytes 17825792 | tf_op jit(solution)/shard_map/forward_far/pallas_call | solution.py:288
  99.6 1.7 collective-permute-start.10
  101.9 1.9 collective-permute-start.8
  103.8 5.8 %all-to-all-done = bf16[8,64,6144]{2,1,0:T(8,128)(2,1)} async-done(((bf16[8,64,6144]{2,1,0:T(8,128)(2,1)}), bf16[8,64,6144]{2,1,0:T(8,128)(2,1)}, u32[]{:S(2)}, u32[]{:S(2)}) %all-to-all-start) | async-done | bytes 6291488 | tf_op jit(solution)/shard_map/all_to_all | solution.py:512
  109.6 19.7 %backward.1 = (bf16[3,4,128,384]{3,2,1,0:T(8,128)(2,1)}, bf16[3,4,128,384]{3,2,1,0:T(8,128)(2,1)}, bf16[4,128,384]{2,1,0:T(8,128)(2,1)}, bf16[4,128,384]{2,1,0:T...) custom-call(s32[2]{0:T(128)} %copy-done.1, ...), custom_call_target="tpu_custom_call" | custom-call | flops 9663676416 | bytes 31457280 | tf_op jit(solution)/shard_map/backward/pallas_call | solution.py:316
  130.2 2.8 ring_join.1
  134.6 1.7 collective-permute-start.13
  139.6 22.6 %collective-permute-done.12.refs_4_.refs_3_.refs_1_ = bf16[3,4,128,384]{3,2,1,0:T(8,128)(2,1)} collective-permute-done((bf16[3,4,128,384]{3,2,1,0:T(8,128)(2,1)}, bf16[3,4,128,384]{3,2,1,0:T(8,128)(2,1)}, u32[]{:S(2)}, u32[]{:S(2)}) %collective-permute-start.12) | collective-permute-done | bytes 1179680 | tf_op jit(solution)/shard_map/ppermute | solution.py:22
  162.2 2.7 collective-permute-done.14.refs_5_.refs_8_.refs_6_
  164.9 2.8 ring_later.1
  168.1 3.0 %collective-permute-start.17 = (bf16[4,128,384]{2,1,0:T(8,128)(2,1)}, bf16[4,128,384]{2,1,0:T(8,128)(2,1)S(1)}, u32[]{:S(2)}, u32[]{:S(2)}) collective-permute-start(bf16[4,128,384]{2,1,0:T(8,128)(2,1)} %get-tuple-element.76), channel_id=1, source_target_pairs={{0,3},{1,0},{2,1},{3,2},{4,7},{5,4},{6,5},{7,6},{8,11},{9,8},{10,9... | collective-permute-start | bytes 1179656 | tf_op jit(solution)/shard_map/ppermute | solution.py:22
  172.6 1.7 collective-permute-start.19
  174.3 3.6 %ring_end.2 = (bf16[4,8,2,32,384]{4,3,2,1,0:T(8,128)(2,1)}, bf16[4,8,2,32,384]{4,3,2,1,0:T(8,128)(2,1)}) custom-call(bf16[4,256,384]{2,1,0:T(8,128)(2,1)} %get-tuple-element.80.refs_0_, bf16[2,4,128,384]{3,2,1,0:T(8,128)(2,1)} %collective-permute-done.8.refs_4_.refs_1_, bf16[2,4,128,384]{3,2,1,0:T(8,128)(2,1)} %copy-done.2, ...), custom_call_target="tpu_custom_call" | custom-call | bytes 6291456 | tf_op jit(solution)/shard_map/ring_end/pallas_call | solution.py:469
  178.4 2.8 collective-permute-done.18.refs_8_
  181.2 3.6 %ring_end.3 = (bf16[4,8,2,32,384]{4,3,2,1,0:T(8,128)(2,1)}, bf16[4,8,2,32,384]{4,3,2,1,0:T(8,128)(2,1)}) custom-call(bf16[4,256,384]{2,1,0:T(8,128)(2,1)} %get-tuple-element.54.refs_0_, bf16[3,4,128,384]{3,2,1,0:T(8,128)(2,1)} %collective-permute-done.12.refs_4_.refs_3_.refs_1_, ...), custom_call_target="tpu_custom_call", output_to_operand_aliasing={{0}: (10, {}), {1}: (11, {})} | custom-call | bytes 6291456 | tf_op jit(solution)/shard_map/ring_end/pallas_call | solution.py:469
  184.8 27.6 %all_to_all.29.refs_0_ = bf16[32,2,32,384]{3,2,1,0:T(8,128)(2,1)S(1)} all-to-all(bf16[32,2,32,384]{3,2,1,0:T(8,128)(2,1)} %bitcast.21), channel_id=1, replica_groups=mesh['z'=4,'core'=2,'y'=4,'x'=4] {'y','z','core'}, dimensions={0} | all-to-all | bytes 3145728 | tf_op jit(solution)/shard_map/all_to_all | solution.py:532
  212.4 4.1 %all-to-all-start.3 = ((bf16[32,2,32,384]{3,2,1,0:T(8,128)(2,1)}), bf16[32,2,32,384]{3,2,1,0:T(8,128)(2,1)S(1)}, u32[]{:S(2)}, u32[]{:S(2)}) async-start(bf16[32,2,32,384]{3,2,1,0:T(8,128)(2,1)} %bitcast.22), calls=%async_computation.3 | async-start | bytes 3145728 | tf_op jit(solution)/shard_map/all_to_all | solution.py:532
  216.6 23.0 %all-to-all-done.3.refs_1_ = bf16[32,2,32,384]{3,2,1,0:T(8,128)(2,1)S(1)} async-done(((bf16[32,2,32,384]{3,2,1,0:T(8,128)(2,1)}), bf16[32,2,32,384]{3,2,1,0:T(8,128)(2,1)S(1)}, u32[]{:S(2)}, u32[]{:S(2)}) %all-to-all-start.3) | async-done | bytes 1572896 | tf_op jit(solution)/shard_map/all_to_all | solution.py:532
  239.6 2.6 combine.1
  242.2 43.3 %all_to_all.30.slices = bf16[16,2,128,384]{3,2,1,0:T(8,128)(2,1)} all-to-all(bf16[16,2,128,384]{3,2,1,0:T(8,128)(2,1)S(1)} %combine.1), channel_id=1, replica_groups=mesh['z'=4,'core'=2,'y'=4,'x'=4] {'x','y'}, dimensions={0} | all-to-all | bytes 6291456 | tf_op jit(solution)/shard_map/all_to_all | solution.py:534
  285.4 3.2 %assemble.1 = (bf16[128,6144]{1,0:T(8,128)(2,1)}, bf16[128,6144]{1,0:T(8,128)(2,1)}) custom-call(bf16[16,2,128,384]{3,2,1,0:T(8,128)(2,1)} %all_to_all.30.slices), custom_call_target="tpu_custom_call" | custom-call | bytes 6291456 | tf_op jit(solution)/shard_map/assemble/pallas_call | solution.py:491
  (63 shorter events, 23.7 us)
Async XLA Ops:
  2.9 2.7 copy-start.1
  5.6 5.7 %copy-start.3 = (bf16[128,6144]{1,0:T(8,128)(2,1)S(1)}, bf16[128,6144]{1,0:T(8,128)(2,1)}, u32[]{:S(2)}) copy-start(bf16[128,6144]{1,0:T(8,128)(2,1)} %param.10) | copy-start | bytes 4718596
  5.6 27.1 %all-to-all-start.1 = ((bf16[8,2,32,1536]{3,2,1,0:T(8,128)(2,1)}), bf16[8,2,32,1536]{3,2,1,0:T(8,128)(2,1)S(1)}, u32[]{:S(2)}, u32[]{:S(2)}) async-start(bf16[8,2,32,1536]{3,2,1,0:T(8,128)(2,1)} %get-tuple-element.45), calls=%async_computation.1 | async-start | bytes 3145728 | tf_op jit(solution)/shard_map/all_to_all | solution.py:512
  32.7 76.9 %all-to-all-start = ((bf16[8,64,6144]{2,1,0:T(8,128)(2,1)}), bf16[8,64,6144]{2,1,0:T(8,128)(2,1)}, u32[]{:S(2)}, u32[]{:S(2)}) async-start(bf16[8,64,6144]{2,1,0:T(8,128)(2,1)} %bitcast.12), calls=%async_computation | async-start | bytes 12582912 | tf_op jit(solution)/shard_map/all_to_all | solution.py:512
  37.6 27.3 %copy-start.4 = (bf16[8,1,32,1536]{3,2,1,0:T(8,128)(2,1)}, bf16[8,1,32,1536]{3,2,1,0:T(8,128)(2,1)S(1)}, u32[]{:S(2)}) copy-start(bf16[8,1,32,1536]{3,2,1,0:T(8,128)(2,1)S(1)} %get-tuple-element.88) | copy-start | bytes 2359300
  37.6 27.3 %copy-start.5 = (bf16[8,1,32,1536]{3,2,1,0:T(8,128)(2,1)}, bf16[8,1,32,1536]{3,2,1,0:T(8,128)(2,1)S(1)}, u32[]{:S(2)}) copy-start(bf16[8,1,32,1536]{3,2,1,0:T(8,128)(2,1)S(1)} %get-tuple-element.89) | copy-start | bytes 2359300
  37.6 21.1 %collective-permute-start = (bf16[256,1536]{1,0:T(8,128)(2,1)S(1)}, bf16[256,1536]{1,0:T(8,128)(2,1)S(1)}, u32[]{:S(2)}, u32[]{:S(2)}) collective-permute-start(bf16[256,1536]{1,0:T(8,128)(2,1)S(1)} %bitcast.26), channel_id=1, source_target_pairs={{0,1},{1,2},{2,3},{3,0},{4,5},{5,6},{6,7},{7,4},{8,9},{9,10},{10,1... | collective-permute-start | bytes 2359304 | tf_op jit(solution)/shard_map/ppermute | solution.py:22
  39.2 20.8 %collective-permute-start.1 = (bf16[256,1536]{1,0:T(8,128)(2,1)S(1)}, bf16[256,1536]{1,0:T(8,128)(2,1)S(1)}, u32[]{:S(2)}, u32[]{:S(2)}) collective-permute-start(bf16[256,1536]{1,0:T(8,128)(2,1)S(1)} %bitcast.23), channel_id=1, source_target_pairs={{0,4},{4,8},{8,12},{12,0},{1,5},{5,9},{9,13},{13,1},{2,6},{6,10},{... | collective-permute-start | bytes 2359304 | tf_op jit(solution)/shard_map/ppermute | solution.py:22
  40.8 19.2 %collective-permute-start.2 = (bf16[256,1536]{1,0:T(8,128)(2,1)S(1)}, bf16[256,1536]{1,0:T(8,128)(2,1)S(1)}, u32[]{:S(2)}, u32[]{:S(2)}) collective-permute-start(bf16[256,1536]{1,0:T(8,128)(2,1)S(1)} %bitcast.27), channel_id=1, source_target_pairs={{0,3},{1,0},{2,1},{3,2},{4,7},{5,4},{6,5},{7,6},{8,11},{9,8},{10,9... | collective-permute-start | bytes 2359304 | tf_op jit(solution)/shard_map/ppermute | solution.py:22
  42.5 19.0 %collective-permute-start.3 = (bf16[256,1536]{1,0:T(8,128)(2,1)S(1)}, bf16[256,1536]{1,0:T(8,128)(2,1)S(1)}, u32[]{:S(2)}, u32[]{:S(2)}) collective-permute-start(bf16[256,1536]{1,0:T(8,128)(2,1)S(1)} %bitcast.24), channel_id=1, source_target_pairs={{0,12},{4,0},{8,4},{12,8},{1,13},{5,1},{9,5},{13,9},{2,14},{6,2},{... | collective-permute-start | bytes 2359304 | tf_op jit(solution)/shard_map/ppermute | solution.py:22
  58.7 2.8 copy-start.6
  60.0 1.5 copy-start.7
  65.0 19.8 %collective-permute-start.4 = (bf16[128,1536]{1,0:T(8,128)(2,1)}, bf16[128,1536]{1,0:T(8,128)(2,1)S(1)}, u32[]{:S(2)}, u32[]{:S(2)}) collective-permute-start(bf16[128,1536]{1,0:T(8,128)(2,1)} %get-tuple-element.46), channel_id=1, source_target_pairs={{0,1},{1,2},{2,3},{3,0},{4,5},{5,6},{6,7},{7,4},{8,9},{9,10},{10,1... | collective-permute-start | bytes 1179656 | tf_op jit(solution)/shard_map/ppermute | solution.py:22
  66.2 18.6 %collective-permute-start.5 = (bf16[128,1536]{1,0:T(8,128)(2,1)}, bf16[128,1536]{1,0:T(8,128)(2,1)S(1)}, u32[]{:S(2)}, u32[]{:S(2)}) collective-permute-start(bf16[128,1536]{1,0:T(8,128)(2,1)} %get-tuple-element.47), channel_id=1, source_target_pairs={{0,3},{1,0},{2,1},{3,2},{4,7},{5,4},{6,5},{7,6},{8,11},{9,8},{10,9... | collective-permute-start | bytes 1179656 | tf_op jit(solution)/shard_map/ppermute | solution.py:22
  68.3 16.6 %collective-permute-start.6 = (bf16[128,1536]{1,0:T(8,128)(2,1)}, bf16[128,1536]{1,0:T(8,128)(2,1)}, u32[]{:S(2)}, u32[]{:S(2)}) collective-permute-start(bf16[128,1536]{1,0:T(8,128)(2,1)} %get-tuple-element.48), channel_id=1, source_target_pairs={{0,4},{4,8},{8,12},{12,0},{1,5},{5,9},{9,13},{13,1},{2,6},{6,10},{... | collective-permute-start | bytes 1179656 | tf_op jit(solution)/shard_map/ppermute | solution.py:22
  69.9 15.0 %collective-permute-start.7 = (bf16[128,1536]{1,0:T(8,128)(2,1)}, bf16[128,1536]{1,0:T(8,128)(2,1)}, u32[]{:S(2)}, u32[]{:S(2)}) collective-permute-start(bf16[128,1536]{1,0:T(8,128)(2,1)} %get-tuple-element.49), channel_id=1, source_target_pairs={{0,12},{4,0},{8,4},{12,8},{1,13},{5,1},{9,5},{13,9},{2,14},{6,2},{... | collective-permute-start | bytes 1179656 | tf_op jit(solution)/shard_map/ppermute | solution.py:22
  99.6 29.7 %collective-permute-start.10 = (bf16[2,4,128,384]{3,2,1,0:T(8,128)(2,1)}, bf16[2,4,128,384]{3,2,1,0:T(8,128)(2,1)S(1)}, u32[]{:S(2)}, u32[]{:S(2)}) collective-permute-start(bf16[2,4,128,384]{3,2,1,0:T(8,128)(2,1)} %get-tuple-element.61), channel_id=1, source_target_pairs={{0,3},{1,0},{2,1},{3,2},{4,7},{5,4},{6,5},{7,6},{8,11},{9,8},{10,9... | collective-permute-start | bytes 2359304 | tf_op jit(solution)/shard_map/ppermute | solution.py:22
  101.3 28.1 %collective-permute-start.11 = (bf16[2,4,128,384]{3,2,1,0:T(8,128)(2,1)}, bf16[2,4,128,384]{3,2,1,0:T(8,128)(2,1)}, u32[]{:S(2)}, u32[]{:S(2)}) collective-permute-start(bf16[2,4,128,384]{3,2,1,0:T(8,128)(2,1)} %get-tuple-element.62), channel_id=1, source_target_pairs={{0,12},{4,0},{8,4},{12,8},{1,13},{5,1},{9,5},{13,9},{2,14},{6,2},{... | collective-permute-start | bytes 2359304 | tf_op jit(solution)/shard_map/ppermute | solution.py:22
  101.9 27.5 %collective-permute-start.8 = (bf16[2,4,128,384]{3,2,1,0:T(8,128)(2,1)}, bf16[2,4,128,384]{3,2,1,0:T(8,128)(2,1)}, u32[]{:S(2)}, u32[]{:S(2)}) collective-permute-start(bf16[2,4,128,384]{3,2,1,0:T(8,128)(2,1)} %get-tuple-element.59), channel_id=1, source_target_pairs={{0,1},{1,2},{2,3},{3,0},{4,5},{5,6},{6,7},{7,4},{8,9},{9,10},{10,1... | collective-permute-start | bytes 2359304 | tf_op jit(solution)/shard_map/ppermute | solution.py:22
  103.8 25.5 %collective-permute-start.9 = (bf16[2,4,128,384]{3,2,1,0:T(8,128)(2,1)}, bf16[2,4,128,384]{3,2,1,0:T(8,128)(2,1)}, u32[]{:S(2)}, u32[]{:S(2)}) collective-permute-start(bf16[2,4,128,384]{3,2,1,0:T(8,128)(2,1)} %get-tuple-element.60), channel_id=1, source_target_pairs={{0,4},{4,8},{8,12},{12,0},{1,5},{5,9},{9,13},{13,1},{2,6},{6,10},{... | collective-permute-start | bytes 2359304 | tf_op jit(solution)/shard_map/ppermute | solution.py:22
  133.1 29.1 %collective-permute-start.12 = (bf16[3,4,128,384]{3,2,1,0:T(8,128)(2,1)}, bf16[3,4,128,384]{3,2,1,0:T(8,128)(2,1)}, u32[]{:S(2)}, u32[]{:S(2)}) collective-permute-start(bf16[3,4,128,384]{3,2,1,0:T(8,128)(2,1)} %get-tuple-element.67), channel_id=1, source_target_pairs={{0,1},{1,2},{2,3},{3,0},{4,5},{5,6},{6,7},{7,4},{8,9},{9,10},{10,1... | collective-permute-start | bytes 3538952 | tf_op jit(solution)/shard_map/ppermute | solution.py:22
  134.6 27.5 %collective-permute-start.13 = (bf16[3,4,128,384]{3,2,1,0:T(8,128)(2,1)}, bf16[3,4,128,384]{3,2,1,0:T(8,128)(2,1)}, u32[]{:S(2)}, u32[]{:S(2)}) collective-permute-start(bf16[3,4,128,384]{3,2,1,0:T(8,128)(2,1)} %get-tuple-element.68), channel_id=1, source_target_pairs={{0,3},{1,0},{2,1},{3,2},{4,7},{5,4},{6,5},{7,6},{8,11},{9,8},{10,9... | collective-permute-start | bytes 3538952 | tf_op jit(solution)/shard_map/ppermute | solution.py:22
  136.4 28.5 %collective-permute-start.14 = (bf16[3,4,128,384]{3,2,1,0:T(8,128)(2,1)}, bf16[3,4,128,384]{3,2,1,0:T(8,128)(2,1)}, u32[]{:S(2)}, u32[]{:S(2)}) collective-permute-start(bf16[3,4,128,384]{3,2,1,0:T(8,128)(2,1)} %get-tuple-element.73), channel_id=1, source_target_pairs={{0,4},{4,8},{8,12},{12,0},{1,5},{5,9},{9,13},{13,1},{2,6},{6,10},{... | collective-permute-start | bytes 3538952 | tf_op jit(solution)/shard_map/ppermute | solution.py:22
  138.0 27.0 %collective-permute-start.15 = (bf16[3,4,128,384]{3,2,1,0:T(8,128)(2,1)}, bf16[3,4,128,384]{3,2,1,0:T(8,128)(2,1)}, u32[]{:S(2)}, u32[]{:S(2)}) collective-permute-start(bf16[3,4,128,384]{3,2,1,0:T(8,128)(2,1)} %get-tuple-element.74), channel_id=1, source_target_pairs={{0,12},{4,0},{8,4},{12,8},{1,13},{5,1},{9,5},{13,9},{2,14},{6,2},{... | collective-permute-start | bytes 3538952 | tf_op jit(solution)/shard_map/ppermute | solution.py:22
  167.7 10.7 %collective-permute-start.16 = (bf16[4,128,384]{2,1,0:T(8,128)(2,1)}, bf16[4,128,384]{2,1,0:T(8,128)(2,1)S(1)}, u32[]{:S(2)}, u32[]{:S(2)}) collective-permute-start(bf16[4,128,384]{2,1,0:T(8,128)(2,1)} %get-tuple-element.75), channel_id=1, source_target_pairs={{0,1},{1,2},{2,3},{3,0},{4,5},{5,6},{6,7},{7,4},{8,9},{9,10},{10,1... | collective-permute-start | bytes 1179656 | tf_op jit(solution)/shard_map/ppermute | solution.py:22
  168.1 10.4 %collective-permute-start.17 = (bf16[4,128,384]{2,1,0:T(8,128)(2,1)}, bf16[4,128,384]{2,1,0:T(8,128)(2,1)S(1)}, u32[]{:S(2)}, u32[]{:S(2)}) collective-permute-start(bf16[4,128,384]{2,1,0:T(8,128)(2,1)} %get-tuple-element.76), channel_id=1, source_target_pairs={{0,3},{1,0},{2,1},{3,2},{4,7},{5,4},{6,5},{7,6},{8,11},{9,8},{10,9... | collective-permute-start | bytes 1179656 | tf_op jit(solution)/shard_map/ppermute | solution.py:22
  171.0 10.2 %collective-permute-start.18 = (bf16[4,128,384]{2,1,0:T(8,128)(2,1)}, bf16[4,128,384]{2,1,0:T(8,128)(2,1)}, u32[]{:S(2)}, u32[]{:S(2)}) collective-permute-start(bf16[4,128,384]{2,1,0:T(8,128)(2,1)} %get-tuple-element.78), channel_id=1, source_target_pairs={{0,4},{4,8},{8,12},{12,0},{1,5},{5,9},{9,13},{13,1},{2,6},{6,10},{... | collective-permute-start | bytes 1179656 | tf_op jit(solution)/shard_map/ppermute | solution.py:22
  172.6 8.6 %collective-permute-start.19 = (bf16[4,128,384]{2,1,0:T(8,128)(2,1)}, bf16[4,128,384]{2,1,0:T(8,128)(2,1)}, u32[]{:S(2)}, u32[]{:S(2)}) collective-permute-start(bf16[4,128,384]{2,1,0:T(8,128)(2,1)} %get-tuple-element.79), channel_id=1, source_target_pairs={{0,12},{4,0},{8,4},{12,8},{1,13},{5,1},{9,5},{13,9},{2,14},{6,2},{... | collective-permute-start | bytes 1179656 | tf_op jit(solution)/shard_map/ppermute | solution.py:22
  178.4 2.8 copy-start.10
  178.4 2.8 copy-start.11
  212.4 4.1 %copy-start.14 = (f32[128,2]{0,1:T(2,128)S(1)}, f32[128,2]{0,1:T(2,128)}, u32[]{:S(2)}) copy-start(f32[128,2]{0,1:T(2,128)} %param.9) | copy-start | bytes 3076
  212.4 27.2 %all-to-all-start.3 = ((bf16[32,2,32,384]{3,2,1,0:T(8,128)(2,1)}), bf16[32,2,32,384]{3,2,1,0:T(8,128)(2,1)S(1)}, u32[]{:S(2)}, u32[]{:S(2)}) async-start(bf16[32,2,32,384]{3,2,1,0:T(8,128)(2,1)} %bitcast.22), calls=%async_computation.3 | async-start | bytes 3145728 | tf_op jit(solution)/shard_map/all_to_all | solution.py:532
  (6 other events, 6.4 us)

commit v7 on v6

--- a/solution.py
+++ b/solution.py
@@ -457,9 +457,9 @@
 
 def ring_end(parts, first, later, totals):
     _, rows, part = parts[0][4].shape
-    own = pl.BlockSpec((2, rows, part), lambda j: (j, 0, 0))
-    blocks = [pl.BlockSpec((1, 2, rows // 2, part), lambda j, n=n: (n, j, 0, 0)) for n in range(3)]
-    last = blocks[2] if totals is None else pl.BlockSpec((2, rows // 2, part), lambda j: (j, 0, 0))
+    own = pl.BlockSpec((RING, rows, part), lambda j: (j, 0, 0))
+    blocks = [pl.BlockSpec((1, RING, rows // 2, part), lambda j, n=n: (n, j, 0, 0)) for n in range(3)]
+    last = blocks[2] if totals is None else pl.BlockSpec((RING, rows // 2, part), lambda j: (j, 0, 0))
     operands, specs = [], []
     for h in range(2):
         operands += [parts[h][4], first[h], first[2 + h], later[h], later[2 + h]]
@@ -469,9 +469,9 @@
     return pl.pallas_call(
         total_kernel,
         out_shape=[jax.ShapeDtypeStruct(shape, BF16)] * 2,
-        grid=(2,),
+        grid=(1,),
         in_specs=specs + [ANYWHERE] * (2 * number),
-        out_specs=[pl.BlockSpec((2, GROUPS, 1, *shape[3:]), lambda j: (j, 0, number, 0, 0))] * 2,
+        out_specs=[pl.BlockSpec((RING, GROUPS, 1, *shape[3:]), lambda j: (j, 0, number, 0, 0))] * 2,
         input_output_aliases={10 + h: h for h in range(2 * number)},
         compiler_params=params(),
         cost_estimate=cost(0, 16 * RING * rows * part),

time: 289 us -> 290 us (level)
  no operation moved by 1% of the time
where the time goes in v7:
time: 290 us; the launch traced here: 289 us
  waiting for transfers between devices  91.3 us (31%)
  Pallas kernels  71.4 us (25%)
  blocking collectives  70.8 us (24%)
  starting transfers between devices  44.8 us (15%)
  local copies, waits for them, and re-layouts  5.28 us (2%)
  matrix products  4.45 us (2%)
    ppermute x20, waiting for transfers between devices, shift(): lax.ppermute(rows, axis, [(i, (i + step) % RING) for i in range(RING)])  45.6 us
    all_to_all x1, blocking collectives, per_device(): lax.all_to_all(copies, AXES, split_axis=0, concat_axis=0, tiled=True)  43.3 us
    ppermute x20, starting transfers between devices, shift(): lax.ppermute(rows, axis, [(i, (i + step) % RING) for i in range(RING)])  30.4 us
    all_to_all x1, blocking collectives, per_device(): lax.all_to_all(pieces, axes, split_axis=0, concat_axis=0, tiled=True)  27.6 us
    all_to_all x1, waiting for transfers between devices, per_device(): lax.all_to_all(pieces, axes, split_axis=0, concat_axis=0, tiled=True)  23 us
    all_to_all x2, waiting for transfers between devices, to_experts(): return lax.all_to_all(rows, EXPERT, split_axis=0, concat_axis=0, tiled=True)  22.8 us
    pallas_call x1, Pallas kernels, backward(): pl.pallas_call(backward_kernel, out_shape=shapes, grid_spec=pltpu.Prefetc...  19.7 us
    pallas_call x1, Pallas kernels, forward(): pl.pallas_call(forward_far_kernel, out_shape=[jax.ShapeDtypeStruct((2 * R...  13.9 us
  transfers between devices with their start and end apart: 23, of which 10 were waited for; matrix products, arithmetic and copies ran while one was open for 2% of the time, Pallas kernels for 18%

profile of v7, /device:TPU:0, one launch (start us, length us, event | category | flops | bytes accessed | tf_op | source)
XLA Modules:
  0.0 289.1 jit_solution(6126253111250103776)
XLA Ops:
  2.9 2.7 dispatch.1
  5.6 5.5 %all-to-all-start.1 = ((bf16[8,2,32,1536]{3,2,1,0:T(8,128)(2,1)}), bf16[8,2,32,1536]{3,2,1,0:T(8,128)(2,1)S(1)}, u32[]{:S(2)}, u32[]{:S(2)}) async-start(bf16[8,2,32,1536]{3,2,1,0:T(8,128)(2,1)} %get-tuple-element.45), calls=%async_computation.1 | async-start | bytes 3145728 | tf_op jit(solution)/shard_map/all_to_all | solution.py:512
  11.3 4.5 %convolution_convert_fusion = bf16[512,6144]{1,0:T(8,128)(2,1)} fusion(bf16[128,6144]{1,0:T(8,128)(2,1)S(1)} %copy-done.3, s32[128]{0:T(128)S(1)} %get-tuple-element.87, s32[128]{0:T(128)S(1)} %get-tuple-element.86), kind=kOutput, calls=%fused_computation | convolution fusion | flops 808648704 | bytes 7865344 | tf_op jit(solution)/shard_map/dot_general | solution.py:26
  15.8 16.9 %all-to-all-done.1 = bf16[8,2,32,1536]{3,2,1,0:T(8,128)(2,1)S(1)} async-done(((bf16[8,2,32,1536]{3,2,1,0:T(8,128)(2,1)}), bf16[8,2,32,1536]{3,2,1,0:T(8,128)(2,1)S(1)}, u32[]{:S(2)}, u32[]{:S(2)}) %all-to-all-start.1) | async-done | bytes 1572896 | tf_op jit(solution)/shard_map/all_to_all | solution.py:512
  32.7 4.8 %all-to-all-start = ((bf16[8,64,6144]{2,1,0:T(8,128)(2,1)}), bf16[8,64,6144]{2,1,0:T(8,128)(2,1)}, u32[]{:S(2)}, u32[]{:S(2)}) async-start(bf16[8,64,6144]{2,1,0:T(8,128)(2,1)} %bitcast.12), calls=%async_computation | async-start | bytes 12582912 | tf_op jit(solution)/shard_map/all_to_all | solution.py:512
  40.8 1.7 collective-permute-start.2
  42.5 1.7 collective-permute-start.3
  44.2 14.5 %collective-permute-done.refs_0_.refs_2_ = bf16[256,1536]{1,0:T(8,128)(2,1)S(1)} collective-permute-done((bf16[256,1536]{1,0:T(8,128)(2,1)S(1)}, bf16[256,1536]{1,0:T(8,128)(2,1)S(1)}, u32[]{:S(2)}, u32[]{:S(2)}) %collective-permute-start) | collective-permute-done | bytes 786464 | tf_op jit(solution)/shard_map/ppermute | solution.py:22
  62.4 2.5 halves.1
  66.2 2.1 collective-permute-start.5
  71.5 13.3 %forward_near.1 = (f32[512,512]{1,0:T(8,128)}, f32[512,512]{1,0:T(8,128)}) custom-call(s32[2]{0:T(128)} %copy-done.1, bf16[256,1536]{1,0:T(8,128)(2,1)} %bitcast.28, bf16[256,1536]{1,0:T(8,128)(2,1)} %copy-done.8, bf16[256,1536]{1,0:T(8,128)(2,1)} %copy-done.6, bf16[256,1536]{1,0:T(8,128)(2,1)} %bitcast.25, bf16[256,1536]{1,0:T(8,128)(2,1)} %copy-done.9, ...), custom_call_target="tpu_custom_call" | custom-call | flops 4831838208 | bytes 23592960 | tf_op jit(solution)/shard_map/forward_near/pallas_call | solution.py:271
  85.7 13.9 %forward_far.1 = (f32[512,512]{1,0:T(8,128)}, f32[512,512]{1,0:T(8,128)}, bf16[2,4,128,384]{3,2,1,0:T(8,128)(2,1)}, bf16[2,4,128,384]{3,2,1,0:T(8,128)(2,1)}, bf...) custom-call(s32[2]{0:T(128)} %copy-done.1, ...), custom_call_target="tpu_custom_call" | custom-call | flops 4831838208 | bytes 17825792 | tf_op jit(solution)/shard_map/forward_far/pallas_call | solution.py:288
  99.6 1.7 collective-permute-start.10
  101.9 1.9 collective-permute-start.8
  103.8 5.8 %all-to-all-done = bf16[8,64,6144]{2,1,0:T(8,128)(2,1)} async-done(((bf16[8,64,6144]{2,1,0:T(8,128)(2,1)}), bf16[8,64,6144]{2,1,0:T(8,128)(2,1)}, u32[]{:S(2)}, u32[]{:S(2)}) %all-to-all-start) | async-done | bytes 6291488 | tf_op jit(solution)/shard_map/all_to_all | solution.py:512
  109.6 19.7 %backward.1 = (bf16[3,4,128,384]{3,2,1,0:T(8,128)(2,1)}, bf16[3,4,128,384]{3,2,1,0:T(8,128)(2,1)}, bf16[4,128,384]{2,1,0:T(8,128)(2,1)}, bf16[4,128,384]{2,1,0:T...) custom-call(s32[2]{0:T(128)} %copy-done.1, ...), custom_call_target="tpu_custom_call" | custom-call | flops 9663676416 | bytes 31457280 | tf_op jit(solution)/shard_map/backward/pallas_call | solution.py:316
  130.2 2.8 ring_join.1
  134.6 1.7 collective-permute-start.13
  139.6 22.6 %collective-permute-done.12.refs_4_.refs_3_.refs_1_ = bf16[3,4,128,384]{3,2,1,0:T(8,128)(2,1)} collective-permute-done((bf16[3,4,128,384]{3,2,1,0:T(8,128)(2,1)}, bf16[3,4,128,384]{3,2,1,0:T(8,128)(2,1)}, u32[]{:S(2)}, u32[]{:S(2)}) %collective-permute-start.12) | collective-permute-done | bytes 1179680 | tf_op jit(solution)/shard_map/ppermute | solution.py:22
  162.2 2.7 collective-permute-done.14.refs_5_.refs_8_.refs_6_
  164.9 2.8 ring_later.1
  168.1 3.0 %collective-permute-start.17 = (bf16[4,128,384]{2,1,0:T(8,128)(2,1)}, bf16[4,128,384]{2,1,0:T(8,128)(2,1)S(1)}, u32[]{:S(2)}, u32[]{:S(2)}) collective-permute-start(bf16[4,128,384]{2,1,0:T(8,128)(2,1)} %get-tuple-element.76), channel_id=1, source_target_pairs={{0,3},{1,0},{2,1},{3,2},{4,7},{5,4},{6,5},{7,6},{8,11},{9,8},{10,9... | collective-permute-start | bytes 1179656 | tf_op jit(solution)/shard_map/ppermute | solution.py:22
  172.6 1.7 collective-permute-start.19
  174.3 4.0 %ring_end.2 = (bf16[4,8,2,32,384]{4,3,2,1,0:T(8,128)(2,1)}, bf16[4,8,2,32,384]{4,3,2,1,0:T(8,128)(2,1)}) custom-call(bf16[4,256,384]{2,1,0:T(8,128)(2,1)} %get-tuple-element.80.refs_0_, bf16[2,4,128,384]{3,2,1,0:T(8,128)(2,1)} %collective-permute-done.8.refs_4_.refs_1_, bf16[2,4,128,384]{3,2,1,0:T(8,128)(2,1)} %copy-done.2, ...), custom_call_target="tpu_custom_call" | custom-call | bytes 6291456 | tf_op jit(solution)/shard_map/ring_end/pallas_call | solution.py:469
  178.4 2.8 collective-permute-done.18.refs_8_
  181.2 4.0 %ring_end.3 = (bf16[4,8,2,32,384]{4,3,2,1,0:T(8,128)(2,1)}, bf16[4,8,2,32,384]{4,3,2,1,0:T(8,128)(2,1)}) custom-call(bf16[4,256,384]{2,1,0:T(8,128)(2,1)} %get-tuple-element.54.refs_0_, bf16[3,4,128,384]{3,2,1,0:T(8,128)(2,1)} %collective-permute-done.12.refs_4_.refs_3_.refs_1_, ...), custom_call_target="tpu_custom_call", output_to_operand_aliasing={{0}: (10, {}), {1}: (11, {})} | custom-call | bytes 6291456 | tf_op jit(solution)/shard_map/ring_end/pallas_call | solution.py:469
  185.3 27.6 %all_to_all.29.refs_0_ = bf16[32,2,32,384]{3,2,1,0:T(8,128)(2,1)S(1)} all-to-all(bf16[32,2,32,384]{3,2,1,0:T(8,128)(2,1)} %bitcast.21), channel_id=1, replica_groups=mesh['z'=4,'core'=2,'y'=4,'x'=4] {'y','z','core'}, dimensions={0} | all-to-all | bytes 3145728 | tf_op jit(solution)/shard_map/all_to_all | solution.py:532
  212.8 4.1 %all-to-all-start.3 = ((bf16[32,2,32,384]{3,2,1,0:T(8,128)(2,1)}), bf16[32,2,32,384]{3,2,1,0:T(8,128)(2,1)S(1)}, u32[]{:S(2)}, u32[]{:S(2)}) async-start(bf16[32,2,32,384]{3,2,1,0:T(8,128)(2,1)} %bitcast.22), calls=%async_computation.3 | async-start | bytes 3145728 | tf_op jit(solution)/shard_map/all_to_all | solution.py:532
  217.1 23.0 %all-to-all-done.3.refs_1_ = bf16[32,2,32,384]{3,2,1,0:T(8,128)(2,1)S(1)} async-done(((bf16[32,2,32,384]{3,2,1,0:T(8,128)(2,1)}), bf16[32,2,32,384]{3,2,1,0:T(8,128)(2,1)S(1)}, u32[]{:S(2)}, u32[]{:S(2)}) %all-to-all-start.3) | async-done | bytes 1572896 | tf_op jit(solution)/shard_map/all_to_all | solution.py:532
  240.1 2.6 combine.1
  242.6 43.3 %all_to_all.30.slices = bf16[16,2,128,384]{3,2,1,0:T(8,128)(2,1)} all-to-all(bf16[16,2,128,384]{3,2,1,0:T(8,128)(2,1)S(1)} %combine.1), channel_id=1, replica_groups=mesh['z'=4,'core'=2,'y'=4,'x'=4] {'x','y'}, dimensions={0} | all-to-all | bytes 6291456 | tf_op jit(solution)/shard_map/all_to_all | solution.py:534
  285.9 3.2 %assemble.1 = (bf16[128,6144]{1,0:T(8,128)(2,1)}, bf16[128,6144]{1,0:T(8,128)(2,1)}) custom-call(bf16[16,2,128,384]{3,2,1,0:T(8,128)(2,1)} %all_to_all.30.slices), custom_call_target="tpu_custom_call" | custom-call | bytes 6291456 | tf_op jit(solution)/shard_map/assemble/pallas_call | solution.py:491
  (63 shorter events, 23.2 us)
Async XLA Ops:
  2.9 2.7 copy-start.1
  5.6 5.7 %copy-start.3 = (bf16[128,6144]{1,0:T(8,128)(2,1)S(1)}, bf16[128,6144]{1,0:T(8,128)(2,1)}, u32[]{:S(2)}) copy-start(bf16[128,6144]{1,0:T(8,128)(2,1)} %param.10) | copy-start | bytes 4718596
  5.6 27.1 %all-to-all-start.1 = ((bf16[8,2,32,1536]{3,2,1,0:T(8,128)(2,1)}), bf16[8,2,32,1536]{3,2,1,0:T(8,128)(2,1)S(1)}, u32[]{:S(2)}, u32[]{:S(2)}) async-start(bf16[8,2,32,1536]{3,2,1,0:T(8,128)(2,1)} %get-tuple-element.45), calls=%async_computation.1 | async-start | bytes 3145728 | tf_op jit(solution)/shard_map/all_to_all | solution.py:512
  32.7 76.9 %all-to-all-start = ((bf16[8,64,6144]{2,1,0:T(8,128)(2,1)}), bf16[8,64,6144]{2,1,0:T(8,128)(2,1)}, u32[]{:S(2)}, u32[]{:S(2)}) async-start(bf16[8,64,6144]{2,1,0:T(8,128)(2,1)} %bitcast.12), calls=%async_computation | async-start | bytes 12582912 | tf_op jit(solution)/shard_map/all_to_all | solution.py:512
  37.6 27.3 %copy-start.4 = (bf16[8,1,32,1536]{3,2,1,0:T(8,128)(2,1)}, bf16[8,1,32,1536]{3,2,1,0:T(8,128)(2,1)S(1)}, u32[]{:S(2)}) copy-start(bf16[8,1,32,1536]{3,2,1,0:T(8,128)(2,1)S(1)} %get-tuple-element.88) | copy-start | bytes 2359300
  37.6 27.3 %copy-start.5 = (bf16[8,1,32,1536]{3,2,1,0:T(8,128)(2,1)}, bf16[8,1,32,1536]{3,2,1,0:T(8,128)(2,1)S(1)}, u32[]{:S(2)}) copy-start(bf16[8,1,32,1536]{3,2,1,0:T(8,128)(2,1)S(1)} %get-tuple-element.89) | copy-start | bytes 2359300
  37.6 21.1 %collective-permute-start = (bf16[256,1536]{1,0:T(8,128)(2,1)S(1)}, bf16[256,1536]{1,0:T(8,128)(2,1)S(1)}, u32[]{:S(2)}, u32[]{:S(2)}) collective-permute-start(bf16[256,1536]{1,0:T(8,128)(2,1)S(1)} %bitcast.26), channel_id=1, source_target_pairs={{0,1},{1,2},{2,3},{3,0},{4,5},{5,6},{6,7},{7,4},{8,9},{9,10},{10,1... | collective-permute-start | bytes 2359304 | tf_op jit(solution)/shard_map/ppermute | solution.py:22
  39.2 20.8 %collective-permute-start.1 = (bf16[256,1536]{1,0:T(8,128)(2,1)S(1)}, bf16[256,1536]{1,0:T(8,128)(2,1)S(1)}, u32[]{:S(2)}, u32[]{:S(2)}) collective-permute-start(bf16[256,1536]{1,0:T(8,128)(2,1)S(1)} %bitcast.23), channel_id=1, source_target_pairs={{0,4},{4,8},{8,12},{12,0},{1,5},{5,9},{9,13},{13,1},{2,6},{6,10},{... | collective-permute-start | bytes 2359304 | tf_op jit(solution)/shard_map/ppermute | solution.py:22
  40.8 19.2 %collective-permute-start.2 = (bf16[256,1536]{1,0:T(8,128)(2,1)S(1)}, bf16[256,1536]{1,0:T(8,128)(2,1)S(1)}, u32[]{:S(2)}, u32[]{:S(2)}) collective-permute-start(bf16[256,1536]{1,0:T(8,128)(2,1)S(1)} %bitcast.27), channel_id=1, source_target_pairs={{0,3},{1,0},{2,1},{3,2},{4,7},{5,4},{6,5},{7,6},{8,11},{9,8},{10,9... | collective-permute-start | bytes 2359304 | tf_op jit(solution)/shard_map/ppermute | solution.py:22
  42.5 19.0 %collective-permute-start.3 = (bf16[256,1536]{1,0:T(8,128)(2,1)S(1)}, bf16[256,1536]{1,0:T(8,128)(2,1)S(1)}, u32[]{:S(2)}, u32[]{:S(2)}) collective-permute-start(bf16[256,1536]{1,0:T(8,128)(2,1)S(1)} %bitcast.24), channel_id=1, source_target_pairs={{0,12},{4,0},{8,4},{12,8},{1,13},{5,1},{9,5},{13,9},{2,14},{6,2},{... | collective-permute-start | bytes 2359304 | tf_op jit(solution)/shard_map/ppermute | solution.py:22
  58.7 2.8 copy-start.6
  60.0 1.5 copy-start.7
  65.0 19.8 %collective-permute-start.4 = (bf16[128,1536]{1,0:T(8,128)(2,1)}, bf16[128,1536]{1,0:T(8,128)(2,1)S(1)}, u32[]{:S(2)}, u32[]{:S(2)}) collective-permute-start(bf16[128,1536]{1,0:T(8,128)(2,1)} %get-tuple-element.46), channel_id=1, source_target_pairs={{0,1},{1,2},{2,3},{3,0},{4,5},{5,6},{6,7},{7,4},{8,9},{9,10},{10,1... | collective-permute-start | bytes 1179656 | tf_op jit(solution)/shard_map/ppermute | solution.py:22
  66.2 18.6 %collective-permute-start.5 = (bf16[128,1536]{1,0:T(8,128)(2,1)}, bf16[128,1536]{1,0:T(8,128)(2,1)S(1)}, u32[]{:S(2)}, u32[]{:S(2)}) collective-permute-start(bf16[128,1536]{1,0:T(8,128)(2,1)} %get-tuple-element.47), channel_id=1, source_target_pairs={{0,3},{1,0},{2,1},{3,2},{4,7},{5,4},{6,5},{7,6},{8,11},{9,8},{10,9... | collective-permute-start | bytes 1179656 | tf_op jit(solution)/shard_map/ppermute | solution.py:22
  68.3 16.6 %collective-permute-start.6 = (bf16[128,1536]{1,0:T(8,128)(2,1)}, bf16[128,1536]{1,0:T(8,128)(2,1)}, u32[]{:S(2)}, u32[]{:S(2)}) collective-permute-start(bf16[128,1536]{1,0:T(8,128)(2,1)} %get-tuple-element.48), channel_id=1, source_target_pairs={{0,4},{4,8},{8,12},{12,0},{1,5},{5,9},{9,13},{13,1},{2,6},{6,10},{... | collective-permute-start | bytes 1179656 | tf_op jit(solution)/shard_map/ppermute | solution.py:22
  69.9 15.0 %collective-permute-start.7 = (bf16[128,1536]{1,0:T(8,128)(2,1)}, bf16[128,1536]{1,0:T(8,128)(2,1)}, u32[]{:S(2)}, u32[]{:S(2)}) collective-permute-start(bf16[128,1536]{1,0:T(8,128)(2,1)} %get-tuple-element.49), channel_id=1, source_target_pairs={{0,12},{4,0},{8,4},{12,8},{1,13},{5,1},{9,5},{13,9},{2,14},{6,2},{... | collective-permute-start | bytes 1179656 | tf_op jit(solution)/shard_map/ppermute | solution.py:22
  99.6 29.7 %collective-permute-start.10 = (bf16[2,4,128,384]{3,2,1,0:T(8,128)(2,1)}, bf16[2,4,128,384]{3,2,1,0:T(8,128)(2,1)S(1)}, u32[]{:S(2)}, u32[]{:S(2)}) collective-permute-start(bf16[2,4,128,384]{3,2,1,0:T(8,128)(2,1)} %get-tuple-element.61), channel_id=1, source_target_pairs={{0,3},{1,0},{2,1},{3,2},{4,7},{5,4},{6,5},{7,6},{8,11},{9,8},{10,9... | collective-permute-start | bytes 2359304 | tf_op jit(solution)/shard_map/ppermute | solution.py:22
  101.3 28.1 %collective-permute-start.11 = (bf16[2,4,128,384]{3,2,1,0:T(8,128)(2,1)}, bf16[2,4,128,384]{3,2,1,0:T(8,128)(2,1)}, u32[]{:S(2)}, u32[]{:S(2)}) collective-permute-start(bf16[2,4,128,384]{3,2,1,0:T(8,128)(2,1)} %get-tuple-element.62), channel_id=1, source_target_pairs={{0,12},{4,0},{8,4},{12,8},{1,13},{5,1},{9,5},{13,9},{2,14},{6,2},{... | collective-permute-start | bytes 2359304 | tf_op jit(solution)/shard_map/ppermute | solution.py:22
  101.9 27.5 %collective-permute-start.8 = (bf16[2,4,128,384]{3,2,1,0:T(8,128)(2,1)}, bf16[2,4,128,384]{3,2,1,0:T(8,128)(2,1)}, u32[]{:S(2)}, u32[]{:S(2)}) collective-permute-start(bf16[2,4,128,384]{3,2,1,0:T(8,128)(2,1)} %get-tuple-element.59), channel_id=1, source_target_pairs={{0,1},{1,2},{2,3},{3,0},{4,5},{5,6},{6,7},{7,4},{8,9},{9,10},{10,1... | collective-permute-start | bytes 2359304 | tf_op jit(solution)/shard_map/ppermute | solution.py:22
  103.8 25.5 %collective-permute-start.9 = (bf16[2,4,128,384]{3,2,1,0:T(8,128)(2,1)}, bf16[2,4,128,384]{3,2,1,0:T(8,128)(2,1)}, u32[]{:S(2)}, u32[]{:S(2)}) collective-permute-start(bf16[2,4,128,384]{3,2,1,0:T(8,128)(2,1)} %get-tuple-element.60), channel_id=1, source_target_pairs={{0,4},{4,8},{8,12},{12,0},{1,5},{5,9},{9,13},{13,1},{2,6},{6,10},{... | collective-permute-start | bytes 2359304 | tf_op jit(solution)/shard_map/ppermute | solution.py:22
  133.1 29.1 %collective-permute-start.12 = (bf16[3,4,128,384]{3,2,1,0:T(8,128)(2,1)}, bf16[3,4,128,384]{3,2,1,0:T(8,128)(2,1)}, u32[]{:S(2)}, u32[]{:S(2)}) collective-permute-start(bf16[3,4,128,384]{3,2,1,0:T(8,128)(2,1)} %get-tuple-element.67), channel_id=1, source_target_pairs={{0,1},{1,2},{2,3},{3,0},{4,5},{5,6},{6,7},{7,4},{8,9},{9,10},{10,1... | collective-permute-start | bytes 3538952 | tf_op jit(solution)/shard_map/ppermute | solution.py:22
  134.6 27.5 %collective-permute-start.13 = (bf16[3,4,128,384]{3,2,1,0:T(8,128)(2,1)}, bf16[3,4,128,384]{3,2,1,0:T(8,128)(2,1)}, u32[]{:S(2)}, u32[]{:S(2)}) collective-permute-start(bf16[3,4,128,384]{3,2,1,0:T(8,128)(2,1)} %get-tuple-element.68), channel_id=1, source_target_pairs={{0,3},{1,0},{2,1},{3,2},{4,7},{5,4},{6,5},{7,6},{8,11},{9,8},{10,9... | collective-permute-start | bytes 3538952 | tf_op jit(solution)/shard_map/ppermute | solution.py:22
  136.4 28.5 %collective-permute-start.14 = (bf16[3,4,128,384]{3,2,1,0:T(8,128)(2,1)}, bf16[3,4,128,384]{3,2,1,0:T(8,128)(2,1)}, u32[]{:S(2)}, u32[]{:S(2)}) collective-permute-start(bf16[3,4,128,384]{3,2,1,0:T(8,128)(2,1)} %get-tuple-element.73), channel_id=1, source_target_pairs={{0,4},{4,8},{8,12},{12,0},{1,5},{5,9},{9,13},{13,1},{2,6},{6,10},{... | collective-permute-start | bytes 3538952 | tf_op jit(solution)/shard_map/ppermute | solution.py:22
  138.0 27.0 %collective-permute-start.15 = (bf16[3,4,128,384]{3,2,1,0:T(8,128)(2,1)}, bf16[3,4,128,384]{3,2,1,0:T(8,128)(2,1)}, u32[]{:S(2)}, u32[]{:S(2)}) collective-permute-start(bf16[3,4,128,384]{3,2,1,0:T(8,128)(2,1)} %get-tuple-element.74), channel_id=1, source_target_pairs={{0,12},{4,0},{8,4},{12,8},{1,13},{5,1},{9,5},{13,9},{2,14},{6,2},{... | collective-permute-start | bytes 3538952 | tf_op jit(solution)/shard_map/ppermute | solution.py:22
  167.7 10.7 %collective-permute-start.16 = (bf16[4,128,384]{2,1,0:T(8,128)(2,1)}, bf16[4,128,384]{2,1,0:T(8,128)(2,1)S(1)}, u32[]{:S(2)}, u32[]{:S(2)}) collective-permute-start(bf16[4,128,384]{2,1,0:T(8,128)(2,1)} %get-tuple-element.75), channel_id=1, source_target_pairs={{0,1},{1,2},{2,3},{3,0},{4,5},{5,6},{6,7},{7,4},{8,9},{9,10},{10,1... | collective-permute-start | bytes 1179656 | tf_op jit(solution)/shard_map/ppermute | solution.py:22
  168.1 10.4 %collective-permute-start.17 = (bf16[4,128,384]{2,1,0:T(8,128)(2,1)}, bf16[4,128,384]{2,1,0:T(8,128)(2,1)S(1)}, u32[]{:S(2)}, u32[]{:S(2)}) collective-permute-start(bf16[4,128,384]{2,1,0:T(8,128)(2,1)} %get-tuple-element.76), channel_id=1, source_target_pairs={{0,3},{1,0},{2,1},{3,2},{4,7},{5,4},{6,5},{7,6},{8,11},{9,8},{10,9... | collective-permute-start | bytes 1179656 | tf_op jit(solution)/shard_map/ppermute | solution.py:22
  171.0 10.2 %collective-permute-start.18 = (bf16[4,128,384]{2,1,0:T(8,128)(2,1)}, bf16[4,128,384]{2,1,0:T(8,128)(2,1)}, u32[]{:S(2)}, u32[]{:S(2)}) collective-permute-start(bf16[4,128,384]{2,1,0:T(8,128)(2,1)} %get-tuple-element.78), channel_id=1, source_target_pairs={{0,4},{4,8},{8,12},{12,0},{1,5},{5,9},{9,13},{13,1},{2,6},{6,10},{... | collective-permute-start | bytes 1179656 | tf_op jit(solution)/shard_map/ppermute | solution.py:22
  172.6 8.6 %collective-permute-start.19 = (bf16[4,128,384]{2,1,0:T(8,128)(2,1)}, bf16[4,128,384]{2,1,0:T(8,128)(2,1)}, u32[]{:S(2)}, u32[]{:S(2)}) collective-permute-start(bf16[4,128,384]{2,1,0:T(8,128)(2,1)} %get-tuple-element.79), channel_id=1, source_target_pairs={{0,12},{4,0},{8,4},{12,8},{1,13},{5,1},{9,5},{13,9},{2,14},{6,2},{... | collective-permute-start | bytes 1179656 | tf_op jit(solution)/shard_map/ppermute | solution.py:22
  178.4 2.8 copy-start.10
  178.4 2.8 copy-start.11
  212.8 4.1 %copy-start.14 = (f32[128,2]{0,1:T(2,128)S(1)}, f32[128,2]{0,1:T(2,128)}, u32[]{:S(2)}) copy-start(f32[128,2]{0,1:T(2,128)} %param.9) | copy-start | bytes 3076
  212.8 27.2 %all-to-all-start.3 = ((bf16[32,2,32,384]{3,2,1,0:T(8,128)(2,1)}), bf16[32,2,32,384]{3,2,1,0:T(8,128)(2,1)S(1)}, u32[]{:S(2)}, u32[]{:S(2)}) async-start(bf16[32,2,32,384]{3,2,1,0:T(8,128)(2,1)} %bitcast.22), calls=%async_computation.3 | async-start | bytes 3145728 | tf_op jit(solution)/shard_map/all_to_all | solution.py:532
  (6 other events, 6.4 us)
